TPU v7x, 32 devices: a whole 2x2x4 slice. The times are simulated.
32 devices in a mesh: dp: 2 (over x), node: 4 (over z), local: 4 (over y, core).
Axes of the slice: x: 2, y: 2, z: 4, core: 2. Of those that a mesh axis runs over, the one named last changes fastest.
Arguments:
- tokens_in: bfloat16 [2, 4, 64, 4, 3584], P('dp', 'node'), may hold values from -6 to 6
- grad_rows: bfloat16 [2, 4, 64, 4, 3584], P('dp', 'node'), may hold values from -6 to 6
- combine_weights: float32 [2, 4, 64, 4], P('dp', 'node'), may hold values from 0.05 to 1
- live_counts: int32 [2, 4, 4], P('dp', 'node'), may hold values from 0 to 64, as said below
- w_gate: bfloat16 [4, 3584, 2048], P('node', None, 'local'), may hold values from -0.09375 to 0.09375
- w_up: bfloat16 [4, 3584, 2048], P('node', None, 'local'), may hold values from -0.09375 to 0.09375
- w_down: bfloat16 [4, 3584, 2048], P('node', None, 'local'), may hold values from -0.125 to 0.125
Outputs:
- d_tokens: bfloat16 [2, 4, 64, 4, 3584], P('dp', 'node', 'local')
- grad_gate: bfloat16 [4, 3584, 2048], P('node', 'dp', 'local')
- grad_up: bfloat16 [4, 3584, 2048], P('node', 'dp', 'local')
- grad_down: bfloat16 [4, 3584, 2048], P('node', 'dp', 'local')
Inputs may be any that keep to these rules, and one draw needn't show every extreme that they name: `live_counts`: each replica has some source and expert pair with all 64 slots live; loads differ strongly between experts.
All inputs are finite; a program needn't handle non-finite values.
Results may differ from a plain program's by a relative error of at most 0.019.
Values may be sent and summed in bfloat16 or wider, within the bound.
No kernel may reach another device: no remote copies, remote signals or barrier semaphores. Data moves between devices by JAX's collectives and lax.ppermute only.
A program may use at most 128 MiB of HBM per device.

v0:
```python
import jax
import jax.numpy as jnp
from jax import lax
from jax.sharding import PartitionSpec as P


def on_device(tokens_in, grad_rows, combine_weights, live_counts, w_gate, w_up, w_down):
    slot_count = tokens_in.shape[2]
    node_count = tokens_in.shape[3]
    feature_width = tokens_in.shape[4]
    gate_weight = w_gate[0]
    up_weight = w_up[0]
    down_weight = w_down[0]
    hid_local = gate_weight.shape[1]
    live_mask = (
        lax.broadcasted_iota(jnp.int32, (slot_count, node_count), 0) < live_counts[0, 0][None, :]
    ).astype(jnp.float32)
    scaled_rows = (
        grad_rows[0, 0].astype(jnp.float32) * (combine_weights[0, 0] * live_mask)[:, :, None]
    ).astype(jnp.bfloat16)
    scaled_rows = scaled_rows.reshape(slot_count * node_count, feature_width)
    flat_tokens = tokens_in[0, 0].reshape(slot_count * node_count, feature_width)
    gate_pre = jnp.dot(flat_tokens, gate_weight, preferred_element_type=jnp.float32)
    up_pre = jnp.dot(flat_tokens, up_weight, preferred_element_type=jnp.float32)
    sigmoid_gate = jax.nn.sigmoid(gate_pre)
    activated = gate_pre * sigmoid_gate
    hidden = (activated * up_pre).astype(jnp.bfloat16)
    hidden_grad = jnp.dot(scaled_rows, down_weight, preferred_element_type=jnp.float32)
    gate_grad = (
        hidden_grad * up_pre * sigmoid_gate * (1.0 + gate_pre * (1.0 - sigmoid_gate))
    ).astype(jnp.bfloat16)
    up_grad = (hidden_grad * activated).astype(jnp.bfloat16)
    joined_grad = jnp.concatenate((gate_grad, up_grad), axis=1)
    keep_rows = slot_count // lax.axis_size("local")
    total = lax.dot_general(
        gate_grad, gate_weight, (((1,), (1,)), ((), ())), preferred_element_type=jnp.float32
    )
    total = total + lax.dot_general(
        up_grad, up_weight, (((1,), (1,)), ((), ())), preferred_element_type=jnp.float32
    )
    summed = lax.psum_scatter(
        total.reshape(lax.axis_size("local") * keep_rows, node_count, feature_width).astype(
            jnp.bfloat16
        ),
        "local",
        scatter_dimension=0,
        tiled=True,
    )
    returned = lax.all_to_all(summed, "node", split_axis=1, concat_axis=1, tiled=True)
    d_tokens = returned[None, None]
    front = lax.dot_general(
        flat_tokens, joined_grad, (((0,), (0,)), ((), ())), preferred_element_type=jnp.float32
    )
    behind = lax.dot_general(
        scaled_rows, hidden, (((0,), (0,)), ((), ())), preferred_element_type=jnp.float32
    )
    weight_sums = lax.psum_scatter(
        jnp.concatenate((front, behind), axis=1).astype(jnp.bfloat16),
        "dp",
        scatter_dimension=0,
        tiled=True,
    ).astype(jnp.float32)
    grad_gate = weight_sums[:, :hid_local].astype(jnp.bfloat16)[None]
    grad_up = weight_sums[:, hid_local : 2 * hid_local].astype(jnp.bfloat16)[None]
    grad_down = weight_sums[:, 2 * hid_local :].astype(jnp.bfloat16)[None]
    return (d_tokens, grad_gate, grad_up, grad_down)


def solution(mesh):
    return jax.shard_map(
        on_device,
        mesh=mesh,
        in_specs=(
            P("dp", "node", None, None, None),
            P("dp", "node", None, None, None),
            P("dp", "node", None, None),
            P("dp", "node", None),
            P("node", None, "local"),
            P("node", None, "local"),
            P("node", None, "local"),
        ),
        out_specs=(
            P("dp", "node", "local", None, None),
            P("node", "dp", "local"),
            P("node", "dp", "local"),
            P("node", "dp", "local"),
        ),
        check_vma=False,
    )
```

profile of v0, /device:TPU:0, one launch (start us, length us, event | category | flops | bytes accessed | tf_op | source)
XLA Modules:
  0.0 204.7 jit_solution(14964287447932882410)
XLA Ops:
  8.9 2.4 %multiply_convert_fusion.1 = bf16[1,1,64,4,3584]{4,3,2,1,0:T(4,128)(2,1)S(1)} fusion(f32[64,4]{1,0:T(8,128)S(1)} %copy.20, bf16[1,1,64,4,3584]{4,3,2,1,0:T(4,128)(2,1)} %param.8), kind=kLoop, calls=%fused_computation.16 | loop fusion | flops 2752512 | bytes 3671040 | tf_op jit(solution)/shard_map/convert_element_type | solution.py:20
  11.2 1.5 convert_element_type.42
  12.7 2.9 %reshape_squeeze.3 = bf16[256,3584]{1,0:T(8,128)(2,1)S(1)} reshape(bf16[1,1,64,4,3584]{4,3,2,1,0:T(4,128)(2,1)} %param.7) | data formatting | bytes 3670016 | tf_op jit(solution)/shard_map/reshape;squeeze | solution.py:22
  15.7 3.8 %fusion.4 = f32[256,512]{1,0:T(8,128)S(1)} fusion(bf16[256,3584]{1,0:T(8,128)(2,1)S(1)} %reshape_squeeze.3, bf16[1,3584,512]{2,1,0:T(8,128)(2,1)} %param.11), kind=kOutput, calls=%fused_computation.8 | convolution fusion | flops 939524096 | bytes 6029312 | tf_op jit(solution)/shard_map/dot_general | solution.py:23
  19.6 1.1 fusion.7
  21.0 1.1 copy-done.7
  22.1 1.2 multiply_convert_fusion.4
  24.2 1.2 fusion.2
  25.4 1.3 fusion.1
  26.6 1.5 convert_element_type.46
  28.3 4.3 %reshape.53 = f32[256,3584]{1,0:T(8,128)} reshape(bf16[1,1,64,4,3584]{4,3,2,1,0:T(4,128)(2,1)} %param.8) | data formatting | bytes 5505024 | tf_op jit(solution)/shard_map/convert_element_type | solution.py:19
  32.6 5.0 %fusion = bf16[3584,1024]{0,1:T(8,128)(2,1)} fusion(bf16[256,3584]{1,0:T(8,128)(2,1)S(1)} %copy-done.1, bf16[256,512]{1,0:T(8,128)(2,1)S(1)} %get-tuple-element.19, bf16[256,512]{1,0:T(8,128)(2,1)S(1)} %get-tuple-element.20), kind=kOutput, calls=%fused_computation.2 | convolution fusion | flops 1883766784 | bytes 9699328 | tf_op jit(solution)/shard_map/dot_general | solution.py:51
  38.0 3.4 %convolution_convert_fusion.1 = bf16[3584,512]{0,1:T(8,128)(2,1)S(1)} fusion(f32[256,3584]{1,0:T(8,128)} %reshape.53, f32[256]{0:T(256)S(1)} %compare_select_fusion, f32[256,512]{1,0:T(8,128)S(1)} %fusion.7, f32[256,512]{1,0:T(8,128)S(1)} %fusion.4), kind=kOutput, calls=%fused_computation.3 | convolution fusion | flops 943980544 | bytes 8389632 | tf_op jit(solution)/shard_map/dot_general | solution.py:54
  41.5 0.8 slice-done.1
  42.3 9.9 %pad_maximum_fusion = bf16[3584,1536]{0,1:T(8,128)(2,1)} fusion(bf16[3584,512]{0,1:T(8,128)(2,1)S(1)} %convolution_convert_fusion.1, bf16[3584,1024]{0,1:T(8,128)(2,1)S(1)} %bitcast.39), kind=kLoop, calls=%fused_computation | loop fusion | flops 22020096 | bytes 22020096 | tf_op jit(solution)/shard_map/concatenate | solution.py:58
  54.1 24.0 %all-reduce.3.cloned.1.call-done = bf16[64,4,3584]{2,1,0:T(4,128)(2,1)} async-done(((bf16[64,4,3584]{2,1,0:T(4,128)(2,1)}), bf16[64,4,3584]{2,1,0:T(4,128)(2,1)}) %all-reduce.3.cloned.1.call-update) | async-done | bytes 1835024
  78.1 1.2 constant_dynamic-slice_fusion
  79.4 17.4 %all_to_all.5 = bf16[16,4,3584]{2,0,1:T(8,128)(2,1)S(1)} all-to-all(bf16[16,4,3584]{2,0,1:T(8,128)(2,1)S(1)} %copy.21), channel_id=1, replica_groups=mesh['dp'=2,'node'=4,'local'=4] {'node'}, dimensions={1} | all-to-all | bytes 917504 | tf_op jit(solution)/shard_map/all_to_all | solution.py:49
  96.8 1.1 copy.23
  97.9 84.6 %reduce-scatter.2.cloned.1.call-done = bf16[1792,1536]{0,1:T(8,128)(2,1)} async-done(((bf16[3584,1536]{0,1:T(8,128)(2,1)}), bf16[1792,1536]{0,1:T(8,128)(2,1)}) %reduce-scatter.2.cloned.1.call-update) | async-done | bytes 5505040 | tf_op jit(solution)/shard_map/reduce_scatter | solution.py:57
  182.5 4.8 %slice_bitcast_fusion = (bf16[1,1792,512]{1,2,0:T(8,128)(2,1)}, bf16[1,1792,512]{1,2,0:T(8,128)(2,1)}, bf16[1,1792,512]{1,2,0:T(8,128)(2,1)S(1)}) fusion(bf16[1792,1536]{0,1:T(8,128)(2,1)} %reduce-scatter.2.cloned.1.call-done), kind=kLoop, calls=%fused_computation.17 | loop fusion | bytes 11010048 | tf_op jit(solution)/shard_map/broadcast_in_dim | solution.py:65
  187.3 3.8 %copy.26 = bf16[1,1792,512]{2,1,0:T(8,128)(2,1)} copy(bf16[1,1792,512]{1,2,0:T(8,128)(2,1)} %get-tuple-element.16) | data formatting | bytes 3670016
  191.2 3.8 %copy.25 = bf16[1,1792,512]{2,1,0:T(8,128)(2,1)} copy(bf16[1,1792,512]{1,2,0:T(8,128)(2,1)} %get-tuple-element.17) | data formatting | bytes 3670016
  195.0 2.3 %copy.24 = bf16[1,1792,512]{2,1,0:T(8,128)(2,1)} copy(bf16[1,1792,512]{1,2,0:T(8,128)(2,1)S(1)} %get-tuple-element.18) | data formatting | bytes 3670016
  (36 shorter events, 3.9 us)
Async XLA Ops:
  8.0 70.1 %all-reduce.3.cloned.1.call-start = ((), (), s32[]{:S(2)}) async-start(), calls=%async_computation.3 | async-start | bytes 3670016
  15.6 5.0 %copy-start = (bf16[256,3584]{1,0:T(8,128)(2,1)}, bf16[256,3584]{1,0:T(8,128)(2,1)S(1)}, u32[]{:S(2)}) copy-start(bf16[256,3584]{1,0:T(8,128)(2,1)S(1)} %reshape_squeeze.3) | copy-start | bytes 5505028
  15.7 3.9 %copy-start.2 = (bf16[1,3584,512]{2,1,0:T(8,128)(2,1)S(1)}, bf16[1,3584,512]{2,1,0:T(8,128)(2,1)}, u32[]{:S(2)}) copy-start(bf16[1,3584,512]{2,1,0:T(8,128)(2,1)} %param.12) | copy-start | bytes 11010052
  19.5 1.5 copy-start.4
  19.5 2.6 %copy-start.7 = (bf16[1,3584,512]{2,1,0:T(8,128)(2,1)S(1)}, bf16[1,3584,512]{2,1,0:T(8,128)(2,1)}, u32[]{:S(2)}) copy-start(bf16[1,3584,512]{2,1,0:T(8,128)(2,1)} %param.13) | copy-start | bytes 11010052
  22.1 2.0 copy-start.3
  26.6 1.5 copy-start.5
  28.1 4.5 %copy-start.1 = (bf16[256,3584]{1,0:T(8,128)(2,1)S(1)}, bf16[256,3584]{1,0:T(8,128)(2,1)}, u32[]{:S(2)}) copy-start(bf16[256,3584]{1,0:T(8,128)(2,1)} %copy-done) | copy-start | bytes 5505028
  28.1 154.4 %reduce-scatter.2.cloned.1.call-start = ((), (), s32[]{:S(2)}) async-start(), calls=%async_computation.2 | async-start | bytes 16515072 | tf_op jit(solution)/shard_map/reduce_scatter | solution.py:57
  32.6 5.1 %copy-start.6 = (s32[1,1,4]{2,1,0:T(1,128)S(1)}, s32[1,1,4]{2,1,0:T(1,128)}, u32[]{:S(2)}) copy-start(s32[1,1,4]{2,1,0:T(1,128)} %param.10) | copy-start | bytes 52
  38.0 3.5 %slice-start = ((s8[7340032]{0:T(1024)(128)(4,1)}), s8[4194304]{0:T(1024)(128)(4,1)S(1)}, s32[]{:S(2)}) async-start(s8[7340032]{0:T(1024)(128)(4,1)} %bitcast.38), calls=%async_computation.4 | async-start | bytes 8388608
  38.0 4.3 %slice-start.1 = ((s8[7340032]{0:T(1024)(128)(4,1)}), s8[3145728]{0:T(1024)(128)(4,1)S(1)}, s32[]{:S(2)}) async-start(s8[7340032]{0:T(1024)(128)(4,1)} %bitcast.38), calls=%async_computation.5 | async-start | bytes 6291456
  52.2 0.7 copy-start.8
Sparse Core Ops, SparseCore 0:
  28.2 49.8 all-reduce.2
Sparse Core Ops, SparseCore 1:
  52.3 130.2 reduce-scatter.1
where the time goes:
time: 205 us
  waiting for transfers between devices  109 us (53%)
  local copies, waits for them, and re-layouts  32.1 us (16%)
  blocking collectives  17.4 us (8%)
  matrix products  17.1 us (8%)
  between operations  16.3 us (8%)
  other arithmetic  13 us (6%)
    reduce_scatter x1, waiting for transfers between devices, on_device(): lax.psum_scatter(jnp.concatenate((front, behind), axis=1).astype(jnp.bflo...  84.6 us
    unnamed x3, waiting for transfers between devices  24.1 us
    all_to_all x1, blocking collectives, on_device(): lax.all_to_all(summed, 'node', split_axis=1, concat_axis=1, tiled=True)  17.4 us
    unnamed x29, local copies, waits for them, and re-layouts  16.7 us
    concatenate x1, other arithmetic, on_device(): jnp.concatenate((front, behind), axis=1).astype(jnp.bfloat16)  9.91 us
    dot_general x1, matrix products, on_device(): lax.dot_general(flat_tokens, joined_grad, (((0,), (0,)), ((), ())), prefe...  5.05 us
    broadcast_in_dim x1, local copies, waits for them, and re-layouts, on_device(): grad_down = weight_sums[:, 2 * hid_local:].astype(jnp.bfloat16)[None]  4.79 us
    convert_element_type x1, local copies, waits for them, and re-layouts, on_device(): grad_rows[0, 0].astype(jnp.float32)  4.31 us
  transfers between devices with their start and end apart: 2, of which 2 were waited for; matrix products, arithmetic and copies ran while one was open for 13% of the time, Pallas kernels for 0%

commit v1 on v0

v1 whole, which is shorter than its diff:
```python
import jax
import jax.numpy as jnp
from jax import lax
from jax.sharding import PartitionSpec as P


def on_device(tokens_in, grad_rows, combine_weights, live_counts, w_gate, w_up, w_down):
    slots, nodes, width = tokens_in.shape[2:]
    replicas, locals_ = lax.axis_size("dp"), lax.axis_size("local")
    replica, local, node = lax.axis_index("dp"), lax.axis_index("local"), lax.axis_index("node")
    keep = slots // locals_
    part = width // replicas
    rows = slots * nodes
    gate_weight, up_weight, down_weight = w_gate[0], w_up[0], w_down[0]
    tokens, grads = tokens_in[0, 0], grad_rows[0, 0]
    live = (lax.broadcasted_iota(jnp.int32, (slots, nodes), 0) < live_counts[0, 0][None, :]).astype(jnp.float32)
    factor = combine_weights[0, 0] * live

    def swap_local(value, bit):
        return lax.ppermute(value, "local", [(i, i ^ bit) for i in range(locals_)])

    def shift(value, axis, by):
        size = lax.axis_size(axis)
        return lax.ppermute(value, axis, [(i, (i + by) % size) for i in range(size)])

    bits = [1 << i for i in range(locals_.bit_length() - 1)]
    order = [0]
    for bit in reversed(bits):
        order = order + [d ^ bit for d in order]

    def gather_local(value):
        for bit in reversed(bits):
            value = jnp.concatenate((value, swap_local(value, bit)), axis=0)
        return value

    others = []
    for by in range(1, replicas):
        there = lax.rem(replica + by, replicas)
        start = (local * keep, 0, there * part)
        token_share = lax.dynamic_slice(tokens, start, (keep, nodes, part))
        grad_share = lax.dynamic_slice(grads, start, (keep, nodes, part))
        factor_share = lax.dynamic_slice(factor, (local * keep, 0), (keep, nodes))
        scaled_share = (grad_share.astype(jnp.float32) * factor_share[:, :, None]).astype(jnp.bfloat16)
        token_share = shift(token_share.reshape(keep * nodes, part), "dp", by)
        scaled_share = shift(scaled_share.reshape(keep * nodes, part), "dp", by)
        others.append((token_share, scaled_share))

    scaled = (grads.astype(jnp.float32) * factor[:, :, None]).astype(jnp.bfloat16).reshape(rows, width)
    tokens = tokens.reshape(rows, width)
    gate_pre = jnp.dot(tokens, gate_weight, preferred_element_type=jnp.float32)
    up_pre = jnp.dot(tokens, up_weight, preferred_element_type=jnp.float32)
    sigmoid_gate = jax.nn.sigmoid(gate_pre)
    activated = gate_pre * sigmoid_gate
    hidden = (activated * up_pre).astype(jnp.bfloat16)
    hidden_grad = jnp.dot(scaled, down_weight, preferred_element_type=jnp.float32)
    gate_grad = (hidden_grad * up_pre * sigmoid_gate * (1.0 + gate_pre * (1.0 - sigmoid_gate))).astype(jnp.bfloat16)
    up_grad = (hidden_grad * activated).astype(jnp.bfloat16)

    blocks = jnp.array(order) ^ local

    def reorder(value):
        return jnp.take(value.reshape(locals_, keep * nodes, -1), blocks, axis=0).reshape(rows, -1)

    sent = [[shift(reorder(v), "dp", by) for v in (gate_grad, up_grad, hidden)] for by in range(1, replicas)]

    place = local ^ jnp.arange(locals_)
    source = lax.rem(node + jnp.arange(nodes), nodes)
    index = ((place[:, None, None] * keep + jnp.arange(keep)[None, None, :]) * nodes + source[None, :, None]).reshape(-1)
    one_hot = (index[:, None] == jnp.arange(rows)[None, :]).astype(jnp.bfloat16)
    gate_moved = jnp.dot(one_hot, gate_grad, preferred_element_type=jnp.bfloat16)
    up_moved = jnp.dot(one_hot, up_grad, preferred_element_type=jnp.bfloat16)
    total = lax.dot_general(gate_moved, gate_weight, (((1,), (1,)), ((), ())), preferred_element_type=jnp.float32)
    total = total + lax.dot_general(up_moved, up_weight, (((1,), (1,)), ((), ())), preferred_element_type=jnp.float32)
    total = total.astype(jnp.bfloat16).reshape(locals_, nodes, keep, width)
    arrived = [None] * nodes
    for k in list(range(1, nodes)) + [0]:
        held = {d: total[d, k] for d in range(locals_)}
        for bit in bits:
            stay = sorted(d for d in held if not d & bit)
            came = swap_local(jnp.stack([held[d | bit] for d in stay]), bit)
            held = {d: (held[d].astype(jnp.float32) + came[i].astype(jnp.float32)).astype(jnp.bfloat16) for i, d in enumerate(stay)}
        arrived[k] = shift(held[0], "node", k) if k else held[0]
    stacked = jnp.stack(arrived)
    origin = lax.rem(node - jnp.arange(nodes) + nodes, nodes)
    d_tokens = jnp.take(stacked, origin, axis=0).transpose(1, 0, 2)[None, None]

    mine = lambda v: lax.dynamic_slice(v, (0, replica * part), (rows, part))
    token_parts, scaled_parts = [mine(tokens)], [mine(scaled)]
    gate_parts, up_parts, hidden_parts = [gate_grad], [up_grad], [hidden]
    for (token_share, scaled_share), (gg, ug, hd) in zip(others, sent):
        token_parts.append(gather_local(token_share))
        scaled_parts.append(gather_local(scaled_share))
        gate_parts.append(gg)
        up_parts.append(ug)
        hidden_parts.append(hd)

    def weight_grad(left, right):
        total = 0.0
        for a, b in zip(left, right):
            total = total + lax.dot_general(a, b, (((0,), (0,)), ((), ())), preferred_element_type=jnp.float32)
        return total.astype(jnp.bfloat16)[None]

    return (d_tokens, weight_grad(token_parts, gate_parts), weight_grad(token_parts, up_parts), weight_grad(scaled_parts, hidden_parts))


def solution(mesh):
    return jax.shard_map(
        on_device,
        mesh=mesh,
        in_specs=(
            P("dp", "node", None, None, None),
            P("dp", "node", None, None, None),
            P("dp", "node", None, None),
            P("dp", "node", None),
            P("node", None, "local"),
            P("node", None, "local"),
            P("node", None, "local"),
        ),
        out_specs=(
            P("dp", "node", "local", None, None),
            P("node", "dp", "local"),
            P("node", "dp", "local"),
            P("node", "dp", "local"),
        ),
        check_vma=False,
    )
```

time: 205 us -> 110 us (0.54)
  waiting for transfers between devices: 109 us -> 18.3 us
  matrix products: 17.1 us -> 37.5 us
  starting transfers between devices: 0.08 us -> 19.2 us
  blocking collectives: 17.4 us -> 0 us
  between operations: 16.3 us -> 0.94 us
  local copies, waits for them, and re-layouts: 32.1 us -> 19.7 us
    reduce_scatter x1 -> x0, waiting for transfers between devices: 84.6 us -> none  [on_device(): lax.psum_scatter(jnp.concatenate((front, behind), axis=1).astype(jnp.bflo...]
    unnamed x3 -> x0, waiting for transfers between devices: 24.1 us -> none
    dot_general x7 -> x11, matrix products: 17.1 us -> 37.5 us  [the longest x6 20.5 us: weight_grad(): lax.dot_general(a, b, (((0,), (0,)), ((), ())), preferred_element_type=jn...]
    ppermute x0 -> x20, starting transfers between devices: none -> 19.2 us  [the longest x8 11.9 us: shift(): lax.ppermute(value, axis, [(i, (i + by) % size) for i in range(size)])]
    ppermute x0 -> x20, waiting for transfers between devices: none -> 18.3 us  [the longest x12 9.59 us: swap_local(): return lax.ppermute(value, 'local', [(i, i ^ bit) for i in range(locals_)])]
    all_to_all x1 -> x0, blocking collectives: 17.4 us -> none  [on_device(): lax.all_to_all(summed, 'node', split_axis=1, concat_axis=1, tiled=True)]
    unnamed x29 -> x30, local copies, waits for them, and re-layouts: 16.7 us -> 3.14 us
    concatenate x1 -> x2, other arithmetic: 9.91 us -> 1.6 us  [gather_local(): value = jnp.concatenate((value, swap_local(value, bit)), axis=0)]
  transfers between devices with their start and end apart: 2 -> 20, of which waited for: 2 -> 7; matrix products, arithmetic and copies ran while one was open for 13% -> 58% of each run, Pallas kernels for 0% -> 0%
where the time goes in v1:
time: 110 us; the launch traced here: 109 us
  matrix products  37.5 us (34%)
  local copies, waits for them, and re-layouts  19.7 us (18%)
  starting transfers between devices  19.2 us (17%)
  waiting for transfers between devices  18.3 us (17%)
  other arithmetic  13.7 us (12%)
    dot_general x6, matrix products, weight_grad(): lax.dot_general(a, b, (((0,), (0,)), ((), ())), preferred_element_type=jn...  20.5 us
    ppermute x8, starting transfers between devices, shift(): lax.ppermute(value, axis, [(i, (i + by) % size) for i in range(size)])  11.9 us
    ppermute x12, waiting for transfers between devices, swap_local(): return lax.ppermute(value, 'local', [(i, i ^ bit) for i in range(locals_)])  9.59 us
    ppermute x8, waiting for transfers between devices, shift(): lax.ppermute(value, axis, [(i, (i + by) % size) for i in range(size)])  8.67 us
    ppermute x12, starting transfers between devices, swap_local(): return lax.ppermute(value, 'local', [(i, i ^ bit) for i in range(locals_)])  7.27 us
    dot_general x1, matrix products, on_device(): lax.dot_general(up_moved, up_weight, (((1,), (1,)), ((), ())), preferred_...  5.67 us
    dot_general x1, matrix products, on_device(): lax.dot_general(gate_moved, gate_weight, (((1,), (1,)), ((), ())), prefer...  5.11 us
    another operation x1, local copies, waits for them, and re-layouts, on_device(): tokens = tokens.reshape(rows, width)  3.9 us
  transfers between devices with their start and end apart: 20, of which 7 were waited for; matrix products, arithmetic and copies ran while one was open for 58% of the time, Pallas kernels for 0%

profile of v1, /device:TPU:0, one launch (start us, length us, event | category | flops | bytes accessed | tf_op | source)
XLA Modules:
  0.0 109.4 jit_solution(16285622066233218017)
XLA Ops:
  3.7 2.9 %collective-permute-start.16 = (bf16[64,1792]{1,0:T(8,128)(2,1)}, bf16[64,1792]{1,0:T(8,128)(2,1)S(1)}, u32[]{:S(2)}, u32[]{:S(2)}) collective-permute-start(bf16[64,1792]{1,0:T(8,128)(2,1)} %multiply_convert_fusion.4), channel_id=1, source_target_pairs={{0,16},{16,0},{1,17},{17,1},{2,18},{18,2},{3,19},{19,3},{4,20},{20... | collective-permute-start | bytes 688136 | tf_op jit(solution)/shard_map/ppermute | solution.py:24
  6.8 3.9 %reshape_squeeze.3 = bf16[256,3584]{1,0:T(8,128)(2,1)} reshape(bf16[1,1,64,4,3584]{4,3,2,1,0:T(4,128)(2,1)} %param.10) | data formatting | bytes 3670016 | tf_op jit(solution)/shard_map/reshape;squeeze | solution.py:49
  10.7 2.1 %multiply_convert_fusion = bf16[1,1,64,4,3584]{4,3,2,1,0:T(4,128)(2,1)} fusion(f32[64,4]{1,0:T(8,128)S(1)} %copy.14, bf16[1,1,64,4,3584]{4,3,2,1,0:T(4,128)(2,1)S(1)} %copy-done.2), kind=kLoop, calls=%fused_computation.18 | loop fusion | flops 2752512 | bytes 3671040 | tf_op jit(solution)/shard_map/convert_element_type | solution.py:48
  12.8 3.9 %convert_element_type.253 = bf16[256,3584]{1,0:T(8,128)(2,1)} reshape(bf16[1,1,64,4,3584]{4,3,2,1,0:T(4,128)(2,1)} %multiply_convert_fusion) | data formatting | bytes 3670016 | tf_op jit(solution)/shard_map/convert_element_type | solution.py:48
  16.9 3.8 %fusion.3 = f32[256,512]{1,0:T(8,128)S(1)} fusion(bf16[256,3584]{1,0:T(8,128)(2,1)} %reshape_squeeze.3, bf16[1,3584,512]{2,1,0:T(8,128)(2,1)} %param.14), kind=kOutput, calls=%fused_computation.8 | convolution fusion | flops 939524096 | bytes 6029312 | tf_op jit(solution)/shard_map/dot_general | solution.py:50
  25.0 5.1 %fusion.1 = f32[256,3584]{1,0:T(8,128)} fusion(bf16[1,3584,512]{2,1,0:T(8,128)(2,1)} %param.14, bf16[256,512]{1,0:T(8,128)(2,1)S(1)} %get-tuple-element.27, s32[256]{0:T(256)S(1)} %add.163), kind=kOutput, calls=%fused_computation.6 | convolution fusion | flops 1006698496 | bytes 7603200 | tf_op jit(solution)/shard_map/dot_general | solution.py:72
  30.1 5.7 %fusion = bf16[256,3584]{1,0:T(8,128)(2,1)} fusion(f32[256,3584]{1,0:T(8,128)} %fusion.1, bf16[1,3584,512]{2,1,0:T(8,128)(2,1)} %param.15, bf16[256,512]{1,0:T(8,128)(2,1)S(1)} %get-tuple-element.28, s32[256]{0:T(256)S(1)} %add.163), kind=kOutput, calls=%fused_computation.5 | convolution fusion | flops 1008533504 | bytes 9438208 | tf_op jit(solution)/shard_map/dot_general | solution.py:73
  41.1 2.0 %reshape.286 = f32[256,3584]{1,0:T(8,128)} reshape(bf16[1,1,64,4,3584]{4,3,2,1,0:T(4,128)(2,1)S(1)} %copy-done.2) | data formatting | bytes 5505024 | tf_op jit(solution)/shard_map/convert_element_type | solution.py:48
  43.1 3.9 %fusion.26 = f32[1792,512]{1,0:T(8,128)} fusion(bf16[256,512]{1,0:T(8,128)(2,1)S(1)} %get-tuple-element.28, bf16[256,3584]{1,0:T(8,128)(2,1)} %reshape_squeeze.3, s32[]{:T(128)S(6)} %select_n.47), kind=kOutput, calls=%fused_computation.33 | convolution fusion | flops 469762048 | bytes 4849668 | tf_op jit(solution)/shard_map/dot_general | solution.py:100
  47.0 2.5 %fusion.28 = f32[1792,512]{1,0:T(8,128)} fusion(bf16[256,512]{1,0:T(8,128)(2,1)S(1)} %get-tuple-element.27, bf16[256,3584]{1,0:T(8,128)(2,1)S(1)} %copy-done.5, s32[]{:T(128)S(6)} %select_n.47), kind=kOutput, calls=%fused_computation.35 | convolution fusion | flops 469762048 | bytes 4849668 | tf_op jit(solution)/shard_map/dot_general | solution.py:100
  51.6 4.2 %fusion.18 = f32[1792,512]{1,0:T(8,128)} fusion(bf16[256,512]{1,0:T(8,128)(2,1)S(1)} %get-tuple-element.26, f32[256,3584]{1,0:T(8,128)} %reshape.286, s32[]{:T(128)S(6)} %select_n.47, f32[256]{0:T(256)S(1)} %compare_select_fusion.9), kind=kOutput, calls=%fused_computation.26 | convolution fusion | flops 470679552 | bytes 5768196 | tf_op jit(solution)/shard_map/dot_general | solution.py:100
  58.8 1.6 %collective-permute-start.1 = (bf16[1,16,3584]{2,1,0:T(8,128)(2,1)S(1)}, bf16[1,16,3584]{2,1,0:T(8,128)(2,1)S(1)}, u32[]{:S(2)}, u32[]{:S(2)}) collective-permute-start(bf16[1,16,3584]{2,1,0:T(8,128)(2,1)S(1)} %fusion.40), channel_id=1, source_target_pairs={{0,2},{1,3},{2,0},{3,1},{4,6},{5,7},{6,4},{7,5},{8,10},{9,11},{10,... | collective-permute-start | bytes 344072 | tf_op jit(solution)/shard_map/ppermute | solution.py:20
  61.1 1.5 %collective-permute-start.11 = (bf16[64,1792]{1,0:T(8,128)(2,1)S(1)}, bf16[64,1792]{1,0:T(8,128)(2,1)S(1)}, u32[]{:S(2)}, u32[]{:S(2)}) collective-permute-start(bf16[64,1792]{1,0:T(8,128)(2,1)S(1)} %reshape.265), channel_id=1, source_target_pairs={{0,16},{16,0},{1,17},{17,1},{2,18},{18,2},{3,19},{19,3},{4,20},{20... | collective-permute-start | bytes 688136 | tf_op jit(solution)/shard_map/ppermute | solution.py:24
  65.0 1.6 %collective-permute-start.3 = (bf16[1,16,3584]{2,1,0:T(8,128)(2,1)S(1)}, bf16[1,16,3584]{2,1,0:T(8,128)(2,1)S(1)}, u32[]{:S(2)}, u32[]{:S(2)}) collective-permute-start(bf16[1,16,3584]{2,1,0:T(8,128)(2,1)S(1)} %get-tuple-element.14), channel_id=1, source_target_pairs={{0,2},{1,3},{2,0},{3,1},{4,6},{5,7},{6,4},{7,5},{8,10},{9,11},{10,... | collective-permute-start | bytes 344072 | tf_op jit(solution)/shard_map/ppermute | solution.py:20
  67.2 6.4 %collective-permute-done.11 = bf16[64,1792]{1,0:T(8,128)(2,1)S(1)} collective-permute-done((bf16[64,1792]{1,0:T(8,128)(2,1)S(1)}, bf16[64,1792]{1,0:T(8,128)(2,1)S(1)}, u32[]{:S(2)}, u32[]{:S(2)}) %collective-permute-start.11) | collective-permute-done | bytes 229408 | tf_op jit(solution)/shard_map/ppermute | solution.py:24
  74.6 1.7 %collective-permute-start.12 = (bf16[64,1792]{1,0:T(8,128)(2,1)S(1)}, bf16[64,1792]{1,0:T(8,128)(2,1)S(1)}, u32[]{:S(2)}, u32[]{:S(2)}) collective-permute-start(bf16[64,1792]{1,0:T(8,128)(2,1)S(1)} %collective-permute-done.11), channel_id=1, source_target_pairs={{0,2},{1,3},{2,0},{3,1},{4,6},{5,7},{6,4},{7,5},{8,10},{9,11},{10,... | collective-permute-start | bytes 688136 | tf_op jit(solution)/shard_map/ppermute | solution.py:20
  76.6 3.1 %collective-permute-done.9 = bf16[1,16,3584]{2,1,0:T(8,128)(2,1)S(1)} collective-permute-done((bf16[1,16,3584]{2,1,0:T(8,128)(2,1)S(1)}, bf16[1,16,3584]{2,1,0:T(8,128)(2,1)S(1)}, u32[]{:S(2)}, u32[]{:S(2)}) %collective-permute-start.9) | collective-permute-done | bytes 114720 | tf_op jit(solution)/shard_map/ppermute | solution.py:20
  80.8 1.6 %collective-permute-start.4 = (bf16[16,3584]{1,0:T(8,128)(2,1)S(1)}, bf16[16,3584]{1,0:T(8,128)(2,1)S(1)}, u32[]{:S(2)}, u32[]{:S(2)}) collective-permute-start(bf16[16,3584]{1,0:T(8,128)(2,1)S(1)} %get-tuple-element.23), channel_id=1, source_target_pairs={{0,4},{4,8},{8,12},{12,0},{1,5},{5,9},{9,13},{13,1},{2,6},{6,10},{... | collective-permute-start | bytes 344072 | tf_op jit(solution)/shard_map/ppermute | solution.py:24
  82.5 4.9 %collective-permute-done.17 = bf16[64,1792]{1,0:T(8,128)(2,1)S(1)} collective-permute-done((bf16[64,1792]{1,0:T(8,128)(2,1)S(1)}, bf16[64,1792]{1,0:T(8,128)(2,1)S(1)}, u32[]{:S(2)}, u32[]{:S(2)}) %collective-permute-start.17) | collective-permute-done | bytes 229408 | tf_op jit(solution)/shard_map/ppermute | solution.py:20
  87.3 2.6 %collective-permute-start.7 = (bf16[16,3584]{1,0:T(8,128)(2,1)S(1)}, bf16[16,3584]{1,0:T(8,128)(2,1)S(1)}, u32[]{:S(2)}, u32[]{:S(2)}) collective-permute-start(bf16[16,3584]{1,0:T(8,128)(2,1)S(1)} %get-tuple-element.25), channel_id=1, source_target_pairs={{0,8},{4,12},{8,0},{12,4},{1,9},{5,13},{9,1},{13,5},{2,10},{6,14},... | collective-permute-start | bytes 344072 | tf_op jit(solution)/shard_map/ppermute | solution.py:24
  93.8 1.5 %collective-permute-done.7 = bf16[16,3584]{1,0:T(8,128)(2,1)S(1)} collective-permute-done((bf16[16,3584]{1,0:T(8,128)(2,1)S(1)}, bf16[16,3584]{1,0:T(8,128)(2,1)S(1)}, u32[]{:S(2)}, u32[]{:S(2)}) %collective-permute-start.7) | collective-permute-done | bytes 114720 | tf_op jit(solution)/shard_map/ppermute | solution.py:24
  99.4 4.0 %fusion.11 = bf16[1,1792,512]{2,1,0:T(8,128)(2,1)} fusion(f32[1792,512]{1,0:T(8,128)} %fusion.26, bf16[256,1792]{1,0:T(8,128)(2,1)S(1)} %constant_dynamic-update-slice_fusion, bf16[256,512]{1,0:T(8,128)(2,1)} %collective-permute-done.15), kind=kOutput, calls=%fused_computation.20 | convolution fusion | flops 471597056 | bytes 6684672 | tf_op jit(solution)/shard_map/dot_general | solution.py:100
  103.4 3.0 %fusion.10 = bf16[1,1792,512]{2,1,0:T(8,128)(2,1)} fusion(f32[1792,512]{1,0:T(8,128)S(1)} %copy-done, bf16[256,1792]{1,0:T(8,128)(2,1)S(1)} %constant_dynamic-update-slice_fusion, bf16[256,512]{1,0:T(8,128)(2,1)} %collective-permute-done.14), kind=kOutput, calls=%fused_computation.19 | convolution fusion | flops 471597056 | bytes 6684672 | tf_op jit(solution)/shard_map/dot_general | solution.py:100
  106.5 2.9 %fusion.12 = bf16[1,1792,512]{2,1,0:T(8,128)(2,1)} fusion(f32[1792,512]{1,0:T(8,128)S(1)} %copy-done.1, bf16[256,512]{1,0:T(8,128)(2,1)} %collective-permute-done.19, bf16[128,1792]{1,0:T(8,128)(2,1)S(1)} %collective-permute-done.18, bf16[64,1792]{1,0:T(8,128)(2,1)S(1)} %collective-permute-done.17, bf16[64,1792]{1,0:T(8,128)(2,1)S(1)} %collective-permute-done.16), kind=kOutput, calls=%fused_computation.21 | convolution fusion | flops 474349568 | bytes 6684672 | tf_op jit(solution)/shard_map/dot_general | solution.py:100
  (104 shorter events, 31.9 us)
Async XLA Ops:
  0.6 10.0 %copy-start.2 = (bf16[1,1,64,4,3584]{4,3,2,1,0:T(4,128)(2,1)S(1)}, bf16[1,1,64,4,3584]{4,3,2,1,0:T(4,128)(2,1)}, u32[]{:S(2)}) copy-start(bf16[1,1,64,4,3584]{4,3,2,1,0:T(4,128)(2,1)} %param.11) | copy-start | bytes 5505028
  3.7 70.4 %collective-permute-start.16 = (bf16[64,1792]{1,0:T(8,128)(2,1)}, bf16[64,1792]{1,0:T(8,128)(2,1)S(1)}, u32[]{:S(2)}, u32[]{:S(2)}) collective-permute-start(bf16[64,1792]{1,0:T(8,128)(2,1)} %multiply_convert_fusion.4), channel_id=1, source_target_pairs={{0,16},{16,0},{1,17},{17,1},{2,18},{18,2},{3,19},{19,3},{4,20},{20... | collective-permute-start | bytes 688136 | tf_op jit(solution)/shard_map/ppermute | solution.py:24
  37.8 20.0 %collective-permute-start = (bf16[2,16,3584]{2,1,0:T(8,128)(2,1)}, bf16[2,16,3584]{2,1,0:T(8,128)(2,1)}, u32[]{:S(2)}, u32[]{:S(2)}) collective-permute-start(bf16[2,16,3584]{2,1,0:T(8,128)(2,1)} %pad_maximum_fusion.3), channel_id=1, source_target_pairs={{0,1},{1,0},{2,3},{3,2},{4,5},{5,4},{6,7},{7,6},{8,9},{9,8},{10,11... | collective-permute-start | bytes 688136 | tf_op jit(solution)/shard_map/ppermute | solution.py:20
  38.5 21.9 %collective-permute-start.5 = (bf16[2,16,3584]{2,1,0:T(8,128)(2,1)}, bf16[2,16,3584]{2,1,0:T(8,128)(2,1)S(1)}, u32[]{:S(2)}, u32[]{:S(2)}) collective-permute-start(bf16[2,16,3584]{2,1,0:T(8,128)(2,1)} %pad_maximum_fusion.5), channel_id=1, source_target_pairs={{0,1},{1,0},{2,3},{3,2},{4,5},{5,4},{6,7},{7,6},{8,9},{9,8},{10,11... | collective-permute-start | bytes 688136 | tf_op jit(solution)/shard_map/ppermute | solution.py:20
  39.8 21.3 %collective-permute-start.8 = (bf16[2,16,3584]{2,1,0:T(8,128)(2,1)}, bf16[2,16,3584]{2,1,0:T(8,128)(2,1)}, u32[]{:S(2)}, u32[]{:S(2)}) collective-permute-start(bf16[2,16,3584]{2,1,0:T(8,128)(2,1)} %pad_maximum_fusion.6), channel_id=1, source_target_pairs={{0,1},{1,0},{2,3},{3,2},{4,5},{5,4},{6,7},{7,6},{8,9},{9,8},{10,11... | collective-permute-start | bytes 688136 | tf_op jit(solution)/shard_map/ppermute | solution.py:20
  40.5 22.1 %collective-permute-start.2 = (bf16[2,16,3584]{2,1,0:T(8,128)(2,1)}, bf16[2,16,3584]{2,1,0:T(8,128)(2,1)}, u32[]{:S(2)}, u32[]{:S(2)}) collective-permute-start(bf16[2,16,3584]{2,1,0:T(8,128)(2,1)} %pad_maximum_fusion.4), channel_id=1, source_target_pairs={{0,1},{1,0},{2,3},{3,2},{4,5},{5,4},{6,7},{7,6},{8,9},{9,8},{10,11... | collective-permute-start | bytes 688136 | tf_op jit(solution)/shard_map/ppermute | solution.py:20
  51.6 6.2 %copy-start.3 = (bf16[256,3584]{1,0:T(8,128)(2,1)S(1)}, bf16[256,3584]{1,0:T(8,128)(2,1)}, u32[]{:S(2)}) copy-start(bf16[256,3584]{1,0:T(8,128)(2,1)} %fusion) | copy-start | bytes 5505028
  58.8 5.1 %collective-permute-start.1 = (bf16[1,16,3584]{2,1,0:T(8,128)(2,1)S(1)}, bf16[1,16,3584]{2,1,0:T(8,128)(2,1)S(1)}, u32[]{:S(2)}, u32[]{:S(2)}) collective-permute-start(bf16[1,16,3584]{2,1,0:T(8,128)(2,1)S(1)} %fusion.40), channel_id=1, source_target_pairs={{0,2},{1,3},{2,0},{3,1},{4,6},{5,7},{6,4},{7,5},{8,10},{9,11},{10,... | collective-permute-start | bytes 344072 | tf_op jit(solution)/shard_map/ppermute | solution.py:20
  60.5 15.8 %copy-start.8 = (bf16[2,16,3584]{2,1,0:T(8,128)(2,1)}, bf16[2,16,3584]{2,1,0:T(8,128)(2,1)S(1)}, u32[]{:S(2)}) copy-start(bf16[2,16,3584]{2,1,0:T(8,128)(2,1)S(1)} %collective-permute-done.5) | copy-start | bytes 688132
  60.5 46.0 %collective-permute-start.19 = (bf16[256,512]{1,0:T(8,128)(2,1)}, bf16[256,512]{1,0:T(8,128)(2,1)}, u32[]{:S(2)}, u32[]{:S(2)}) collective-permute-start(bf16[256,512]{1,0:T(8,128)(2,1)} %bitcast.41), channel_id=1, source_target_pairs={{0,16},{16,0},{1,17},{17,1},{2,18},{18,2},{3,19},{19,3},{4,20},{20... | collective-permute-start | bytes 786440 | tf_op jit(solution)/shard_map/ppermute | solution.py:24
  61.1 12.5 %collective-permute-start.11 = (bf16[64,1792]{1,0:T(8,128)(2,1)S(1)}, bf16[64,1792]{1,0:T(8,128)(2,1)S(1)}, u32[]{:S(2)}, u32[]{:S(2)}) collective-permute-start(bf16[64,1792]{1,0:T(8,128)(2,1)S(1)} %reshape.265), channel_id=1, source_target_pairs={{0,16},{16,0},{1,17},{17,1},{2,18},{18,2},{3,19},{19,3},{4,20},{20... | collective-permute-start | bytes 688136 | tf_op jit(solution)/shard_map/ppermute | solution.py:24
  65.0 9.5 %collective-permute-start.3 = (bf16[1,16,3584]{2,1,0:T(8,128)(2,1)S(1)}, bf16[1,16,3584]{2,1,0:T(8,128)(2,1)S(1)}, u32[]{:S(2)}, u32[]{:S(2)}) collective-permute-start(bf16[1,16,3584]{2,1,0:T(8,128)(2,1)S(1)} %get-tuple-element.14), channel_id=1, source_target_pairs={{0,2},{1,3},{2,0},{3,1},{4,6},{5,7},{6,4},{7,5},{8,10},{9,11},{10,... | collective-permute-start | bytes 344072 | tf_op jit(solution)/shard_map/ppermute | solution.py:20
  66.6 9.7 %collective-permute-start.6 = (bf16[1,16,3584]{2,1,0:T(8,128)(2,1)S(1)}, bf16[1,16,3584]{2,1,0:T(8,128)(2,1)S(1)}, u32[]{:S(2)}, u32[]{:S(2)}) collective-permute-start(bf16[1,16,3584]{2,1,0:T(8,128)(2,1)S(1)} %get-tuple-element.13), channel_id=1, source_target_pairs={{0,2},{1,3},{2,0},{3,1},{4,6},{5,7},{6,4},{7,5},{8,10},{9,11},{10,... | collective-permute-start | bytes 344072 | tf_op jit(solution)/shard_map/ppermute | solution.py:20
  73.6 6.1 %collective-permute-start.9 = (bf16[1,16,3584]{2,1,0:T(8,128)(2,1)S(1)}, bf16[1,16,3584]{2,1,0:T(8,128)(2,1)S(1)}, u32[]{:S(2)}, u32[]{:S(2)}) collective-permute-start(bf16[1,16,3584]{2,1,0:T(8,128)(2,1)S(1)} %get-tuple-element.12), channel_id=1, source_target_pairs={{0,2},{1,3},{2,0},{3,1},{4,6},{5,7},{6,4},{7,5},{8,10},{9,11},{10,... | collective-permute-start | bytes 344072 | tf_op jit(solution)/shard_map/ppermute | solution.py:20
  74.2 25.2 %collective-permute-start.15 = (bf16[256,512]{1,0:T(8,128)(2,1)}, bf16[256,512]{1,0:T(8,128)(2,1)}, u32[]{:S(2)}, u32[]{:S(2)}) collective-permute-start(bf16[256,512]{1,0:T(8,128)(2,1)} %bitcast.38), channel_id=1, source_target_pairs={{0,16},{16,0},{1,17},{17,1},{2,18},{18,2},{3,19},{19,3},{4,20},{20... | collective-permute-start | bytes 786440 | tf_op jit(solution)/shard_map/ppermute | solution.py:24
  74.6 16.2 %collective-permute-start.12 = (bf16[64,1792]{1,0:T(8,128)(2,1)S(1)}, bf16[64,1792]{1,0:T(8,128)(2,1)S(1)}, u32[]{:S(2)}, u32[]{:S(2)}) collective-permute-start(bf16[64,1792]{1,0:T(8,128)(2,1)S(1)} %collective-permute-done.11), channel_id=1, source_target_pairs={{0,2},{1,3},{2,0},{3,1},{4,6},{5,7},{6,4},{7,5},{8,10},{9,11},{10,... | collective-permute-start | bytes 688136 | tf_op jit(solution)/shard_map/ppermute | solution.py:20
  76.3 11.0 %collective-permute-start.17 = (bf16[64,1792]{1,0:T(8,128)(2,1)S(1)}, bf16[64,1792]{1,0:T(8,128)(2,1)S(1)}, u32[]{:S(2)}, u32[]{:S(2)}) collective-permute-start(bf16[64,1792]{1,0:T(8,128)(2,1)S(1)} %collective-permute-done.16), channel_id=1, source_target_pairs={{0,2},{1,3},{2,0},{3,1},{4,6},{5,7},{6,4},{7,5},{8,10},{9,11},{10,... | collective-permute-start | bytes 688136 | tf_op jit(solution)/shard_map/ppermute | solution.py:20
  80.8 12.1 %collective-permute-start.4 = (bf16[16,3584]{1,0:T(8,128)(2,1)S(1)}, bf16[16,3584]{1,0:T(8,128)(2,1)S(1)}, u32[]{:S(2)}, u32[]{:S(2)}) collective-permute-start(bf16[16,3584]{1,0:T(8,128)(2,1)S(1)} %get-tuple-element.23), channel_id=1, source_target_pairs={{0,4},{4,8},{8,12},{12,0},{1,5},{5,9},{9,13},{13,1},{2,6},{6,10},{... | collective-permute-start | bytes 344072 | tf_op jit(solution)/shard_map/ppermute | solution.py:24
  87.3 8.0 %collective-permute-start.7 = (bf16[16,3584]{1,0:T(8,128)(2,1)S(1)}, bf16[16,3584]{1,0:T(8,128)(2,1)S(1)}, u32[]{:S(2)}, u32[]{:S(2)}) collective-permute-start(bf16[16,3584]{1,0:T(8,128)(2,1)S(1)} %get-tuple-element.25), channel_id=1, source_target_pairs={{0,8},{4,12},{8,0},{12,4},{1,9},{5,13},{9,1},{13,5},{2,10},{6,14},... | collective-permute-start | bytes 344072 | tf_op jit(solution)/shard_map/ppermute | solution.py:24
  90.7 5.3 %collective-permute-start.10 = (bf16[16,3584]{1,0:T(8,128)(2,1)S(1)}, bf16[16,3584]{1,0:T(8,128)(2,1)S(1)}, u32[]{:S(2)}, u32[]{:S(2)}) collective-permute-start(bf16[16,3584]{1,0:T(8,128)(2,1)S(1)} %get-tuple-element.24), channel_id=1, source_target_pairs={{0,12},{4,0},{8,4},{12,8},{1,13},{5,1},{9,5},{13,9},{2,14},{6,2},{... | collective-permute-start | bytes 344072 | tf_op jit(solution)/shard_map/ppermute | solution.py:24
  92.9 10.5 %collective-permute-start.14 = (bf16[256,512]{1,0:T(8,128)(2,1)}, bf16[256,512]{1,0:T(8,128)(2,1)}, u32[]{:S(2)}, u32[]{:S(2)}) collective-permute-start(bf16[256,512]{1,0:T(8,128)(2,1)} %bitcast.35), channel_id=1, source_target_pairs={{0,16},{16,0},{1,17},{17,1},{2,18},{18,2},{3,19},{19,3},{4,20},{20... | collective-permute-start | bytes 786440 | tf_op jit(solution)/shard_map/ppermute | solution.py:24
  95.3 11.2 %collective-permute-start.18 = (bf16[128,1792]{1,0:T(8,128)(2,1)}, bf16[128,1792]{1,0:T(8,128)(2,1)S(1)}, u32[]{:S(2)}, u32[]{:S(2)}) collective-permute-start(bf16[128,1792]{1,0:T(8,128)(2,1)} %pad_maximum_fusion.2), channel_id=1, source_target_pairs={{0,1},{1,0},{2,3},{3,2},{4,5},{5,4},{6,7},{7,6},{8,9},{9,8},{10,11... | collective-permute-start | bytes 1376264 | tf_op jit(solution)/shard_map/ppermute | solution.py:20
  96.0 2.2 %collective-permute-start.13 = (bf16[128,1792]{1,0:T(8,128)(2,1)}, bf16[128,1792]{1,0:T(8,128)(2,1)}, u32[]{:S(2)}, u32[]{:S(2)}) collective-permute-start(bf16[128,1792]{1,0:T(8,128)(2,1)} %pad_maximum_fusion.1), channel_id=1, source_target_pairs={{0,1},{1,0},{2,3},{3,2},{4,5},{5,4},{6,7},{7,6},{8,9},{9,8},{10,11... | collective-permute-start | bytes 1376264 | tf_op jit(solution)/shard_map/ppermute | solution.py:20
  97.9 5.5 %copy-start = (f32[1792,512]{1,0:T(8,128)S(1)}, f32[1792,512]{1,0:T(8,128)}, u32[]{:S(2)}) copy-start(f32[1792,512]{1,0:T(8,128)} %fusion.28) | copy-start | bytes 11010052
  (9 other events, 31.1 us)

commit v2 on v1

v2 whole, which is shorter than its diff:
```python
import functools

import jax
import jax.numpy as jnp
from jax import lax
from jax.experimental import pallas as pl
from jax.experimental.pallas import tpu as pltpu
from jax.sharding import PartitionSpec as P

F32, BF16 = jnp.float32, jnp.bfloat16
VMEM_LIMIT = 56 * 1024 * 1024


def dot(a, b, contract_a, contract_b):
    return lax.dot_general(a, b, (((contract_a,), (contract_b,)), ((), ())), preferred_element_type=F32)


def flat_rows(block):
    return block.reshape(block.shape[0] * block.shape[1], block.shape[2])


def log2(n):
    assert n & (n - 1) == 0
    return n.bit_length() - 1


def halving_order(size):
    order = [0]
    for i in reversed(range(log2(size))):
        order = order + [d ^ (1 << i) for d in order]
    return order


def bit_reverse(value, bits):
    out = jnp.zeros_like(value)
    for i in range(bits):
        out = out | (((value >> i) & 1) << (bits - 1 - i))
    return out


def forward_kernel(locals_, chunk, tok_hbm, grad_hbm, factor_ref, wg_hbm, wu_hbm, wd_hbm,
                   pair_hbm, hid_hbm, own_hbm, send_hbm,
                   tok, grad, wg, wu, wd, acc_g, acc_u, acc_h, pair, hid, total, in_sem, out_sem):
    slots, nodes, width = tok.shape
    rows = slots * nodes
    keep = slots // locals_
    steps = width // chunk
    me, node = lax.axis_index("local"), lax.axis_index("node")

    def fetch(i):
        cols = pl.ds(i * chunk, chunk)
        pairs = [(tok_hbm.at[:, :, cols], tok.at[:, :, cols]), (wg_hbm.at[cols], wg.at[cols]), (wu_hbm.at[cols], wu.at[cols]),
                 (grad_hbm.at[:, :, cols], grad.at[:, :, cols]), (wd_hbm.at[cols], wd.at[cols])]
        return [pltpu.make_async_copy(src, dst, in_sem.at[i, n]) for n, (src, dst) in enumerate(pairs)]

    for i in range(steps):
        for copy in fetch(i):
            copy.start()
    for i in range(steps):
        cols = pl.ds(i * chunk, chunk)
        copies = fetch(i)
        for copy in copies[:3]:
            copy.wait()
        t = flat_rows(tok[:, :, cols])
        gate = dot(t, wg[cols], 1, 0)
        up = dot(t, wu[cols], 1, 0)
        for copy in copies[3:]:
            copy.wait()
        scaled = (flat_rows(grad[:, :, cols].astype(F32)) * factor_ref[...]).astype(BF16)
        back = dot(scaled, wd[cols], 1, 0)
        if i:
            acc_g[...] += gate
            acc_u[...] += up
            acc_h[...] += back
        else:
            acc_g[...] = gate
            acc_u[...] = up
            acc_h[...] = back

    band = 64

    def activate(i, carry):
        at = pl.ds(pl.multiple_of(i * band, band), band)
        gate, up, back = acc_g[at], acc_u[at], acc_h[at]
        sig = jax.nn.sigmoid(gate)
        act = gate * sig
        hid[at] = (act * up).astype(BF16)
        pair[0, at] = (back * up * sig * (1.0 + gate * (1.0 - sig))).astype(BF16)
        pair[1, at] = (back * act).astype(BF16)
        return carry

    lax.fori_loop(0, rows // band, activate, 0)
    acts_out = [pltpu.make_async_copy(pair, pair_hbm, out_sem.at[0]), pltpu.make_async_copy(hid, hid_hbm, out_sem.at[1])]
    for copy in acts_out:
        copy.start()

    p = lax.broadcasted_iota(jnp.int32, (rows, rows), 0)
    j = p & (keep - 1)
    low = (p >> log2(keep)) & (locals_ // 2 - 1)
    k = (p >> log2(keep * locals_ // 2)) & (nodes - 1)
    high = p >> (log2(rows) - 1)
    place = bit_reverse(high * (locals_ // 2) + low, log2(locals_)) ^ me
    index = (place * keep + j) * nodes + ((node + k) & (nodes - 1))
    one_hot = jnp.where(index == lax.broadcasted_iota(jnp.int32, (rows, rows), 1), 1.0, 0.0).astype(BF16)
    gate_moved = dot(one_hot, pair[0], 1, 0).astype(BF16)
    up_moved = dot(one_hot, pair[1], 1, 0).astype(BF16)
    half = rows // 2

    def leave(i):
        cols = pl.ds(i * chunk, chunk)
        return [pltpu.make_async_copy(total.at[:half, cols], own_hbm.at[:, cols], out_sem.at[2 + 2 * i]),
                pltpu.make_async_copy(total.at[half:, cols], send_hbm.at[:, cols], out_sem.at[3 + 2 * i])]

    for i in range(steps):
        cols = pl.ds(i * chunk, chunk)
        total[:, cols] = (dot(gate_moved, wg[cols], 1, 1) + dot(up_moved, wu[cols], 1, 1)).astype(BF16)
        for copy in leave(i):
            copy.start()
    for copy in acts_out:
        copy.wait()
    for i in range(steps):
        for copy in leave(i):
            copy.wait()


def forward(locals_, tokens, grads, factor, gate_weight, up_weight, down_weight):
    slots, nodes, width = tokens.shape
    rows = slots * nodes
    hid_local = gate_weight.shape[1]
    chunk = 512
    steps = width // chunk
    hbm = pl.BlockSpec(memory_space=pl.ANY)
    weight = pltpu.VMEM(gate_weight.shape, BF16)
    acc = pltpu.VMEM((rows, hid_local), F32)
    return pl.pallas_call(
        functools.partial(forward_kernel, locals_, chunk),
        out_shape=[
            jax.ShapeDtypeStruct((2, rows, hid_local), BF16),
            jax.ShapeDtypeStruct((rows, hid_local), BF16),
            jax.ShapeDtypeStruct((rows // 2, width), BF16),
            jax.ShapeDtypeStruct((rows // 2, width), BF16),
        ],
        in_specs=[hbm, hbm, pl.BlockSpec(memory_space=pltpu.VMEM), hbm, hbm, hbm],
        out_specs=[hbm] * 4,
        scratch_shapes=[
            pltpu.VMEM(tokens.shape, BF16), pltpu.VMEM(tokens.shape, BF16), weight, weight, weight, acc, acc, acc,
            pltpu.VMEM((2, rows, hid_local), BF16), pltpu.VMEM((rows, hid_local), BF16), pltpu.VMEM((rows, width), BF16),
            pltpu.SemaphoreType.DMA((steps, 5)), pltpu.SemaphoreType.DMA((2 + 2 * steps,)),
        ],
        compiler_params=pltpu.CompilerParams(vmem_limit_bytes=VMEM_LIMIT),
        cost_estimate=pl.CostEstimate(flops=10 * rows * width * hid_local, bytes_accessed=18_000_000, transcendentals=0),
        name="forward",
    )(tokens, grads, factor, gate_weight, up_weight, down_weight)


def weight_kernel(order, count, scaled, *refs):
    rows_ref, factor_ref = refs[0], refs[1]
    shares = refs[2:2 + len(order)]
    own_refs = refs[2 + len(order):2 + len(order) + count]
    there_refs = refs[2 + len(order) + count:2 + len(order) + 2 * count]
    outs = refs[2 + len(order) + 2 * count:2 + len(order) + 3 * count]
    me = lax.axis_index("local")
    own = flat_rows(rows_ref[...])
    if scaled:
        own = (own.astype(F32) * factor_ref[...]).astype(BF16)
    left = jnp.concatenate([own] + [flat_rows(s[0]) for s in shares], axis=0)
    block = shares[0].shape[1] * shares[0].shape[2]
    for own_ref, there_ref, out in zip(own_refs, there_refs, outs):
        own_act = own_ref[...].reshape(own_ref.shape[-2:])
        there = there_ref.at[0] if len(there_ref.shape) == 3 else there_ref
        right = jnp.concatenate(
            [own_act] + [there[pl.ds(pl.multiple_of((me ^ d) * block, block), block), :] for d in order], axis=0)
        out[...] = dot(left, right, 0, 0).astype(BF16)


def weight_grads(order, scaled, replica, rows3, factor, shares, own_acts, there_acts, count):
    slots, nodes, width = rows3.shape
    part = shares[0].shape[-1]
    hid_local = own_acts.shape[-1]
    fb = 256
    per = part // fb
    which = 1 if scaled else 0
    rows = slots * nodes
    if count == 1:
        acts = [own_acts]
        theres = [there_acts]
        act_specs = [pl.BlockSpec((rows, hid_local), lambda i, r: (0, 0))]
    else:
        acts = [own_acts] * count
        theres = [there_acts] * count
        act_specs = [pl.BlockSpec((1, rows, hid_local), functools.partial(lambda n, i, r: (n, 0, 0), n)) for n in range(count)]
    out = pl.pallas_call(
        functools.partial(weight_kernel_prefetch, order, count, scaled),
        out_shape=[jax.ShapeDtypeStruct((part, hid_local), BF16)] * count,
        grid_spec=pltpu.PrefetchScalarGridSpec(
            num_scalar_prefetch=1,
            grid=(per,),
            in_specs=[pl.BlockSpec((slots, nodes, fb), lambda i, r: (0, 0, r[0] * per + i)),
                      pl.BlockSpec((rows, 1), lambda i, r: (0, 0))]
            + [pl.BlockSpec((1,) + shares[0].shape[1:3] + (fb,), lambda i, r: (which, 0, 0, i))] * len(shares)
            + act_specs + act_specs,
            out_specs=[pl.BlockSpec((fb, hid_local), lambda i, r: (i, 0))] * count,
        ),
        compiler_params=pltpu.CompilerParams(vmem_limit_bytes=VMEM_LIMIT),
        cost_estimate=pl.CostEstimate(flops=4 * rows * part * hid_local * count, bytes_accessed=4_000_000, transcendentals=0),
        name="weight_grads",
    )(replica, rows3, factor, *shares, *acts, *theres)
    return out


def weight_kernel_prefetch(order, count, scaled, replica_ref, *refs):
    weight_kernel(order, count, scaled, *refs)


def collect_kernel(*refs):
    *arrived, kept, came, out = refs
    keep, nodes, width = out.shape
    node = lax.axis_index("node")
    last = (kept[...].astype(F32) + came[...].astype(F32)).astype(BF16)
    stacked = jnp.concatenate([last] + [a[...] for a in arrived], axis=0)
    rows = keep * nodes
    p = lax.broadcasted_iota(jnp.int32, (rows, rows), 0)
    source = ((node - (p & (nodes - 1))) & (nodes - 1)) * keep + (p >> log2(nodes))
    one_hot = jnp.where(source == lax.broadcasted_iota(jnp.int32, (rows, rows), 1), 1.0, 0.0).astype(BF16)
    out[...] = dot(one_hot, stacked, 1, 0).astype(BF16).reshape(out.shape)


def on_device(tokens_in, grad_rows, combine_weights, live_counts, w_gate, w_up, w_down):
    slots, nodes, width = tokens_in.shape[2:]
    replicas, locals_ = lax.axis_size("dp"), lax.axis_size("local")
    assert replicas == 2
    replica, local = lax.axis_index("dp"), lax.axis_index("local")
    keep = slots // locals_
    part = width // replicas
    rows = slots * nodes
    gate_weight, up_weight, down_weight = w_gate[0], w_up[0], w_down[0]
    tokens, grads = tokens_in[0, 0], grad_rows[0, 0]
    live = (lax.broadcasted_iota(jnp.int32, (slots, nodes), 0) < live_counts[0, 0][None, :]).astype(F32)
    factor = combine_weights[0, 0] * live
    column = factor.reshape(rows, 1)
    order = halving_order(locals_)
    bits = [1 << i for i in range(log2(locals_))]

    def swap_local(value, bit):
        return lax.ppermute(value, "local", [(i, i ^ bit) for i in range(locals_)])

    def swap_dp(value):
        return lax.ppermute(value, "dp", [(0, 1), (1, 0)])

    start = (local * keep, 0, (1 - replica) * part)
    token_share = lax.dynamic_slice(tokens, start, (keep, nodes, part))
    grad_share = lax.dynamic_slice(grads, start, (keep, nodes, part))
    factor_share = lax.dynamic_slice(factor, (local * keep, 0), (keep, nodes))
    scaled_share = (grad_share.astype(F32) * factor_share[:, :, None]).astype(BF16)
    shares = [swap_dp(jnp.stack((token_share, scaled_share)))]
    for bit in reversed(bits):
        shares = shares + [swap_local(v, bit) for v in shares]

    pair, hidden, own, send = forward(locals_, tokens, grads, column, gate_weight, up_weight, down_weight)
    pair_there = swap_dp(pair)
    hidden_there = swap_dp(hidden)

    came = swap_local(send, bits[0])
    size = locals_ // 2
    own = own.reshape(nodes, size * keep, width)
    came = came.reshape(nodes, size * keep, width)
    arrived = [None] * nodes
    for k in list(range(1, nodes)) + [0]:
        mine, other = own[k], came[k]
        n = size
        for bit in bits[1:]:
            total = (mine.astype(F32) + other.astype(F32)).astype(BF16)
            n //= 2
            mine = total[: n * keep]
            other = swap_local(total[n * keep :], bit)
        if k:
            arrived[k] = lax.ppermute((mine.astype(F32) + other.astype(F32)).astype(BF16), "node",
                                      [(i, (i + k) % nodes) for i in range(nodes)])
        else:
            arrived[0] = (mine, other)
    d_tokens = pl.pallas_call(
        collect_kernel,
        out_shape=jax.ShapeDtypeStruct((keep, nodes, width), BF16),
        compiler_params=pltpu.CompilerParams(vmem_limit_bytes=VMEM_LIMIT),
        name="collect",
    )(*arrived[1:], *arrived[0])

    where = replica.reshape(1).astype(jnp.int32)
    grad_gate, grad_up = weight_grads(order, False, where, tokens, column, shares, pair, pair_there, 2)
    (grad_down,) = weight_grads(order, True, where, grads, column, shares, hidden, hidden_there, 1)
    return d_tokens[None, None], grad_gate[None], grad_up[None], grad_down[None]


def solution(mesh):
    return jax.shard_map(
        on_device,
        mesh=mesh,
        in_specs=(
            P("dp", "node", None, None, None),
            P("dp", "node", None, None, None),
            P("dp", "node", None, None),
            P("dp", "node", None),
            P("node", None, "local"),
            P("node", None, "local"),
            P("node", None, "local"),
        ),
        out_specs=(
            P("dp", "node", "local", None, None),
            P("node", "dp", "local"),
            P("node", "dp", "local"),
            P("node", "dp", "local"),
        ),
        check_vma=False,
    )
```

time: 110 us -> 82.7 us (0.75)
  matrix products: 37.5 us -> 0 us
  Pallas kernels: 0 us -> 26.7 us
  local copies, waits for them, and re-layouts: 19.7 us -> 5.39 us
  other arithmetic: 13.7 us -> 3.19 us
  waiting for transfers between devices: 18.3 us -> 28.6 us
  starting transfers between devices: 19.2 us -> 17.5 us
    dot_general x11 -> x0, matrix products: 37.5 us -> none  [the longest x6 20.5 us: weight_grad(): lax.dot_general(a, b, (((0,), (0,)), ((), ())), preferred_element_type=jn...]
    pallas_call x0 -> x4, Pallas kernels: none -> 26.7 us  [the longest x2 14 us: weight_grads(): pl.pallas_call(functools.partial(weight_kernel_prefetch, order, count, sc...]
    ppermute x8 -> x6, waiting for transfers between devices: 8.67 us -> 15.3 us  [the longest x3 11.3 us: swap_dp(): return lax.ppermute(value, 'dp', [(0, 1), (1, 0)])]
    convert_element_type x3 -> x0, local copies, waits for them, and re-layouts: 6.08 us -> none  [the longest x1 3.9 us: on_device(): (grads.astype(jnp.float32) * factor[:, :, None]).astype(jnp.bfloat16)]
    convert_element_type x6 -> x5, other arithmetic: 7.17 us -> 1.39 us  [the longest x1 1.09 us: on_device(): (grad_share.astype(F32) * factor_share[:, :, None]).astype(BF16)]
    another operation x2 -> x1, local copies, waits for them, and re-layouts: 5.22 us -> 1.03 us  [on_device(): shares = [swap_dp(jnp.stack((token_share, scaled_share)))]]
    ppermute x12 -> x8, waiting for transfers between devices: 9.59 us -> 13.4 us  [swap_local(): return lax.ppermute(value, 'local', [(i, i ^ bit) for i in range(locals_)])]
    another operation x5 -> x1, other arithmetic: 2.93 us -> 0.32 us  [on_device(): shares = [swap_dp(jnp.stack((token_share, scaled_share)))]]
  transfers between devices with their start and end apart: 20 -> 14, of which waited for: 7 -> 7; matrix products, arithmetic and copies ran while one was open for 58% -> 4% of each run, Pallas kernels for 0% -> 11%
where the time goes in v2:
time: 82.7 us; the launch traced here: 82.2 us
  waiting for transfers between devices  28.6 us (35%)
  Pallas kernels  26.7 us (32%)
  starting transfers between devices  17.5 us (21%)
  local copies, waits for them, and re-layouts  5.39 us (7%)
  other arithmetic  3.19 us (4%)
  between operations  0.83 us (1%)
    pallas_call x2, Pallas kernels, weight_grads(): pl.pallas_call(functools.partial(weight_kernel_prefetch, order, count, sc...  14 us
    ppermute x8, waiting for transfers between devices, swap_local(): return lax.ppermute(value, 'local', [(i, i ^ bit) for i in range(locals_)])  13.4 us
    ppermute x3, waiting for transfers between devices, swap_dp(): return lax.ppermute(value, 'dp', [(0, 1), (1, 0)])  11.3 us
    pallas_call x1, Pallas kernels, forward(): pl.pallas_call(functools.partial(forward_kernel, locals_, chunk), out_sha...  10.5 us
    ppermute x8, starting transfers between devices, swap_local(): return lax.ppermute(value, 'local', [(i, i ^ bit) for i in range(locals_)])  6.75 us
    ppermute x3, starting transfers between devices, on_device(): lax.ppermute((mine.astype(F32) + other.astype(F32)).astype(BF16), 'node',...  6.41 us
    ppermute x3, starting transfers between devices, swap_dp(): return lax.ppermute(value, 'dp', [(0, 1), (1, 0)])  4.29 us
    ppermute x3, waiting for transfers between devices, on_device(): lax.ppermute((mine.astype(F32) + other.astype(F32)).astype(BF16), 'node',...  4 us
  transfers between devices with their start and end apart: 14, of which 7 were waited for; matrix products, arithmetic and copies ran while one was open for 4% of the time, Pallas kernels for 11%

profile of v2, /device:TPU:0, one launch (start us, length us, event | category | flops | bytes accessed | tf_op | source)
XLA Modules:
  0.0 82.2 jit_solution(6976170728202605148)
XLA Ops:
  0.6 0.7 iota_compare_fusion
  1.6 0.8 copy.15
  2.5 0.7 broadcast_select_fusion.factor_ref.refs_1_
  3.1 10.5 %forward.1 = (bf16[2,256,512]{2,1,0:T(8,128)(2,1)}, bf16[256,512]{1,0:T(8,128)(2,1)}, bf16[128,3584]{1,0:T(8,128)(2,1)}, bf16[128,3584]{1,0:T(8,128)(2,1)}) custom-call(bf16[64,4,3584]{2,1,0:T(4,128)(2,1)} %bitcast.24, bf16[64,4,3584]{2,1,0:T(4,128)(2,1)} %bitcast.20, f32[256,1]{1,0:T(8,128)} %broadcast_select_fusion.factor_ref.refs_1_, ...), custom_call_target="tpu_custom_call" | custom-call | flops 4697620480 | bytes 18000000 | tf_op jit(solution)/shard_map/forward/pallas_call | solution.py:135
  14.4 1.1 %fusion = bf16[1,16,4,1792]{3,2,1,0:T(4,128)(2,1)S(1)} fusion(f32[16,4]{1,0:T(8,128)S(1)} %copy.18, bf16[1,1,64,4,3584]{4,3,2,1,0:T(4,128)(2,1)} %param.8, s32[]{:T(128)S(6)} %select_n.4, s32[]{:T(128)S(6)} %select_n.10), kind=kLoop, calls=%fused_computation.2 | loop fusion | flops 344064 | bytes 459016 | tf_op jit(solution)/shard_map/convert_element_type | solution.py:254
  15.5 1.0 %dynamic-slice_bitcast_fusion = bf16[1,16,4,1792]{3,2,1,0:T(4,128)(2,1)S(1)} fusion(bf16[1,1,64,4,3584]{4,3,2,1,0:T(4,128)(2,1)} %param.7, s32[]{:T(128)S(6)} %select_n.4, s32[]{:T(128)S(6)} %select_n.10), kind=kLoop, calls=%fused_computation.7 | loop fusion | bytes 458760 | tf_op jit(solution)/shard_map/stack | solution.py:255
  16.9 2.7 %collective-permute-start.8 = (bf16[2,16,4,1792]{3,2,1,0:T(4,128)(2,1)S(1)}, bf16[2,16,4,1792]{3,2,1,0:T(4,128)(2,1)S(1)}, u32[]{:S(2)}, u32[]{:S(2)}) collective-permute-start(bf16[2,16,4,1792]{3,2,1,0:T(4,128)(2,1)S(1)} %pad_maximum_fusion), channel_id=1, source_target_pairs={{0,16},{16,0},{1,17},{17,1},{2,18},{18,2},{3,19},{19,3},{4,20},{20... | collective-permute-start | bytes 1376264 | tf_op jit(solution)/shard_map/ppermute | solution.py:248
  19.7 11.3 %collective-permute-done.8.refs_2_ = bf16[2,16,4,1792]{3,2,1,0:T(4,128)(2,1)S(1)} collective-permute-done((bf16[2,16,4,1792]{3,2,1,0:T(4,128)(2,1)S(1)}, bf16[2,16,4,1792]{3,2,1,0:T(4,128)(2,1)S(1)}, u32[]{:S(2)}, u32[]{:S(2)}) %collective-permute-start.8) | collective-permute-done | bytes 458784 | tf_op jit(solution)/shard_map/ppermute | solution.py:248
  30.9 2.0 %collective-permute-start.9 = (bf16[2,16,4,1792]{3,2,1,0:T(4,128)(2,1)S(1)}, bf16[2,16,4,1792]{3,2,1,0:T(4,128)(2,1)S(1)}, u32[]{:S(2)}, u32[]{:S(2)}) collective-permute-start(bf16[2,16,4,1792]{3,2,1,0:T(4,128)(2,1)S(1)} %collective-permute-done.8.refs_2_), channel_id=1, source_target_pairs={{0,2},{1,3},{2,0},{3,1},{4,6},{5,7},{6,4},{7,5},{8,10},{9,11},{10,... | collective-permute-start | bytes 1376264 | tf_op jit(solution)/shard_map/ppermute | solution.py:245
  33.3 2.0 %collective-permute-start.3 = (bf16[16,3584]{1,0:T(8,128)(2,1)S(1)}, bf16[16,3584]{1,0:T(8,128)(2,1)S(1)}, u32[]{:S(2)}, u32[]{:S(2)}) collective-permute-start(bf16[16,3584]{1,0:T(8,128)(2,1)S(1)} %slice.77), channel_id=1, source_target_pairs={{0,2},{1,3},{2,0},{3,1},{4,6},{5,7},{6,4},{7,5},{8,10},{9,11},{10,... | collective-permute-start | bytes 344072 | tf_op jit(solution)/shard_map/ppermute | solution.py:245
  36.0 10.6 %collective-permute-done.1 = bf16[16,3584]{1,0:T(8,128)(2,1)S(1)} collective-permute-done((bf16[16,3584]{1,0:T(8,128)(2,1)S(1)}, bf16[16,3584]{1,0:T(8,128)(2,1)S(1)}, u32[]{:S(2)}, u32[]{:S(2)}) %collective-permute-start.1) | collective-permute-done | bytes 114720 | tf_op jit(solution)/shard_map/ppermute | solution.py:245
  46.6 1.9 %collective-permute-start.5 = (bf16[16,3584]{1,0:T(8,128)(2,1)S(1)}, bf16[16,3584]{1,0:T(8,128)(2,1)S(1)}, u32[]{:S(2)}, u32[]{:S(2)}) collective-permute-start(bf16[16,3584]{1,0:T(8,128)(2,1)S(1)} %slice.80), channel_id=1, source_target_pairs={{0,2},{1,3},{2,0},{3,1},{4,6},{5,7},{6,4},{7,5},{8,10},{9,11},{10,... | collective-permute-start | bytes 344072 | tf_op jit(solution)/shard_map/ppermute | solution.py:245
  49.0 2.5 %collective-permute-done.5 = bf16[16,3584]{1,0:T(8,128)(2,1)S(1)} collective-permute-done((bf16[16,3584]{1,0:T(8,128)(2,1)S(1)}, bf16[16,3584]{1,0:T(8,128)(2,1)S(1)}, u32[]{:S(2)}, u32[]{:S(2)}) %collective-permute-start.5) | collective-permute-done | bytes 114720 | tf_op jit(solution)/shard_map/ppermute | solution.py:245
  51.5 1.9 %collective-permute-start.2 = (bf16[16,3584]{1,0:T(8,128)(2,1)S(1)}, bf16[16,3584]{1,0:T(8,128)(2,1)S(1)}, u32[]{:S(2)}, u32[]{:S(2)}) collective-permute-start(bf16[16,3584]{1,0:T(8,128)(2,1)S(1)} %add_convert_fusion.6), channel_id=1, source_target_pairs={{0,4},{4,8},{8,12},{12,0},{1,5},{5,9},{9,13},{13,1},{2,6},{6,10},{... | collective-permute-start | bytes 344072 | tf_op jit(solution)/shard_map/ppermute | solution.py:277
  53.4 2.6 %collective-permute-start.4 = (bf16[16,3584]{1,0:T(8,128)(2,1)S(1)}, bf16[16,3584]{1,0:T(8,128)(2,1)S(1)}, u32[]{:S(2)}, u32[]{:S(2)}) collective-permute-start(bf16[16,3584]{1,0:T(8,128)(2,1)S(1)} %add_convert_fusion.5), channel_id=1, source_target_pairs={{0,8},{4,12},{8,0},{12,4},{1,9},{5,13},{9,1},{13,5},{2,10},{6,14},... | collective-permute-start | bytes 344072 | tf_op jit(solution)/shard_map/ppermute | solution.py:277
  56.1 2.3 %collective-permute-done.2.refs_0_ = bf16[16,3584]{1,0:T(8,128)(2,1)S(1)} collective-permute-done((bf16[16,3584]{1,0:T(8,128)(2,1)S(1)}, bf16[16,3584]{1,0:T(8,128)(2,1)S(1)}, u32[]{:S(2)}, u32[]{:S(2)}) %collective-permute-start.2) | collective-permute-done | bytes 114720 | tf_op jit(solution)/shard_map/ppermute | solution.py:277
  58.3 2.0 %collective-permute-start.6 = (bf16[16,3584]{1,0:T(8,128)(2,1)S(1)}, bf16[16,3584]{1,0:T(8,128)(2,1)S(1)}, u32[]{:S(2)}, u32[]{:S(2)}) collective-permute-start(bf16[16,3584]{1,0:T(8,128)(2,1)S(1)} %add_convert_fusion.4), channel_id=1, source_target_pairs={{0,12},{4,0},{8,4},{12,8},{1,13},{5,1},{9,5},{13,9},{2,14},{6,2},{... | collective-permute-start | bytes 344072 | tf_op jit(solution)/shard_map/ppermute | solution.py:277
  60.3 1.7 %collective-permute-done.4.refs_1_ = bf16[16,3584]{1,0:T(8,128)(2,1)S(1)} collective-permute-done((bf16[16,3584]{1,0:T(8,128)(2,1)S(1)}, bf16[16,3584]{1,0:T(8,128)(2,1)S(1)}, u32[]{:S(2)}, u32[]{:S(2)}) %collective-permute-start.4) | collective-permute-done | bytes 114720 | tf_op jit(solution)/shard_map/ppermute | solution.py:277
  62.0 1.5 %collective-permute-start.13 = (bf16[256,512]{1,0:T(8,128)(2,1)S(1)}, bf16[256,512]{1,0:T(8,128)(2,1)S(1)}, u32[]{:S(2)}, u32[]{:S(2)}) collective-permute-start(bf16[256,512]{1,0:T(8,128)(2,1)S(1)} %copy-done.5), channel_id=1, source_target_pairs={{0,16},{16,0},{1,17},{17,1},{2,18},{18,2},{3,19},{19,3},{4,20},{20... | collective-permute-start | bytes 786440 | tf_op jit(solution)/shard_map/ppermute | solution.py:248
  64.2 2.2 %collect.1 = bf16[16,4,3584]{2,1,0:T(4,128)(2,1)} custom-call(bf16[16,3584]{1,0:T(8,128)(2,1)} %copy-done.8, bf16[16,3584]{1,0:T(8,128)(2,1)} %copy-done.9, bf16[16,3584]{1,0:T(8,128)(2,1)} %copy-done.10, bf16[16,3584]{1,0:T(8,128)(2,1)} %get-tuple-element.21.refs_3_, bf16[16,3584]{1,0:T(8,128)(2,1)} %copy-done.7), custom_call_target="tpu_custom_call" | custom-call | tf_op jit(solution)/shard_map/collect/pallas_call | solution.py:281
  66.4 0.7 copy-done.14
  67.5 7.2 %weight_grads.2 = (bf16[1792,512]{1,0:T(8,128)(2,1)}, bf16[1792,512]{1,0:T(8,128)(2,1)}) custom-call(s32[1]{0:T(128)} %bitcast.7.replica_ref, bf16[64,4,3584]{2,1,0:T(4,128)(2,1)} %bitcast.25, f32[256,1]{1,0:T(8,128)} %broadcast_select_fusion.factor_ref.refs_1_, bf16[2,16,4,1792]{3,2,1,0:T(4,128)(2,1)} %copy-done.1, bf16[2,16,4,1792]{3,2,1,0:T(4,128)(2,1)} %copy-done.2, ...), custom_call_target="tpu_custom_call" | custom-call | flops 1879048192 | bytes 4000000 | tf_op jit(solution)/shard_map/weight_grads/pallas_call | solution.py:192
  74.7 0.7 copy-done.6
  75.4 6.8 %weight_grads.3 = bf16[1792,512]{1,0:T(8,128)(2,1)} custom-call(s32[1]{0:T(128)} %bitcast.7.replica_ref, bf16[64,4,3584]{2,1,0:T(4,128)(2,1)} %bitcast.21, f32[256,1]{1,0:T(8,128)} %broadcast_select_fusion.factor_ref.refs_1_, bf16[2,16,4,1792]{3,2,1,0:T(4,128)(2,1)} %copy-done.1, bf16[2,16,4,1792]{3,2,1,0:T(4,128)(2,1)} %copy-done.2, ...), custom_call_target="tpu_custom_call" | custom-call | flops 939524096 | bytes 4000000 | tf_op jit(solution)/shard_map/weight_grads/pallas_call | solution.py:192
  (58 shorter events, 4.1 us)
Async XLA Ops:
  3.1 11.1 %copy-start.11 = (f32[1,1,64,4]{2,3,1,0:T(4,128)S(1)}, f32[1,1,64,4]{2,3,1,0:T(4,128)}, u32[]{:S(2)}) copy-start(f32[1,1,64,4]{2,3,1,0:T(4,128)} %param.9) | copy-start | bytes 3076
  3.1 11.1 %copy-start.12 = (s32[1,1,4]{2,1,0:T(1,128)S(1)}, s32[1,1,4]{2,1,0:T(1,128)}, u32[]{:S(2)}) copy-start(s32[1,1,4]{2,1,0:T(1,128)} %param.10) | copy-start | bytes 52
  13.7 5.9 %copy-start.13 = (bf16[2,256,512]{2,1,0:T(8,128)(2,1)S(1)}, bf16[2,256,512]{2,1,0:T(8,128)(2,1)}, u32[]{:S(2)}) copy-start(bf16[2,256,512]{2,1,0:T(8,128)(2,1)} %get-tuple-element.12.refs_6_.refs_7_) | copy-start | bytes 1572868
  13.7 19.2 %copy-start = (bf16[128,3584]{1,0:T(8,128)(2,1)S(1)}, bf16[128,3584]{1,0:T(8,128)(2,1)}, u32[]{:S(2)}) copy-start(bf16[128,3584]{1,0:T(8,128)(2,1)} %get-tuple-element.10) | copy-start | bytes 2752516
  13.7 19.2 %collective-permute-start = (bf16[128,3584]{1,0:T(8,128)(2,1)}, bf16[128,3584]{1,0:T(8,128)(2,1)S(1)}, u32[]{:S(2)}, u32[]{:S(2)}) collective-permute-start(bf16[128,3584]{1,0:T(8,128)(2,1)} %get-tuple-element.11), channel_id=1, source_target_pairs={{0,1},{1,0},{2,3},{3,2},{4,5},{5,4},{6,7},{7,6},{8,9},{9,8},{10,11... | collective-permute-start | bytes 2752520 | tf_op jit(solution)/shard_map/ppermute | solution.py:245
  16.9 14.0 %collective-permute-start.8 = (bf16[2,16,4,1792]{3,2,1,0:T(4,128)(2,1)S(1)}, bf16[2,16,4,1792]{3,2,1,0:T(4,128)(2,1)S(1)}, u32[]{:S(2)}, u32[]{:S(2)}) collective-permute-start(bf16[2,16,4,1792]{3,2,1,0:T(4,128)(2,1)S(1)} %pad_maximum_fusion), channel_id=1, source_target_pairs={{0,16},{16,0},{1,17},{17,1},{2,18},{18,2},{3,19},{19,3},{4,20},{20... | collective-permute-start | bytes 1376264 | tf_op jit(solution)/shard_map/ppermute | solution.py:248
  19.6 46.8 %collective-permute-start.12 = (bf16[2,256,512]{2,1,0:T(8,128)(2,1)S(1)}, bf16[2,256,512]{2,1,0:T(8,128)(2,1)S(1)}, u32[]{:S(2)}, u32[]{:S(2)}) collective-permute-start(bf16[2,256,512]{2,1,0:T(8,128)(2,1)S(1)} %copy-done.13), channel_id=1, source_target_pairs={{0,16},{16,0},{1,17},{17,1},{2,18},{18,2},{3,19},{19,3},{4,20},{20... | collective-permute-start | bytes 1572872 | tf_op jit(solution)/shard_map/ppermute | solution.py:248
  30.9 5.1 %copy-start.1 = (bf16[2,16,4,1792]{3,2,1,0:T(4,128)(2,1)}, bf16[2,16,4,1792]{3,2,1,0:T(4,128)(2,1)S(1)}, u32[]{:S(2)}) copy-start(bf16[2,16,4,1792]{3,2,1,0:T(4,128)(2,1)S(1)} %collective-permute-done.8.refs_2_) | copy-start | bytes 1376260
  30.9 17.6 %collective-permute-start.9 = (bf16[2,16,4,1792]{3,2,1,0:T(4,128)(2,1)S(1)}, bf16[2,16,4,1792]{3,2,1,0:T(4,128)(2,1)S(1)}, u32[]{:S(2)}, u32[]{:S(2)}) collective-permute-start(bf16[2,16,4,1792]{3,2,1,0:T(4,128)(2,1)S(1)} %collective-permute-done.8.refs_2_), channel_id=1, source_target_pairs={{0,2},{1,3},{2,0},{3,1},{4,6},{5,7},{6,4},{7,5},{8,10},{9,11},{10,... | collective-permute-start | bytes 1376264 | tf_op jit(solution)/shard_map/ppermute | solution.py:245
  32.9 33.5 %collective-permute-start.10 = (bf16[2,16,4,1792]{3,2,1,0:T(4,128)(2,1)S(1)}, bf16[2,16,4,1792]{3,2,1,0:T(4,128)(2,1)S(1)}, u32[]{:S(2)}, u32[]{:S(2)}) collective-permute-start(bf16[2,16,4,1792]{3,2,1,0:T(4,128)(2,1)S(1)} %collective-permute-done.8.refs_2_), channel_id=1, source_target_pairs={{0,1},{1,0},{2,3},{3,2},{4,5},{5,4},{6,7},{7,6},{8,9},{9,8},{10,11... | collective-permute-start | bytes 1376264 | tf_op jit(solution)/shard_map/ppermute | solution.py:245
  32.9 29.1 %copy-start.5 = (bf16[256,512]{1,0:T(8,128)(2,1)S(1)}, bf16[256,512]{1,0:T(8,128)(2,1)}, u32[]{:S(2)}) copy-start(bf16[256,512]{1,0:T(8,128)(2,1)} %get-tuple-element.15.refs_6_) | copy-start | bytes 786436
  33.2 13.4 %collective-permute-start.1 = (bf16[16,3584]{1,0:T(8,128)(2,1)S(1)}, bf16[16,3584]{1,0:T(8,128)(2,1)S(1)}, u32[]{:S(2)}, u32[]{:S(2)}) collective-permute-start(bf16[16,3584]{1,0:T(8,128)(2,1)S(1)} %slice.74), channel_id=1, source_target_pairs={{0,2},{1,3},{2,0},{3,1},{4,6},{5,7},{6,4},{7,5},{8,10},{9,11},{10,... | collective-permute-start | bytes 344072 | tf_op jit(solution)/shard_map/ppermute | solution.py:245
  33.3 15.7 %collective-permute-start.3 = (bf16[16,3584]{1,0:T(8,128)(2,1)S(1)}, bf16[16,3584]{1,0:T(8,128)(2,1)S(1)}, u32[]{:S(2)}, u32[]{:S(2)}) collective-permute-start(bf16[16,3584]{1,0:T(8,128)(2,1)S(1)} %slice.77), channel_id=1, source_target_pairs={{0,2},{1,3},{2,0},{3,1},{4,6},{5,7},{6,4},{7,5},{8,10},{9,11},{10,... | collective-permute-start | bytes 344072 | tf_op jit(solution)/shard_map/ppermute | solution.py:245
  46.6 4.9 %collective-permute-start.5 = (bf16[16,3584]{1,0:T(8,128)(2,1)S(1)}, bf16[16,3584]{1,0:T(8,128)(2,1)S(1)}, u32[]{:S(2)}, u32[]{:S(2)}) collective-permute-start(bf16[16,3584]{1,0:T(8,128)(2,1)S(1)} %slice.80), channel_id=1, source_target_pairs={{0,2},{1,3},{2,0},{3,1},{4,6},{5,7},{6,4},{7,5},{8,10},{9,11},{10,... | collective-permute-start | bytes 344072 | tf_op jit(solution)/shard_map/ppermute | solution.py:245
  48.6 17.9 %copy-start.2 = (bf16[2,16,4,1792]{3,2,1,0:T(4,128)(2,1)}, bf16[2,16,4,1792]{3,2,1,0:T(4,128)(2,1)S(1)}, u32[]{:S(2)}) copy-start(bf16[2,16,4,1792]{3,2,1,0:T(4,128)(2,1)S(1)} %collective-permute-done.9.refs_3_) | copy-start | bytes 1376260
  48.6 4.9 %collective-permute-start.7 = (bf16[16,3584]{1,0:T(8,128)(2,1)S(1)}, bf16[16,3584]{1,0:T(8,128)(2,1)S(1)}, u32[]{:S(2)}, u32[]{:S(2)}) collective-permute-start(bf16[16,3584]{1,0:T(8,128)(2,1)S(1)} %get-tuple-element.20), channel_id=1, source_target_pairs={{0,2},{1,3},{2,0},{3,1},{4,6},{5,7},{6,4},{7,5},{8,10},{9,11},{10,... | collective-permute-start | bytes 344072 | tf_op jit(solution)/shard_map/ppermute | solution.py:245
  49.0 17.4 %collective-permute-start.11 = (bf16[2,16,4,1792]{3,2,1,0:T(4,128)(2,1)S(1)}, bf16[2,16,4,1792]{3,2,1,0:T(4,128)(2,1)S(1)}, u32[]{:S(2)}, u32[]{:S(2)}) collective-permute-start(bf16[2,16,4,1792]{3,2,1,0:T(4,128)(2,1)S(1)} %collective-permute-done.9.refs_3_), channel_id=1, source_target_pairs={{0,1},{1,0},{2,3},{3,2},{4,5},{5,4},{6,7},{7,6},{8,9},{9,8},{10,11... | collective-permute-start | bytes 1376264 | tf_op jit(solution)/shard_map/ppermute | solution.py:245
  51.5 6.8 %collective-permute-start.2 = (bf16[16,3584]{1,0:T(8,128)(2,1)S(1)}, bf16[16,3584]{1,0:T(8,128)(2,1)S(1)}, u32[]{:S(2)}, u32[]{:S(2)}) collective-permute-start(bf16[16,3584]{1,0:T(8,128)(2,1)S(1)} %add_convert_fusion.6), channel_id=1, source_target_pairs={{0,4},{4,8},{8,12},{12,0},{1,5},{5,9},{9,13},{13,1},{2,6},{6,10},{... | collective-permute-start | bytes 344072 | tf_op jit(solution)/shard_map/ppermute | solution.py:277
  53.4 10.1 %copy-start.7 = (bf16[16,3584]{1,0:T(8,128)(2,1)}, bf16[16,3584]{1,0:T(8,128)(2,1)S(1)}, u32[]{:S(2)}) copy-start(bf16[16,3584]{1,0:T(8,128)(2,1)S(1)} %collective-permute-done.7.refs_4_) | copy-start | bytes 344068
  53.4 8.6 %collective-permute-start.4 = (bf16[16,3584]{1,0:T(8,128)(2,1)S(1)}, bf16[16,3584]{1,0:T(8,128)(2,1)S(1)}, u32[]{:S(2)}, u32[]{:S(2)}) collective-permute-start(bf16[16,3584]{1,0:T(8,128)(2,1)S(1)} %add_convert_fusion.5), channel_id=1, source_target_pairs={{0,8},{4,12},{8,0},{12,4},{1,9},{5,13},{9,1},{13,5},{2,10},{6,14},... | collective-permute-start | bytes 344072 | tf_op jit(solution)/shard_map/ppermute | solution.py:277
  58.3 5.2 %copy-start.8 = (bf16[16,3584]{1,0:T(8,128)(2,1)}, bf16[16,3584]{1,0:T(8,128)(2,1)S(1)}, u32[]{:S(2)}) copy-start(bf16[16,3584]{1,0:T(8,128)(2,1)S(1)} %collective-permute-done.2.refs_0_) | copy-start | bytes 344068
  58.3 5.2 %collective-permute-start.6 = (bf16[16,3584]{1,0:T(8,128)(2,1)S(1)}, bf16[16,3584]{1,0:T(8,128)(2,1)S(1)}, u32[]{:S(2)}, u32[]{:S(2)}) collective-permute-start(bf16[16,3584]{1,0:T(8,128)(2,1)S(1)} %add_convert_fusion.4), channel_id=1, source_target_pairs={{0,12},{4,0},{8,4},{12,8},{1,13},{5,1},{9,5},{13,9},{2,14},{6,2},{... | collective-permute-start | bytes 344072 | tf_op jit(solution)/shard_map/ppermute | solution.py:277
  62.0 1.6 %copy-start.9 = (bf16[16,3584]{1,0:T(8,128)(2,1)}, bf16[16,3584]{1,0:T(8,128)(2,1)S(1)}, u32[]{:S(2)}) copy-start(bf16[16,3584]{1,0:T(8,128)(2,1)S(1)} %collective-permute-done.4.refs_1_) | copy-start | bytes 344068
  62.0 12.7 %collective-permute-start.13 = (bf16[256,512]{1,0:T(8,128)(2,1)S(1)}, bf16[256,512]{1,0:T(8,128)(2,1)S(1)}, u32[]{:S(2)}, u32[]{:S(2)}) collective-permute-start(bf16[256,512]{1,0:T(8,128)(2,1)S(1)} %copy-done.5), channel_id=1, source_target_pairs={{0,16},{16,0},{1,17},{17,1},{2,18},{18,2},{3,19},{19,3},{4,20},{20... | collective-permute-start | bytes 786440 | tf_op jit(solution)/shard_map/ppermute | solution.py:248
  (5 other events, 4.2 us)

commit v3 on v2

v3 whole, which is shorter than its diff:
```python
import functools

import jax
import jax.numpy as jnp
from jax import lax
from jax.experimental import pallas as pl
from jax.experimental.pallas import tpu as pltpu
from jax.sharding import PartitionSpec as P

F32, BF16 = jnp.float32, jnp.bfloat16
VMEM_LIMIT = 24 * 1024 * 1024


def dot(a, b, contract_a, contract_b):
    return lax.dot_general(a, b, (((contract_a,), (contract_b,)), ((), ())), preferred_element_type=F32)


def flat_rows(block):
    return block.reshape(block.shape[0] * block.shape[1], block.shape[2])


def log2(n):
    assert n & (n - 1) == 0
    return n.bit_length() - 1


def halving_order(size):
    order = [0]
    for i in reversed(range(log2(size))):
        order = order + [d ^ (1 << i) for d in order]
    return order


def bit_reverse(value, bits):
    out = jnp.zeros_like(value)
    for i in range(bits):
        out = out | (((value >> i) & 1) << (bits - 1 - i))
    return out


def shift_order(nodes):
    return sorted(range(1, nodes), key=lambda k: (-min(k, nodes - k), k)) + [0]


def column(weights, counts, first, out_rows):
    slots, nodes = weights.shape
    slot = first + lax.broadcasted_iota(jnp.int32, (slots, nodes), 0)
    factor = weights * jnp.where(slot < counts, 1.0, 0.0)
    spread = jnp.broadcast_to(factor[:, None, :], (slots, nodes, nodes)).reshape(out_rows, nodes)
    row = lax.broadcasted_iota(jnp.int32, (out_rows, nodes), 0)
    lane = lax.broadcasted_iota(jnp.int32, (out_rows, nodes), 1)
    return jnp.sum(jnp.where((row & (nodes - 1)) == lane, spread, 0.0), axis=1, keepdims=True)


def share_kernel(locals_, tok_hbm, grad_hbm, weights_ref, counts_ref, out, tok, grad, sem):
    keep, nodes, part = tok.shape
    me, other = lax.axis_index("local"), 1 - lax.axis_index("dp")
    slots = pl.ds(me * keep, keep)
    cols = pl.ds(pl.multiple_of(other * part, 128), part)
    copies = [pltpu.make_async_copy(tok_hbm.at[slots, :, cols], tok, sem.at[0]),
              pltpu.make_async_copy(grad_hbm.at[slots, :, cols], grad, sem.at[1])]
    for copy in copies:
        copy.start()
    factor = column(weights_ref[slots], counts_ref[...], me * keep, keep * nodes)
    copies[0].wait()
    out[0] = flat_rows(tok[...])
    copies[1].wait()
    out[1] = (flat_rows(grad[...].astype(F32)) * factor).astype(BF16)


def share(locals_, tokens, grads, weights, counts):
    slots, nodes, width = tokens.shape
    keep, part = slots // locals_, width // 2
    vmem, hbm = pl.BlockSpec(memory_space=pltpu.VMEM), pl.BlockSpec(memory_space=pltpu.HBM)
    return pl.pallas_call(
        functools.partial(share_kernel, locals_),
        out_shape=jax.ShapeDtypeStruct((2, keep * nodes, part), BF16),
        in_specs=[hbm, hbm, vmem, vmem],
        out_specs=vmem,
        scratch_shapes=[pltpu.VMEM((keep, nodes, part), BF16)] * 2 + [pltpu.SemaphoreType.DMA((2,))],
        compiler_params=pltpu.CompilerParams(vmem_limit_bytes=VMEM_LIMIT),
        name="share",
    )(tokens, grads, weights, counts)


def forward_kernel(locals_, tok, grad, weights_ref, counts_ref, wg, wu, wd, pair, hid, own_a, own_b, send_a, send_b,
                   acc_g, acc_u, acc_h, moved):
    slots, nodes, width = tok.shape
    rows = slots * nodes
    keep = slots // locals_
    chunk = 512
    steps = width // chunk
    me, node = lax.axis_index("local"), lax.axis_index("node")
    factor = column(weights_ref[...], counts_ref[...], 0, rows)

    for i in range(steps):
        cols = pl.ds(i * chunk, chunk)
        t = flat_rows(tok[:, :, cols])
        gate = dot(t, wg[cols], 1, 0)
        up = dot(t, wu[cols], 1, 0)
        scaled = (flat_rows(grad[:, :, cols].astype(F32)) * factor).astype(BF16)
        back = dot(scaled, wd[cols], 1, 0)
        if i:
            acc_g[...] += gate
            acc_u[...] += up
            acc_h[...] += back
        else:
            acc_g[...] = gate
            acc_u[...] = up
            acc_h[...] = back

    band = 64

    def activate(i, carry):
        at = pl.ds(pl.multiple_of(i * band, band), band)
        gate, up, back = acc_g[at], acc_u[at], acc_h[at]
        sig = jax.nn.sigmoid(gate)
        act = gate * sig
        hid[at] = (act * up).astype(BF16)
        pair[0, at] = (back * up * sig * (1.0 + gate * (1.0 - sig))).astype(BF16)
        pair[1, at] = (back * act).astype(BF16)
        return carry

    lax.fori_loop(0, rows // band, activate, 0)

    per = nodes // 2
    p = lax.broadcasted_iota(jnp.int32, (rows, 1), 0)
    j = p & (keep - 1)
    at = log2(keep)
    quick = (p >> at) & (per - 1)
    at += log2(per)
    low = (p >> at) & (locals_ // 2 - 1)
    at += log2(locals_ // 2)
    group = (p >> at) & 1
    high = p >> (at + 1)
    place = bit_reverse(high * (locals_ // 2) + low, log2(locals_)) ^ me
    hop = jnp.zeros_like(p)
    for n, k in enumerate(shift_order(nodes)):
        hop = jnp.where(group * per + quick == n, k, hop)
    index = (place * keep + j) * nodes + ((node + hop) & (nodes - 1))
    one_hot = jnp.where(index == lax.broadcasted_iota(jnp.int32, (rows, rows), 1), 1.0, 0.0).astype(BF16)
    moved[0] = dot(one_hot, pair[0], 1, 0).astype(BF16)
    moved[1] = dot(one_hot, pair[1], 1, 0).astype(BF16)
    quarter = rows // 4
    for i in range(steps):
        cols = pl.ds(i * chunk, chunk)
        total = (dot(moved[0], wg[cols], 1, 1) + dot(moved[1], wu[cols], 1, 1)).astype(BF16)
        for n, out in enumerate((own_a, own_b, send_a, send_b)):
            out[:, cols] = total[n * quarter:(n + 1) * quarter]


def forward(locals_, tokens, grads, weights, counts, gate_weight, up_weight, down_weight):
    slots, nodes, width = tokens.shape
    rows = slots * nodes
    hid_local = gate_weight.shape[1]
    vmem = pl.BlockSpec(memory_space=pltpu.VMEM)
    acc = pltpu.VMEM((rows, hid_local), F32)
    return pl.pallas_call(
        functools.partial(forward_kernel, locals_),
        out_shape=[jax.ShapeDtypeStruct((2, rows, hid_local), BF16), jax.ShapeDtypeStruct((rows, hid_local), BF16)]
        + [jax.ShapeDtypeStruct((rows // 4, width), BF16)] * 4,
        in_specs=[vmem] * 7,
        out_specs=[vmem] * 6,
        scratch_shapes=[acc, acc, acc, pltpu.VMEM((2, rows, hid_local), BF16)],
        compiler_params=pltpu.CompilerParams(vmem_limit_bytes=VMEM_LIMIT),
        cost_estimate=pl.CostEstimate(flops=10 * rows * width * hid_local, bytes_accessed=18_000_000, transcendentals=0),
        name="forward",
    )(tokens, grads, weights, counts, gate_weight, up_weight, down_weight)


def weight_kernel(order, count, *refs):
    rows_ref, weights_ref, counts_ref = refs[:3]
    shares = refs[3:3 + len(order)]
    own_ref, there_ref = refs[3 + len(order):5 + len(order)]
    outs = refs[5 + len(order):5 + len(order) + count]
    left, right, bufs, sem = refs[5 + len(order) + count:]
    slots, nodes, width = rows_ref.shape
    rows = slots * nodes
    part, hid_local = outs[0].shape
    me, replica = lax.axis_index("local"), lax.axis_index("dp")
    block = rows // len(order)
    which = 0 if count == 2 else 1
    factor = None if count == 2 else column(weights_ref[...], counts_ref[...], 0, rows)
    for n in range(count):
        right[n, :rows] = own_ref[n]
        for b, d in enumerate(order):
            right[n, rows + b * block:rows + (b + 1) * block] = there_ref[n, pl.ds(pl.multiple_of((me ^ d) * block, block), block)]
    chunk = 896
    copies = []
    for i in range(part // chunk):
        cols = pl.ds(i * chunk, chunk)
        own = rows_ref[:, :, pl.ds(pl.multiple_of(replica * part + i * chunk, 128), chunk)]
        left[:rows] = flat_rows(own) if count == 2 else (flat_rows(own.astype(F32)) * factor).astype(BF16)
        for b, ref in enumerate(shares):
            left[rows + b * block:rows + (b + 1) * block] = ref[which, :, cols]
        for n, out in enumerate(outs):
            bufs[n, cols] = dot(left[...], right[n], 0, 0).astype(BF16)
            copies.append(pltpu.make_async_copy(bufs.at[n, cols], out.at[cols], sem.at[i, n]))
            copies[-1].start()
    for copy in copies:
        copy.wait()


def weight_grads(order, rows3, weights, counts, shares, own_acts, there_acts):
    slots, nodes, width = rows3.shape
    part = shares[0].shape[-1]
    count, rows, hid_local = own_acts.shape
    vmem = pl.BlockSpec(memory_space=pltpu.VMEM)
    return pl.pallas_call(
        functools.partial(weight_kernel, order, count),
        out_shape=[jax.ShapeDtypeStruct((part, hid_local), BF16)] * count,
        in_specs=[vmem] * (5 + len(shares)),
        out_specs=[pl.BlockSpec(memory_space=pltpu.HBM)] * count,
        scratch_shapes=[pltpu.VMEM((2 * rows, 896), BF16), pltpu.VMEM((count, 2 * rows, hid_local), BF16),
                        pltpu.VMEM((count, part, hid_local), BF16), pltpu.SemaphoreType.DMA((part // 896, count))],
        compiler_params=pltpu.CompilerParams(vmem_limit_bytes=VMEM_LIMIT),
        cost_estimate=pl.CostEstimate(flops=4 * rows * part * hid_local * count, bytes_accessed=4_000_000, transcendentals=0),
        name="weight_grads",
    )(rows3, weights, counts, *shares, own_acts, there_acts)


def collect_kernel(*refs):
    *arrived, kept, came, out = refs
    keep, nodes, width = out.shape
    node = lax.axis_index("node")
    last = (kept[...].astype(F32) + came[...].astype(F32)).astype(BF16)
    stacked = jnp.concatenate([last] + [a[...] for a in arrived], axis=0)
    rows = keep * nodes
    p = lax.broadcasted_iota(jnp.int32, (rows, rows), 0)
    source = ((node - (p & (nodes - 1))) & (nodes - 1)) * keep + (p >> log2(nodes))
    one_hot = jnp.where(source == lax.broadcasted_iota(jnp.int32, (rows, rows), 1), 1.0, 0.0).astype(BF16)
    out[...] = dot(one_hot, stacked, 1, 0).astype(BF16).reshape(out.shape)


def add(a, b):
    return (a.astype(F32) + b.astype(F32)).astype(BF16)


def on_device(tokens_in, grad_rows, combine_weights, live_counts, w_gate, w_up, w_down):
    slots, nodes, width = tokens_in.shape[2:]
    replicas, locals_ = lax.axis_size("dp"), lax.axis_size("local")
    assert replicas == 2
    keep = slots // locals_
    tokens, grads, weights, counts = tokens_in[0, 0], grad_rows[0, 0], combine_weights[0, 0], live_counts[0]
    order = halving_order(locals_)
    bits = [1 << i for i in range(log2(locals_))]

    def swap_local(value, bit):
        return lax.ppermute(value, "local", [(i, i ^ bit) for i in range(locals_)])

    def swap_dp(value):
        return lax.ppermute(value, "dp", [(0, 1), (1, 0)])

    def gather_shares(value):
        out = [value]
        for bit in reversed(bits):
            out = out + [swap_local(v, bit) for v in out]
        return out

    first = swap_dp(share(locals_, tokens, grads, weights, counts))
    pair, hidden, own_a, own_b, send_a, send_b = forward(locals_, tokens, grads, weights, counts, w_gate[0], w_up[0], w_down[0])
    pair_there = swap_dp(pair)
    hidden_there = swap_dp(hidden)
    send_a, send_b, first = lax.optimization_barrier((send_a, send_b, first))
    shares = gather_shares(first)

    per = nodes // 2
    hops = shift_order(nodes)
    arrived = [None] * nodes
    held = [(own_a, swap_local(send_a, bits[0])), (own_b, swap_local(send_b, bits[0]))]
    for bit in bits[1:]:
        for g, (mine, other) in enumerate(held):
            half = mine.shape[0] // 2
            held[g] = (add(mine[:half], other[:half]), swap_local(add(mine[half:], other[half:]), bit))
    for n, k in enumerate(hops):
        mine, other = (v[n % per * keep:(n % per + 1) * keep] for v in held[n // per])
        if k:
            arrived[k] = lax.ppermute(add(mine, other), "node", [(i, (i + k) % nodes) for i in range(nodes)])
        else:
            arrived[0] = (mine, other)
    d_tokens = pl.pallas_call(
        collect_kernel,
        out_shape=jax.ShapeDtypeStruct((keep, nodes, width), BF16),
        in_specs=[pl.BlockSpec(memory_space=pltpu.VMEM)] * (nodes + 1),
        out_specs=pl.BlockSpec(memory_space=pltpu.VMEM),
        compiler_params=pltpu.CompilerParams(vmem_limit_bytes=VMEM_LIMIT),
        name="collect",
    )(*arrived[1:], *arrived[0])

    grad_gate, grad_up = weight_grads(order, tokens, weights, counts, shares, pair, pair_there)
    (grad_down,) = weight_grads(order, grads, weights, counts, shares, hidden[None], hidden_there[None])
    return d_tokens[None, None], grad_gate[None], grad_up[None], grad_down[None]


def solution(mesh):
    return jax.shard_map(
        on_device,
        mesh=mesh,
        in_specs=(
            P("dp", "node", None, None, None),
            P("dp", "node", None, None, None),
            P("dp", "node", None, None),
            P("dp", "node", None),
            P("node", None, "local"),
            P("node", None, "local"),
            P("node", None, "local"),
        ),
        out_specs=(
            P("dp", "node", "local", None, None),
            P("node", "dp", "local"),
            P("node", "dp", "local"),
            P("node", "dp", "local"),
        ),
        check_vma=False,
    )
```

time: 82.7 us -> 62.6 us (0.76)
  the two profiles are of different devices: /device:TPU:0 before, /device:TPU:28 now
where the time goes in v3:
time: 62.6 us; the launch traced here: 62.3 us
  waiting for transfers between devices  31.1 us (50%)
  Pallas kernels  12.6 us (20%)
  starting transfers between devices  8.83 us (14%)
  local copies, waits for them, and re-layouts  8.76 us (14%)
  between operations  0.73 us (1%)
    ppermute x7, waiting for transfers between devices, swap_local(): return lax.ppermute(value, 'local', [(i, i ^ bit) for i in range(locals_)])  17.7 us
    ppermute x3, waiting for transfers between devices, on_device(): lax.ppermute(add(mine, other), 'node', [(i, (i + k) % nodes) for i in ran...  9.34 us
    unnamed x17, local copies, waits for them, and re-layouts  8.74 us
    pallas_call x1, Pallas kernels, forward(): pl.pallas_call(functools.partial(forward_kernel, locals_), out_shape=[jax...  5.82 us
    pallas_call x2, Pallas kernels, weight_grads(): pl.pallas_call(functools.partial(weight_kernel, order, count), out_shape=...  5.49 us
    ppermute x7, starting transfers between devices, swap_local(): return lax.ppermute(value, 'local', [(i, i ^ bit) for i in range(locals_)])  4.19 us
    ppermute x3, waiting for transfers between devices, swap_dp(): return lax.ppermute(value, 'dp', [(0, 1), (1, 0)])  4.03 us
    ppermute x3, starting transfers between devices, swap_dp(): return lax.ppermute(value, 'dp', [(0, 1), (1, 0)])  3.58 us
  transfers between devices with their start and end apart: 13, of which 8 were waited for; matrix products, arithmetic and copies ran while one was open for 1% of the time, Pallas kernels for 16%

profile of v3, /device:TPU:28, one launch (start us, length us, event | category | flops | bytes accessed | tf_op | source)
XLA Modules:
  0.0 62.3 jit_solution(15850935356944783513)
XLA Ops:
  0.6 0.8 %copy.11 = f32[1,1,64,4]{3,2,1,0:T(8,128)S(1)} copy(f32[1,1,64,4]{2,3,1,0:T(4,128)} %param.9) | data formatting | bytes 2048 | tf_op args[2]
  1.4 1.5 %copy-done = bf16[1,1,64,4,3584]{4,3,2,1,0:T(4,128)(2,1)S(1)} copy-done((bf16[1,1,64,4,3584]{4,3,2,1,0:T(4,128)(2,1)S(1)}, bf16[1,1,64,4,3584]{4,3,2,1,0:T(4,128)(2,1)}, u32[]{:S(2)}) %copy-start) | copy-done | bytes 1835032
  2.9 1.5 %copy-done.2 = bf16[1,1,64,4,3584]{4,3,2,1,0:T(4,128)(2,1)S(1)} copy-done((bf16[1,1,64,4,3584]{4,3,2,1,0:T(4,128)(2,1)S(1)}, bf16[1,1,64,4,3584]{4,3,2,1,0:T(4,128)(2,1)}, u32[]{:S(2)}) %copy-start.2) | copy-done | bytes 1835032
  4.4 0.7 %copy-done.4 = s32[1,1,4]{2,1,0:T(1,128)S(1)} copy-done((s32[1,1,4]{2,1,0:T(1,128)S(1)}, s32[1,1,4]{2,1,0:T(1,128)}, u32[]{:S(2)}) %copy-start.4) | copy-done | bytes 40
  5.3 1.6 %collective-permute-start = (bf16[2,64,1792]{2,1,0:T(8,128)(2,1)S(1)}, bf16[2,64,1792]{2,1,0:T(8,128)(2,1)S(1)}, u32[]{:S(2)}, u32[]{:S(2)}) collective-permute-start(bf16[2,64,1792]{2,1,0:T(8,128)(2,1)S(1)} %share.1), channel_id=1, source_target_pairs={{0,16},{16,0},{1,17},{17,1},{2,18},{18,2},{3,19},{19,3},{4,20},{20... | collective-permute-start | bytes 1376264 | tf_op jit(solution)/shard_map/ppermute | solution.py:252
  7.1 2.0 %copy-done.6 = bf16[1,3584,512]{2,1,0:T(8,128)(2,1)S(1)} copy-done((bf16[1,3584,512]{2,1,0:T(8,128)(2,1)S(1)}, bf16[1,3584,512]{2,1,0:T(8,128)(2,1)}, u32[]{:S(2)}) %copy-start.6) | copy-done | bytes 3670040
  9.1 2.0 %copy-done.7 = bf16[1,3584,512]{2,1,0:T(8,128)(2,1)S(1)} copy-done((bf16[1,3584,512]{2,1,0:T(8,128)(2,1)S(1)}, bf16[1,3584,512]{2,1,0:T(8,128)(2,1)}, u32[]{:S(2)}) %copy-start.7) | copy-done | bytes 3670040
  11.2 5.8 %forward.1 = (bf16[2,256,512]{2,1,0:T(8,128)(2,1)S(1)}, bf16[256,512]{1,0:T(8,128)(2,1)S(1)}, bf16[64,3584]{1,0:T(8,128)(2,1)S(1)}, bf16[64,3584]{1,0:T(8,128)(2...) custom-call(bf16[64,4,3584]{2,1,0:T(4,128)(2,1)S(1)} %bitcast.17, bf16[64,4,3584]{2,1,0:T(4,128)(2,1)S(1)} %bitcast.14, ...), custom_call_target="tpu_custom_call" | custom-call | flops 4697620480 | bytes 18000000 | tf_op jit(solution)/shard_map/forward/pallas_call | solution.py:158
  17.0 0.6 %collective-permute-done.refs_3_ = bf16[2,64,1792]{2,1,0:T(8,128)(2,1)S(1)} collective-permute-done((bf16[2,64,1792]{2,1,0:T(8,128)(2,1)S(1)}, bf16[2,64,1792]{2,1,0:T(8,128)(2,1)S(1)}, u32[]{:S(2)}, u32[]{:S(2)}) %collective-permute-start) | collective-permute-done | bytes 458784 | tf_op jit(solution)/shard_map/ppermute | solution.py:252
  17.6 1.5 %collective-permute-start.11 = (bf16[2,256,512]{2,1,0:T(8,128)(2,1)S(1)}, bf16[2,256,512]{2,1,0:T(8,128)(2,1)S(1)}, u32[]{:S(2)}, u32[]{:S(2)}) collective-permute-start(bf16[2,256,512]{2,1,0:T(8,128)(2,1)S(1)} %get-tuple-element.22.refs_7_), channel_id=1, source_target_pairs={{0,16},{16,0},{1,17},{17,1},{2,18},{18,2},{3,19},{19,3},{4,20},{20... | collective-permute-start | bytes 1572872 | tf_op jit(solution)/shard_map/ppermute | solution.py:252
  19.1 0.5 collective-permute-start.8
  19.6 0.5 collective-permute-start.5
  20.3 1.6 %collective-permute-start.2 = (bf16[32,3584]{1,0:T(8,128)(2,1)S(1)}, bf16[32,3584]{1,0:T(8,128)(2,1)S(1)}, u32[]{:S(2)}, u32[]{:S(2)}) collective-permute-start(bf16[32,3584]{1,0:T(8,128)(2,1)S(1)} %get-tuple-element.29), channel_id=1, source_target_pairs={{0,2},{1,3},{2,0},{3,1},{4,6},{5,7},{6,4},{7,5},{8,10},{9,11},{10,... | collective-permute-start | bytes 688136 | tf_op jit(solution)/shard_map/ppermute | solution.py:249
  22.2 1.6 %collective-permute-start.6 = (bf16[32,3584]{1,0:T(8,128)(2,1)S(1)}, bf16[32,3584]{1,0:T(8,128)(2,1)S(1)}, u32[]{:S(2)}, u32[]{:S(2)}) collective-permute-start(bf16[32,3584]{1,0:T(8,128)(2,1)S(1)} %get-tuple-element.27), channel_id=1, source_target_pairs={{0,2},{1,3},{2,0},{3,1},{4,6},{5,7},{6,4},{7,5},{8,10},{9,11},{10,... | collective-permute-start | bytes 688136 | tf_op jit(solution)/shard_map/ppermute | solution.py:249
  23.8 8.7 %collective-permute-done.8.refs_4_ = bf16[2,64,1792]{2,1,0:T(8,128)(2,1)S(1)} collective-permute-done((bf16[2,64,1792]{2,1,0:T(8,128)(2,1)S(1)}, bf16[2,64,1792]{2,1,0:T(8,128)(2,1)S(1)}, u32[]{:S(2)}, u32[]{:S(2)}) %collective-permute-start.8) | collective-permute-done | bytes 458784 | tf_op jit(solution)/shard_map/ppermute | solution.py:249
  32.5 4.9 %collective-permute-done.2 = bf16[32,3584]{1,0:T(8,128)(2,1)S(1)} collective-permute-done((bf16[32,3584]{1,0:T(8,128)(2,1)S(1)}, bf16[32,3584]{1,0:T(8,128)(2,1)S(1)}, u32[]{:S(2)}, u32[]{:S(2)}) %collective-permute-start.2) | collective-permute-done | bytes 229408 | tf_op jit(solution)/shard_map/ppermute | solution.py:249
  37.7 3.9 %collective-permute-done.6 = bf16[32,3584]{1,0:T(8,128)(2,1)S(1)} collective-permute-done((bf16[32,3584]{1,0:T(8,128)(2,1)S(1)}, bf16[32,3584]{1,0:T(8,128)(2,1)S(1)}, u32[]{:S(2)}, u32[]{:S(2)}) %collective-permute-start.6) | collective-permute-done | bytes 229408 | tf_op jit(solution)/shard_map/ppermute | solution.py:249
  42.3 0.4 collective-permute-start.7
  42.8 9.0 %collective-permute-done.4.refs_1_ = bf16[16,3584]{1,0:T(8,128)(2,1)S(1)} collective-permute-done((bf16[16,3584]{1,0:T(8,128)(2,1)S(1)}, bf16[16,3584]{1,0:T(8,128)(2,1)S(1)}, u32[]{:S(2)}, u32[]{:S(2)}) %collective-permute-start.4) | collective-permute-done | bytes 114720 | tf_op jit(solution)/shard_map/ppermute | solution.py:278
  51.8 0.5 collective-permute-start.12
  52.3 1.0 %collect.1 = bf16[16,4,3584]{2,1,0:T(4,128)(2,1)} custom-call(bf16[16,3584]{1,0:T(8,128)(2,1)S(1)} %collective-permute-done.3.refs_0_, bf16[16,3584]{1,0:T(8,128)(2,1)S(1)} %collective-permute-done.4.refs_1_, bf16[16,3584]{1,0:T(8,128)(2,1)S(1)} %collective-permute-done.7.refs_2_, bf16[16,3584]{1,0:T(8,128)(2,1)S(1)} %slice.74.refs_3_, ...), custom_call_target="tpu_custom_call" | custom-call | tf_op jit(solution)/shard_map/collect/pallas_call | solution.py:281
  53.4 3.2 %weight_grads.2 = (bf16[1792,512]{1,0:T(8,128)(2,1)}, bf16[1792,512]{1,0:T(8,128)(2,1)}) custom-call(bf16[64,4,3584]{2,1,0:T(4,128)(2,1)S(1)} %bitcast.18, f32[64,4]{1,0:T(8,128)S(1)} %bitcast.21, s32[1,4]{1,0:T(1,128)S(1)} %bitcast.27, bf16[2,64,1792]{2,1,0:T(8,128)(2,1)S(1)} %collective-permute-done.refs_3_, ...), custom_call_target="tpu_custom_call" | custom-call | flops 1879048192 | bytes 4000000 | tf_op jit(solution)/shard_map/weight_grads/pallas_call | solution.py:209
  56.6 3.4 %collective-permute-done.12 = bf16[256,512]{1,0:T(8,128)(2,1)S(1)} collective-permute-done((bf16[256,512]{1,0:T(8,128)(2,1)S(1)}, bf16[256,512]{1,0:T(8,128)(2,1)S(1)}, u32[]{:S(2)}, u32[]{:S(2)}) %collective-permute-start.12) | collective-permute-done | bytes 262176 | tf_op jit(solution)/shard_map/ppermute | solution.py:252
  60.0 2.3 %weight_grads.3 = bf16[1792,512]{1,0:T(8,128)(2,1)} custom-call(bf16[64,4,3584]{2,1,0:T(4,128)(2,1)S(1)} %bitcast.15, f32[64,4]{1,0:T(8,128)S(1)} %bitcast.22, s32[1,4]{1,0:T(1,128)S(1)} %bitcast.28, bf16[2,64,1792]{2,1,0:T(8,128)(2,1)S(1)} %collective-permute-done.refs_3_, bf16[2,64,1792]{2,1,0:T(8,128)(2,1)S(1)} %collective-permute-done.8.refs_4_, ...), custom_call_target="tpu_custom_call" | custom-call | flops 939524096 | bytes 4000000 | tf_op jit(solution)/shard_map/weight_grads/pallas_call | solution.py:209
  (30 shorter events, 2.0 us)
Async XLA Ops:
  1.4 1.5 %copy-start = (bf16[1,1,64,4,3584]{4,3,2,1,0:T(4,128)(2,1)S(1)}, bf16[1,1,64,4,3584]{4,3,2,1,0:T(4,128)(2,1)}, u32[]{:S(2)}) copy-start(bf16[1,1,64,4,3584]{4,3,2,1,0:T(4,128)(2,1)} %param.8) | copy-start | bytes 5505028
  2.9 1.5 %copy-start.2 = (bf16[1,1,64,4,3584]{4,3,2,1,0:T(4,128)(2,1)S(1)}, bf16[1,1,64,4,3584]{4,3,2,1,0:T(4,128)(2,1)}, u32[]{:S(2)}) copy-start(bf16[1,1,64,4,3584]{4,3,2,1,0:T(4,128)(2,1)} %param.7) | copy-start | bytes 5505028
  4.4 0.7 %copy-start.4 = (s32[1,1,4]{2,1,0:T(1,128)S(1)}, s32[1,1,4]{2,1,0:T(1,128)}, u32[]{:S(2)}) copy-start(s32[1,1,4]{2,1,0:T(1,128)} %param.10) | copy-start | bytes 52
  5.1 2.0 %copy-start.5 = (bf16[1,3584,512]{2,1,0:T(8,128)(2,1)S(1)}, bf16[1,3584,512]{2,1,0:T(8,128)(2,1)}, u32[]{:S(2)}) copy-start(bf16[1,3584,512]{2,1,0:T(8,128)(2,1)} %param.11) | copy-start | bytes 11010052
  5.3 12.3 %collective-permute-start = (bf16[2,64,1792]{2,1,0:T(8,128)(2,1)S(1)}, bf16[2,64,1792]{2,1,0:T(8,128)(2,1)S(1)}, u32[]{:S(2)}, u32[]{:S(2)}) collective-permute-start(bf16[2,64,1792]{2,1,0:T(8,128)(2,1)S(1)} %share.1), channel_id=1, source_target_pairs={{0,16},{16,0},{1,17},{17,1},{2,18},{18,2},{3,19},{19,3},{4,20},{20... | collective-permute-start | bytes 1376264 | tf_op jit(solution)/shard_map/ppermute | solution.py:252
  7.1 2.0 %copy-start.6 = (bf16[1,3584,512]{2,1,0:T(8,128)(2,1)S(1)}, bf16[1,3584,512]{2,1,0:T(8,128)(2,1)}, u32[]{:S(2)}) copy-start(bf16[1,3584,512]{2,1,0:T(8,128)(2,1)} %param.12) | copy-start | bytes 11010052
  9.1 2.0 %copy-start.7 = (bf16[1,3584,512]{2,1,0:T(8,128)(2,1)S(1)}, bf16[1,3584,512]{2,1,0:T(8,128)(2,1)}, u32[]{:S(2)}) copy-start(bf16[1,3584,512]{2,1,0:T(8,128)(2,1)} %param.13) | copy-start | bytes 11010052
  17.6 2.5 %collective-permute-start.1 = (bf16[64,3584]{1,0:T(8,128)(2,1)S(1)}, bf16[64,3584]{1,0:T(8,128)(2,1)S(1)}, u32[]{:S(2)}, u32[]{:S(2)}) collective-permute-start(bf16[64,3584]{1,0:T(8,128)(2,1)S(1)} %get-tuple-element.18), channel_id=1, source_target_pairs={{0,1},{1,0},{2,3},{3,2},{4,5},{5,4},{6,7},{7,6},{8,9},{9,8},{10,11... | collective-permute-start | bytes 1376264 | tf_op jit(solution)/shard_map/ppermute | solution.py:249
  17.6 35.8 %collective-permute-start.11 = (bf16[2,256,512]{2,1,0:T(8,128)(2,1)S(1)}, bf16[2,256,512]{2,1,0:T(8,128)(2,1)S(1)}, u32[]{:S(2)}, u32[]{:S(2)}) collective-permute-start(bf16[2,256,512]{2,1,0:T(8,128)(2,1)S(1)} %get-tuple-element.22.refs_7_), channel_id=1, source_target_pairs={{0,16},{16,0},{1,17},{17,1},{2,18},{18,2},{3,19},{19,3},{4,20},{20... | collective-permute-start | bytes 1572872 | tf_op jit(solution)/shard_map/ppermute | solution.py:252
  19.1 13.4 %collective-permute-start.8 = (bf16[2,64,1792]{2,1,0:T(8,128)(2,1)S(1)}, bf16[2,64,1792]{2,1,0:T(8,128)(2,1)S(1)}, u32[]{:S(2)}, u32[]{:S(2)}) collective-permute-start(bf16[2,64,1792]{2,1,0:T(8,128)(2,1)S(1)} %collective-permute-done.refs_3_), channel_id=1, source_target_pairs={{0,2},{1,3},{2,0},{3,1},{4,6},{5,7},{6,4},{7,5},{8,10},{9,11},{10,... | collective-permute-start | bytes 1376264 | tf_op jit(solution)/shard_map/ppermute | solution.py:249
  19.6 33.8 %collective-permute-start.9 = (bf16[2,64,1792]{2,1,0:T(8,128)(2,1)S(1)}, bf16[2,64,1792]{2,1,0:T(8,128)(2,1)S(1)}, u32[]{:S(2)}, u32[]{:S(2)}) collective-permute-start(bf16[2,64,1792]{2,1,0:T(8,128)(2,1)S(1)} %collective-permute-done.refs_3_), channel_id=1, source_target_pairs={{0,1},{1,0},{2,3},{3,2},{4,5},{5,4},{6,7},{7,6},{8,9},{9,8},{10,11... | collective-permute-start | bytes 1376264 | tf_op jit(solution)/shard_map/ppermute | solution.py:249
  19.6 2.5 %collective-permute-start.5 = (bf16[64,3584]{1,0:T(8,128)(2,1)S(1)}, bf16[64,3584]{1,0:T(8,128)(2,1)S(1)}, u32[]{:S(2)}, u32[]{:S(2)}) collective-permute-start(bf16[64,3584]{1,0:T(8,128)(2,1)S(1)} %get-tuple-element.20), channel_id=1, source_target_pairs={{0,1},{1,0},{2,3},{3,2},{4,5},{5,4},{6,7},{7,6},{8,9},{9,8},{10,11... | collective-permute-start | bytes 1376264 | tf_op jit(solution)/shard_map/ppermute | solution.py:249
  20.3 17.1 %collective-permute-start.2 = (bf16[32,3584]{1,0:T(8,128)(2,1)S(1)}, bf16[32,3584]{1,0:T(8,128)(2,1)S(1)}, u32[]{:S(2)}, u32[]{:S(2)}) collective-permute-start(bf16[32,3584]{1,0:T(8,128)(2,1)S(1)} %get-tuple-element.29), channel_id=1, source_target_pairs={{0,2},{1,3},{2,0},{3,1},{4,6},{5,7},{6,4},{7,5},{8,10},{9,11},{10,... | collective-permute-start | bytes 688136 | tf_op jit(solution)/shard_map/ppermute | solution.py:249
  22.1 31.3 %copy-start.3 = (bf16[1,1,64,4,3584]{4,3,2,1,0:T(4,128)(2,1)S(1)}, bf16[1,1,64,4,3584]{4,3,2,1,0:T(4,128)(2,1)}, u32[]{:S(2)}) copy-start(bf16[1,1,64,4,3584]{4,3,2,1,0:T(4,128)(2,1)} %param.7) | copy-start | bytes 5505028
  22.2 19.4 %collective-permute-start.6 = (bf16[32,3584]{1,0:T(8,128)(2,1)S(1)}, bf16[32,3584]{1,0:T(8,128)(2,1)S(1)}, u32[]{:S(2)}, u32[]{:S(2)}) collective-permute-start(bf16[32,3584]{1,0:T(8,128)(2,1)S(1)} %get-tuple-element.27), channel_id=1, source_target_pairs={{0,2},{1,3},{2,0},{3,1},{4,6},{5,7},{6,4},{7,5},{8,10},{9,11},{10,... | collective-permute-start | bytes 688136 | tf_op jit(solution)/shard_map/ppermute | solution.py:249
  32.5 20.9 %collective-permute-start.10 = (bf16[2,64,1792]{2,1,0:T(8,128)(2,1)S(1)}, bf16[2,64,1792]{2,1,0:T(8,128)(2,1)S(1)}, u32[]{:S(2)}, u32[]{:S(2)}) collective-permute-start(bf16[2,64,1792]{2,1,0:T(8,128)(2,1)S(1)} %collective-permute-done.8.refs_4_), channel_id=1, source_target_pairs={{0,1},{1,0},{2,3},{3,2},{4,5},{5,4},{6,7},{7,6},{8,9},{9,8},{10,11... | collective-permute-start | bytes 1376264 | tf_op jit(solution)/shard_map/ppermute | solution.py:249
  37.5 4.8 %collective-permute-start.3 = (bf16[16,3584]{1,0:T(8,128)(2,1)S(1)}, bf16[16,3584]{1,0:T(8,128)(2,1)S(1)}, u32[]{:S(2)}, u32[]{:S(2)}) collective-permute-start(bf16[16,3584]{1,0:T(8,128)(2,1)S(1)} %get-tuple-element.31), channel_id=1, source_target_pairs={{0,4},{4,8},{8,12},{12,0},{1,5},{5,9},{9,13},{13,1},{2,6},{6,10},{... | collective-permute-start | bytes 344072 | tf_op jit(solution)/shard_map/ppermute | solution.py:278
  41.6 10.2 %collective-permute-start.4 = (bf16[16,3584]{1,0:T(8,128)(2,1)S(1)}, bf16[16,3584]{1,0:T(8,128)(2,1)S(1)}, u32[]{:S(2)}, u32[]{:S(2)}) collective-permute-start(bf16[16,3584]{1,0:T(8,128)(2,1)S(1)} %get-tuple-element.30), channel_id=1, source_target_pairs={{0,8},{4,12},{8,0},{12,4},{1,9},{5,13},{9,1},{13,5},{2,10},{6,14},... | collective-permute-start | bytes 344072 | tf_op jit(solution)/shard_map/ppermute | solution.py:278
  42.3 10.0 %collective-permute-start.7 = (bf16[16,3584]{1,0:T(8,128)(2,1)S(1)}, bf16[16,3584]{1,0:T(8,128)(2,1)S(1)}, u32[]{:S(2)}, u32[]{:S(2)}) collective-permute-start(bf16[16,3584]{1,0:T(8,128)(2,1)S(1)} %add_convert_fusion.4), channel_id=1, source_target_pairs={{0,12},{4,0},{8,4},{12,8},{1,13},{5,1},{9,5},{13,9},{2,14},{6,2},{... | collective-permute-start | bytes 344072 | tf_op jit(solution)/shard_map/ppermute | solution.py:278
  51.8 8.2 %collective-permute-start.12 = (bf16[256,512]{1,0:T(8,128)(2,1)S(1)}, bf16[256,512]{1,0:T(8,128)(2,1)S(1)}, u32[]{:S(2)}, u32[]{:S(2)}) collective-permute-start(bf16[256,512]{1,0:T(8,128)(2,1)S(1)} %get-tuple-element.25), channel_id=1, source_target_pairs={{0,16},{16,0},{1,17},{17,1},{2,18},{18,2},{3,19},{19,3},{4,20},{20... | collective-permute-start | bytes 786440 | tf_op jit(solution)/shard_map/ppermute | solution.py:252
  53.4 6.6 %copy-start.1 = (bf16[1,1,64,4,3584]{4,3,2,1,0:T(4,128)(2,1)S(1)}, bf16[1,1,64,4,3584]{4,3,2,1,0:T(4,128)(2,1)}, u32[]{:S(2)}) copy-start(bf16[1,1,64,4,3584]{4,3,2,1,0:T(4,128)(2,1)} %param.8) | copy-start | bytes 5505028

commit v4 on v3

v4 whole, which is shorter than its diff:
```python
import functools

import jax
import jax.numpy as jnp
from jax import lax
from jax.experimental import pallas as pl
from jax.experimental.pallas import tpu as pltpu
from jax.sharding import PartitionSpec as P

F32, BF16 = jnp.float32, jnp.bfloat16
MIB = 1024 * 1024
VMEM_LIMIT = 24 * MIB
VMEM = 58 * MIB


def dot(a, b, contract_a, contract_b):
    return lax.dot_general(a, b, (((contract_a,), (contract_b,)), ((), ())), preferred_element_type=F32)


def flat_rows(block):
    return block.reshape(block.shape[0] * block.shape[1], block.shape[2])


def log2(n):
    assert n & (n - 1) == 0
    return n.bit_length() - 1


def halving_order(size):
    order = [0]
    for i in reversed(range(log2(size))):
        order = order + [d ^ (1 << i) for d in order]
    return order


def bit_reverse(value, bits):
    out = jnp.zeros_like(value)
    for i in range(bits):
        out = out | (((value >> i) & 1) << (bits - 1 - i))
    return out


def shift_order(nodes):
    return sorted(range(1, nodes), key=lambda k: (-min(k, nodes - k), k)) + [0]


def column(weights, counts, first, out_rows):
    weights = weights.T
    slots, nodes = weights.shape
    slot = first + lax.broadcasted_iota(jnp.int32, (slots, nodes), 0)
    factor = weights * jnp.where(slot < counts, 1.0, 0.0)
    spread = jnp.broadcast_to(factor[:, None, :], (slots, nodes, nodes)).reshape(out_rows, nodes)
    row = lax.broadcasted_iota(jnp.int32, (out_rows, nodes), 0)
    lane = lax.broadcasted_iota(jnp.int32, (out_rows, nodes), 1)
    return jnp.sum(jnp.where((row & (nodes - 1)) == lane, spread, 0.0), axis=1, keepdims=True)


def pick_slots(weights, first, keep):
    out = weights[:, :keep]
    for at in range(keep, weights.shape[1], keep):
        out = jnp.where(first == at, weights[:, at:at + keep], out)
    return out


def share_kernel(blocks, tok_hbm, grad_hbm, weights_hbm, counts_hbm, out, tok, grad, weights, counts, sem):
    keep, nodes, part = tok.shape
    me, other = lax.axis_index("local"), 1 - lax.axis_index("dp")
    cols = pl.ds(pl.multiple_of(other * part, 128), part)
    firsts = [(me ^ d) * keep for d in blocks]
    copies = [pltpu.make_async_copy(grad_hbm.at[pl.ds(first, keep), :, cols], grad.at[b], sem.at[b]) for b, first in enumerate(firsts)]
    copies.append(pltpu.make_async_copy(tok_hbm.at[pl.ds(firsts[0], keep), :, cols], tok, sem.at[len(blocks)]))
    small = [pltpu.make_async_copy(weights_hbm, weights, sem.at[len(blocks) + 1]),
             pltpu.make_async_copy(counts_hbm, counts, sem.at[len(blocks) + 2])]
    for copy in small + copies:
        copy.start()
    rows = keep * nodes
    for copy in small:
        copy.wait()
    for b, first in enumerate(firsts):
        factor = column(pick_slots(weights[...], first, keep), counts[...], first, rows)
        copies[b].wait()
        out[b * rows:(b + 1) * rows] = (flat_rows(grad[b].astype(F32)) * factor).astype(BF16)
    copies[-1].wait()
    out[len(blocks) * rows:] = flat_rows(tok[...])


def share(order, tokens, grads, weights, counts):
    slots, nodes, width = tokens.shape
    keep, part = slots // len(order), width // 2
    blocks = order[:1]
    vmem, hbm = pl.BlockSpec(memory_space=pltpu.VMEM), pl.BlockSpec(memory_space=pltpu.HBM)
    return pl.pallas_call(
        functools.partial(share_kernel, blocks),
        out_shape=jax.ShapeDtypeStruct(((len(blocks) + 1) * keep * nodes, part), BF16),
        in_specs=[hbm] * 4,
        out_specs=vmem,
        scratch_shapes=[pltpu.VMEM((keep, nodes, part), BF16), pltpu.VMEM((len(blocks), keep, nodes, part), BF16),
                        pltpu.VMEM(weights.shape, F32), pltpu.VMEM(counts.shape, jnp.int32),
                        pltpu.SemaphoreType.DMA((len(blocks) + 3,))],
        compiler_params=pltpu.CompilerParams(vmem_limit_bytes=VMEM),
        name="share",
    )(tokens, grads, weights, counts)


def forward_kernel(locals_, chunk, tok_hbm, grad_hbm, weights_hbm, counts_hbm, wg_hbm, wu_hbm, wd_hbm,
                   acts, own_a, own_b, send_a, send_b,
                   tok, grad, weights, counts, wgu, wd, acc, acc_h, moved, sem):
    slots, nodes, width = tok.shape
    rows = slots * nodes
    keep = slots // locals_
    steps = width // chunk
    hid_local = wd.shape[1]
    me, node = lax.axis_index("local"), lax.axis_index("node")

    def fetch(i):
        cols = pl.ds(i * chunk, chunk)
        ends = [(tok_hbm.at[:, :, cols], tok.at[:, :, cols]), (wg_hbm.at[cols], wgu.at[cols, :hid_local]),
                (wu_hbm.at[cols], wgu.at[cols, hid_local:]), (grad_hbm.at[:, :, cols], grad.at[:, :, cols]), (wd_hbm.at[cols], wd.at[cols])]
        return [pltpu.make_async_copy(src, dst, sem.at[i, n]) for n, (src, dst) in enumerate(ends)]

    small = [pltpu.make_async_copy(weights_hbm, weights, sem.at[steps, 0]), pltpu.make_async_copy(counts_hbm, counts, sem.at[steps, 1])]
    copies = [fetch(i) for i in range(steps)]
    for group in [small] + copies:
        for copy in group:
            copy.start()
    for copy in small:
        copy.wait()
    factor = column(weights[...], counts[...], 0, rows)
    for i in range(steps):
        cols = pl.ds(i * chunk, chunk)
        for copy in copies[i][:3]:
            copy.wait()
        both = dot(flat_rows(tok[:, :, cols]), wgu[cols], 1, 0)
        for copy in copies[i][3:]:
            copy.wait()
        scaled = (flat_rows(grad[:, :, cols].astype(F32)) * factor).astype(BF16)
        back = dot(scaled, wd[cols], 1, 0)
        if i:
            acc[...] += both
            acc_h[...] += back
        else:
            acc[...] = both
            acc_h[...] = back

    band = 64

    def activate(i, carry):
        at = pl.ds(pl.multiple_of(i * band, band), band)
        gate, up, back = acc[at, :hid_local], acc[at, hid_local:], acc_h[at]
        sig = jax.nn.sigmoid(gate)
        act = gate * sig
        acts[2, at] = (act * up).astype(BF16)
        acts[0, at] = (back * up * sig * (1.0 + gate * (1.0 - sig))).astype(BF16)
        acts[1, at] = (back * act).astype(BF16)
        return carry

    lax.fori_loop(0, rows // band, activate, 0)

    per = nodes // 2
    p = lax.broadcasted_iota(jnp.int32, (rows, 1), 0)
    j = p & (keep - 1)
    at = log2(keep)
    quick = (p >> at) & (per - 1)
    at += log2(per)
    low = (p >> at) & (locals_ // 2 - 1)
    at += log2(locals_ // 2)
    group = (p >> at) & 1
    high = p >> (at + 1)
    place = bit_reverse(high * (locals_ // 2) + low, log2(locals_)) ^ me
    hop = jnp.zeros_like(p)
    for n, k in enumerate(shift_order(nodes)):
        hop = jnp.where(group * per + quick == n, k, hop)
    index = (place * keep + j) * nodes + ((node + hop) & (nodes - 1))
    one_hot = jnp.where(index == lax.broadcasted_iota(jnp.int32, (rows, rows), 1), 1.0, 0.0).astype(BF16)
    moved[:, :hid_local] = dot(one_hot, acts[0], 1, 0).astype(BF16)
    moved[:, hid_local:] = dot(one_hot, acts[1], 1, 0).astype(BF16)
    quarter = rows // 4
    for i in range(steps):
        cols = pl.ds(i * chunk, chunk)
        total = dot(moved[...], wgu[cols], 1, 1).astype(BF16)
        for n, out in enumerate((own_a, own_b, send_a, send_b)):
            out[:, cols] = total[n * quarter:(n + 1) * quarter]


def forward(locals_, tokens, grads, weights, counts, gate_weight, up_weight, down_weight):
    slots, nodes, width = tokens.shape
    rows = slots * nodes
    hid_local = gate_weight.shape[1]
    vmem, hbm = pl.BlockSpec(memory_space=pltpu.VMEM), pl.BlockSpec(memory_space=pltpu.HBM)
    chunk = 512
    outside = 2 * (3 * rows * hid_local + rows * width + tokens.size // 2)
    return pl.pallas_call(
        functools.partial(forward_kernel, locals_, chunk),
        out_shape=[jax.ShapeDtypeStruct((3, rows, hid_local), BF16)] + [jax.ShapeDtypeStruct((rows // 4, width), BF16)] * 4,
        in_specs=[hbm] * 7,
        out_specs=[vmem] * 5,
        scratch_shapes=[
            pltpu.VMEM(tokens.shape, BF16), pltpu.VMEM(tokens.shape, BF16), pltpu.VMEM(weights.shape, F32),
            pltpu.VMEM(counts.shape, jnp.int32), pltpu.VMEM((width, 2 * hid_local), BF16), pltpu.VMEM((width, hid_local), BF16),
            pltpu.VMEM((rows, 2 * hid_local), F32), pltpu.VMEM((rows, hid_local), F32), pltpu.VMEM((rows, 2 * hid_local), BF16),
            pltpu.SemaphoreType.DMA((width // chunk + 1, 5))],
        compiler_params=pltpu.CompilerParams(vmem_limit_bytes=VMEM - outside),
        cost_estimate=pl.CostEstimate(flops=10 * rows * width * hid_local, bytes_accessed=18_000_000, transcendentals=0),
        name="forward",
    )(tokens, grads, weights, counts, gate_weight, up_weight, down_weight)


def weight_kernel(order, pieces, acts_at, scaled, *refs):
    count = len(acts_at)
    rows_ref, weights_ref, counts_ref = refs[:3]
    shares = refs[3:3 + len(pieces)]
    own_ref, there_ref = refs[3 + len(pieces):5 + len(pieces)]
    outs = refs[5 + len(pieces):5 + len(pieces) + count]
    left, right, bufs, sem = refs[5 + len(pieces) + count:]
    slots, nodes, width = rows_ref.shape
    rows = slots * nodes
    part, hid_local = outs[0].shape
    me, replica = lax.axis_index("local"), lax.axis_index("dp")
    block = rows // len(order)
    factor = column(weights_ref[...], counts_ref[...], 0, rows) if scaled else None
    for n, a in enumerate(acts_at):
        right[n, :rows] = own_ref[a]
        for b, d in enumerate(order):
            right[n, rows + b * block:rows + (b + 1) * block] = there_ref[a, pl.ds(pl.multiple_of((me ^ d) * block, block), block)]
    chunk = left.shape[1]
    copies = []
    for i in range(part // chunk):
        cols = pl.ds(i * chunk, chunk)
        own = rows_ref[:, :, pl.ds(pl.multiple_of(replica * part + i * chunk, 128), chunk)]
        left[:rows] = (flat_rows(own.astype(F32)) * factor).astype(BF16) if scaled else flat_rows(own)
        at = rows
        for ref, (first, size) in zip(shares, pieces):
            left[at:at + size] = ref[first:first + size, cols]
            at += size
        for n, out in enumerate(outs):
            bufs[n, cols] = dot(left[...], right[n], 0, 0).astype(BF16)
            copies.append(pltpu.make_async_copy(bufs.at[n, cols], out.at[cols], sem.at[i, n]))
            copies[-1].start()
    for copy in copies:
        copy.wait()


def weight_grads(order, rows3, weights, counts, shares, pieces, own_acts, there_acts, acts_at, scaled):
    slots, nodes, width = rows3.shape
    part = shares[0].shape[-1]
    rows, hid_local = own_acts.shape[1:]
    count = len(acts_at)
    chunk = 896
    vmem = pl.BlockSpec(memory_space=pltpu.VMEM)
    return pl.pallas_call(
        functools.partial(weight_kernel, order, pieces, acts_at, scaled),
        out_shape=[jax.ShapeDtypeStruct((part, hid_local), BF16)] * count,
        in_specs=[vmem] * (5 + len(shares)),
        out_specs=[pl.BlockSpec(memory_space=pltpu.HBM)] * count,
        scratch_shapes=[pltpu.VMEM((2 * rows, chunk), BF16), pltpu.VMEM((count, 2 * rows, hid_local), BF16),
                        pltpu.VMEM((count, part, hid_local), BF16), pltpu.SemaphoreType.DMA((part // chunk, count))],
        compiler_params=pltpu.CompilerParams(vmem_limit_bytes=VMEM_LIMIT),
        cost_estimate=pl.CostEstimate(flops=4 * rows * part * hid_local * count, bytes_accessed=4_000_000, transcendentals=0),
        name="weight_grads",
    )(rows3, weights, counts, *shares, own_acts, there_acts)


def collect_kernel(*refs):
    *arrived, kept, came, out = refs
    keep, nodes, width = out.shape
    node = lax.axis_index("node")
    last = (kept[...].astype(F32) + came[...].astype(F32)).astype(BF16)
    stacked = jnp.concatenate([last] + [a[...] for a in arrived], axis=0)
    rows = keep * nodes
    p = lax.broadcasted_iota(jnp.int32, (rows, rows), 0)
    source = ((node - (p & (nodes - 1))) & (nodes - 1)) * keep + (p >> log2(nodes))
    one_hot = jnp.where(source == lax.broadcasted_iota(jnp.int32, (rows, rows), 1), 1.0, 0.0).astype(BF16)
    out[...] = dot(one_hot, stacked, 1, 0).astype(BF16).reshape(out.shape)


def after(value, other):
    return lax.optimization_barrier((value, other))[0]


def add(a, b):
    return (a.astype(F32) + b.astype(F32)).astype(BF16)


def on_device(tokens_in, grad_rows, combine_weights, live_counts, w_gate, w_up, w_down):
    slots, nodes, width = tokens_in.shape[2:]
    replicas, locals_ = lax.axis_size("dp"), lax.axis_size("local")
    assert replicas == 2
    keep = slots // locals_
    tokens, grads, weights, counts = tokens_in[0, 0], grad_rows[0, 0], combine_weights[0, 0].T, live_counts[0]
    order = halving_order(locals_)
    bits = [1 << i for i in range(log2(locals_))]

    def swap_local(value, bit):
        return lax.ppermute(value, "local", [(i, i ^ bit) for i in range(locals_)])

    def swap_dp(value):
        return lax.ppermute(value, "dp", [(0, 1), (1, 0)])

    rows = slots * nodes
    block = rows // locals_
    first, weights = lax.optimization_barrier((share(order, tokens, grads, weights, counts), weights))
    first = swap_dp(first)
    acts, own_a, own_b, send_a, send_b = forward(locals_, tokens, grads, weights, counts, w_gate[0], w_up[0], w_down[0])
    there = swap_dp(acts)

    per = nodes // 2
    hops = shift_order(nodes)
    arrived = [None] * nodes
    send_a, send_b = after(send_a, first), after(send_b, first)
    held = [(own_a, swap_local(send_a, bits[0])), (own_b, swap_local(send_b, bits[0]))]
    for bit in bits[1:]:
        for g, (mine, other) in enumerate(held):
            half = mine.shape[0] // 2
            held[g] = (add(mine[:half], other[:half]), swap_local(add(mine[half:], other[half:]), bit))
    first = after(first, held[0][1])
    shares = [first]
    for bit in reversed(bits[1:]):
        shares = shares + [swap_local(v, bit) for v in shares]
    for n, k in enumerate(hops):
        mine, other = (v[n % per * keep:(n % per + 1) * keep] for v in held[n // per])
        if k:
            total = add(mine, other)
            if n == nodes - 2:
                total = after(total, there)
            arrived[k] = lax.ppermute(total, "node", [(i, (i + k) % nodes) for i in range(nodes)])
        else:
            arrived[0] = (mine, other)
    d_tokens = pl.pallas_call(
        collect_kernel,
        out_shape=jax.ShapeDtypeStruct((keep, nodes, width), BF16),
        in_specs=[pl.BlockSpec(memory_space=pltpu.VMEM)] * (nodes + 1),
        out_specs=pl.BlockSpec(memory_space=pltpu.VMEM),
        compiler_params=pltpu.CompilerParams(vmem_limit_bytes=VMEM_LIMIT),
        name="collect",
    )(*arrived[1:], *arrived[0])
    shares[-1] = after(shares[-1], d_tokens)
    shares = shares + [swap_local(v, bits[0]) for v in shares]

    grad_gate, grad_up = weight_grads(order, tokens, weights, counts, shares, [(block, block)] * locals_, acts, there, (0, 1), False)
    (grad_down,) = weight_grads(order, grads, weights, counts, shares, [(0, block)] * locals_, acts, there, (2,), True)
    return d_tokens[None, None], grad_gate[None], grad_up[None], grad_down[None]


def solution(mesh):
    return jax.shard_map(
        on_device,
        mesh=mesh,
        in_specs=(
            P("dp", "node", None, None, None),
            P("dp", "node", None, None, None),
            P("dp", "node", None, None),
            P("dp", "node", None),
            P("node", None, "local"),
            P("node", None, "local"),
            P("node", None, "local"),
        ),
        out_specs=(
            P("dp", "node", "local", None, None),
            P("node", "dp", "local"),
            P("node", "dp", "local"),
            P("node", "dp", "local"),
        ),
        check_vma=False,
    )
```

time: 62.6 us -> 51.4 us (0.82)
  the two profiles are of different devices: /device:TPU:28 before, /device:TPU:0 now
where the time goes in v4:
time: 51.4 us; the launch traced here: 51.2 us
  Pallas kernels  18.5 us (36%)
  starting transfers between devices  17.1 us (33%)
  waiting for transfers between devices  12.2 us (24%)
  other arithmetic  2.57 us (5%)
  between operations  0.76 us (1%)
    pallas_call x1, Pallas kernels, forward(): pl.pallas_call(functools.partial(forward_kernel, locals_, chunk), out_sha...  9.97 us
    ppermute x3, starting transfers between devices, on_device(): lax.ppermute(total, 'node', [(i, (i + k) % nodes) for i in range(nodes)])  8.33 us
    ppermute x7, waiting for transfers between devices, swap_local(): return lax.ppermute(value, 'local', [(i, i ^ bit) for i in range(locals_)])  6.85 us
    pallas_call x2, Pallas kernels, weight_grads(): pl.pallas_call(functools.partial(weight_kernel, order, pieces, acts_at, s...  5.51 us
    ppermute x2, starting transfers between devices, swap_dp(): return lax.ppermute(value, 'dp', [(0, 1), (1, 0)])  4.74 us
    ppermute x7, starting transfers between devices, swap_local(): return lax.ppermute(value, 'local', [(i, i ^ bit) for i in range(locals_)])  3.98 us
    ppermute x2, waiting for transfers between devices, swap_dp(): return lax.ppermute(value, 'dp', [(0, 1), (1, 0)])  3.13 us
    convert_element_type x4, other arithmetic, add(): return (a.astype(F32) + b.astype(F32)).astype(BF16)  2.57 us
  transfers between devices with their start and end apart: 12, of which 6 were waited for; matrix products, arithmetic and copies ran while one was open for 5% of the time, Pallas kernels for 22%

profile of v4, /device:TPU:0, one launch (start us, length us, event | category | flops | bytes accessed | tf_op | source)
XLA Modules:
  0.0 51.2 jit_solution(13426508010905231808)
XLA Ops:
  0.6 2.0 %share.1 = bf16[128,1792]{1,0:T(8,128)(2,1)} custom-call(bf16[64,4,3584]{2,1,0:T(4,128)(2,1)} %bitcast.16, bf16[64,4,3584]{2,1,0:T(4,128)(2,1)} %bitcast.13, f32[4,64]{1,0:T(4,128)} %bitcast.19, s32[1,4]{1,0:T(1,128)} %bitcast.23), custom_call_target="tpu_custom_call" | custom-call | tf_op jit(solution)/shard_map/share/pallas_call | solution.py:92
  2.6 3.0 %collective-permute-start = (bf16[128,1792]{1,0:T(8,128)(2,1)}, bf16[128,1792]{1,0:T(8,128)(2,1)S(1)}, u32[]{:S(2)}, u32[]{:S(2)}) collective-permute-start(bf16[128,1792]{1,0:T(8,128)(2,1)} %share.1), channel_id=1, source_target_pairs={{0,16},{16,0},{1,17},{17,1},{2,18},{18,2},{3,19},{19,3},{4,20},{20... | collective-permute-start | bytes 1376264 | tf_op jit(solution)/shard_map/ppermute | solution.py:297
  5.7 10.0 %forward.1 = (bf16[3,256,512]{2,1,0:T(8,128)(2,1)}, bf16[64,3584]{1,0:T(8,128)(2,1)}, bf16[64,3584]{1,0:T(8,128)(2,1)}, bf16[64,3584]{1,0:T(8,128)(2,1)}, bf16[64,3584]{1,0:T(8,128)(2,1)}) custom-call(bf16[64,4,3584]{2,1,0:T(4,128)(2,1)} %bitcast.17, bf16[64,4,3584]{2,1,0:T(4,128)(2,1)} %bitcast.14, f32[4,64]{1,0:T(4,128)} %bitcast.20, s32[1,4]{1,0:T(1,128)} %bitcast.24, ...), custom_call_target="tpu_custom_call" | custom-call | flops 4697620480 | bytes 18000000 | tf_op jit(solution)/shard_map/forward/pallas_call | solution.py:192
  15.6 0.7 %collective-permute-done.refs_3_ = bf16[128,1792]{1,0:T(8,128)(2,1)S(1)} collective-permute-done((bf16[128,1792]{1,0:T(8,128)(2,1)}, bf16[128,1792]{1,0:T(8,128)(2,1)S(1)}, u32[]{:S(2)}, u32[]{:S(2)}) %collective-permute-start) | collective-permute-done | bytes 458784 | tf_op jit(solution)/shard_map/ppermute | solution.py:297
  16.4 1.7 %collective-permute-start.7 = (bf16[3,256,512]{2,1,0:T(8,128)(2,1)}, bf16[3,256,512]{2,1,0:T(8,128)(2,1)S(1)}, u32[]{:S(2)}, u32[]{:S(2)}) collective-permute-start(bf16[3,256,512]{2,1,0:T(8,128)(2,1)} %get-tuple-element.26.refs_7_), channel_id=1, source_target_pairs={{0,16},{16,0},{1,17},{17,1},{2,18},{18,2},{3,19},{19,3},{4,20},{20... | collective-permute-start | bytes 2359304 | tf_op jit(solution)/shard_map/ppermute | solution.py:297
  18.1 0.2 collective-permute-start.5
  18.4 0.1 collective-permute-done.1
  18.4 1.2 %add_convert_fusion.3 = (bf16[32,3584]{1,0:T(8,128)(2,1)S(1)}, bf16[32,3584]{1,0:T(8,128)(2,1)S(1)}) fusion(bf16[64,3584]{1,0:T(8,128)(2,1)S(1)} %collective-permute-done.1, bf16[64,3584]{1,0:T(8,128)(2,1)} %get-tuple-element.19), kind=kLoop, calls=%fused_computation.3 | loop fusion | flops 917504 | bytes 1376256 | tf_op jit(solution)/shard_map/convert_element_type | solution.py:281
  19.6 1.8 %collective-permute-start.2 = (bf16[32,3584]{1,0:T(8,128)(2,1)S(1)}, bf16[32,3584]{1,0:T(8,128)(2,1)S(1)}, u32[]{:S(2)}, u32[]{:S(2)}) collective-permute-start(bf16[32,3584]{1,0:T(8,128)(2,1)S(1)} %get-tuple-element.35), channel_id=1, source_target_pairs={{0,2},{1,3},{2,0},{3,1},{4,6},{5,7},{6,4},{7,5},{8,10},{9,11},{10,... | collective-permute-start | bytes 688136 | tf_op jit(solution)/shard_map/ppermute | solution.py:294
  21.4 1.3 %add_convert_fusion.1 = (bf16[32,3584]{1,0:T(8,128)(2,1)S(1)}, bf16[32,3584]{1,0:T(8,128)(2,1)S(1)}) fusion(bf16[64,3584]{1,0:T(8,128)(2,1)S(1)} %collective-permute-done.5, bf16[64,3584]{1,0:T(8,128)(2,1)} %get-tuple-element.23), kind=kLoop, calls=%fused_computation.1 | loop fusion | flops 917504 | bytes 1376256 | tf_op jit(solution)/shard_map/convert_element_type | solution.py:281
  22.8 0.3 collective-permute-start.6
  23.1 5.0 %collective-permute-done.2 = bf16[32,3584]{1,0:T(8,128)(2,1)S(1)} collective-permute-done((bf16[32,3584]{1,0:T(8,128)(2,1)S(1)}, bf16[32,3584]{1,0:T(8,128)(2,1)S(1)}, u32[]{:S(2)}, u32[]{:S(2)}) %collective-permute-start.2) | collective-permute-done | bytes 229408 | tf_op jit(solution)/shard_map/ppermute | solution.py:294
  28.1 0.1 add_convert_fusion.5
  28.1 1.9 %collective-permute-start.3 = (bf16[16,3584]{1,0:T(8,128)(2,1)S(1)}, bf16[16,3584]{1,0:T(8,128)(2,1)S(1)}, u32[]{:S(2)}, u32[]{:S(2)}) collective-permute-start(bf16[16,3584]{1,0:T(8,128)(2,1)S(1)} %get-tuple-element.37), channel_id=1, source_target_pairs={{0,4},{4,8},{8,12},{12,0},{1,5},{5,9},{9,13},{13,1},{2,6},{6,10},{... | collective-permute-start | bytes 344072 | tf_op jit(solution)/shard_map/ppermute | solution.py:325
  30.0 2.6 %collective-permute-start.4 = (bf16[16,3584]{1,0:T(8,128)(2,1)S(1)}, bf16[16,3584]{1,0:T(8,128)(2,1)S(1)}, u32[]{:S(2)}, u32[]{:S(2)}) collective-permute-start(bf16[16,3584]{1,0:T(8,128)(2,1)S(1)} %get-tuple-element.36), channel_id=1, source_target_pairs={{0,8},{4,12},{8,0},{12,4},{1,9},{5,13},{9,1},{13,5},{2,10},{6,14},... | collective-permute-start | bytes 344072 | tf_op jit(solution)/shard_map/ppermute | solution.py:325
  32.6 1.5 %collective-permute-start.9 = (bf16[128,1792]{1,0:T(8,128)(2,1)S(1)}, bf16[128,1792]{1,0:T(8,128)(2,1)S(1)}, u32[]{:S(2)}, u32[]{:S(2)}) collective-permute-start(bf16[128,1792]{1,0:T(8,128)(2,1)S(1)} %collective-permute-done.refs_3_), channel_id=1, source_target_pairs={{0,2},{1,3},{2,0},{3,1},{4,6},{5,7},{6,4},{7,5},{8,10},{9,11},{10,... | collective-permute-start | bytes 1376264 | tf_op jit(solution)/shard_map/ppermute | solution.py:294
  34.2 2.4 %collective-permute-done.7.refs_8_ = bf16[3,256,512]{2,1,0:T(8,128)(2,1)S(1)} collective-permute-done((bf16[3,256,512]{2,1,0:T(8,128)(2,1)}, bf16[3,256,512]{2,1,0:T(8,128)(2,1)S(1)}, u32[]{:S(2)}, u32[]{:S(2)}) %collective-permute-start.7) | collective-permute-done | bytes 786464 | tf_op jit(solution)/shard_map/ppermute | solution.py:297
  36.5 3.9 %collective-permute-start.8 = (bf16[16,3584]{1,0:T(8,128)(2,1)S(1)}, bf16[16,3584]{1,0:T(8,128)(2,1)S(1)}, u32[]{:S(2)}, u32[]{:S(2)}) collective-permute-start(bf16[16,3584]{1,0:T(8,128)(2,1)S(1)} %add_convert_fusion.4), channel_id=1, source_target_pairs={{0,12},{4,0},{8,4},{12,8},{1,13},{5,1},{9,5},{13,9},{2,14},{6,2},{... | collective-permute-start | bytes 344072 | tf_op jit(solution)/shard_map/ppermute | solution.py:325
  40.4 0.1 collective-permute-start.10
  40.5 2.2 %collective-permute-done.8.refs_2_ = bf16[16,3584]{1,0:T(8,128)(2,1)S(1)} collective-permute-done((bf16[16,3584]{1,0:T(8,128)(2,1)S(1)}, bf16[16,3584]{1,0:T(8,128)(2,1)S(1)}, u32[]{:S(2)}, u32[]{:S(2)}) %collective-permute-start.8) | collective-permute-done | bytes 114720 | tf_op jit(solution)/shard_map/ppermute | solution.py:325
  42.8 1.0 %collect.1 = bf16[16,4,3584]{2,1,0:T(4,128)(2,1)} custom-call(bf16[16,3584]{1,0:T(8,128)(2,1)S(1)} %collective-permute-done.3.refs_0_, bf16[16,3584]{1,0:T(8,128)(2,1)S(1)} %collective-permute-done.4.refs_1_, bf16[16,3584]{1,0:T(8,128)(2,1)S(1)} %collective-permute-done.8.refs_2_, bf16[16,3584]{1,0:T(8,128)(2,1)S(1)} %slice.74.refs_3_, ...), custom_call_target="tpu_custom_call" | custom-call | tf_op jit(solution)/shard_map/collect/pallas_call | solution.py:328
  43.8 1.8 %collective-permute-done.11.refs_6_ = bf16[128,1792]{1,0:T(8,128)(2,1)S(1)} collective-permute-done((bf16[128,1792]{1,0:T(8,128)(2,1)S(1)}, bf16[128,1792]{1,0:T(8,128)(2,1)S(1)}, u32[]{:S(2)}, u32[]{:S(2)}) %collective-permute-start.11) | collective-permute-done | bytes 458784 | tf_op jit(solution)/shard_map/ppermute | solution.py:294
  45.7 3.1 %weight_grads.2 = (bf16[1792,512]{1,0:T(8,128)(2,1)}, bf16[1792,512]{1,0:T(8,128)(2,1)}) custom-call(bf16[64,4,3584]{2,1,0:T(4,128)(2,1)S(1)} %bitcast.18, f32[4,64]{1,0:T(4,128)S(1)} %bitcast.21, s32[1,4]{1,0:T(1,128)S(1)} %bitcast.25, bf16[128,1792]{1,0:T(8,128)(2,1)S(1)} %collective-permute-done.refs_3_, ...), custom_call_target="tpu_custom_call" | custom-call | flops 1879048192 | bytes 4000000 | tf_op jit(solution)/shard_map/weight_grads/pallas_call | solution.py:250
  48.8 2.4 %weight_grads.3 = bf16[1792,512]{1,0:T(8,128)(2,1)} custom-call(bf16[64,4,3584]{2,1,0:T(4,128)(2,1)S(1)} %bitcast.15, f32[4,64]{1,0:T(4,128)S(1)} %bitcast.22, s32[1,4]{1,0:T(1,128)S(1)} %bitcast.26, bf16[128,1792]{1,0:T(8,128)(2,1)S(1)} %collective-permute-done.refs_3_, bf16[128,1792]{1,0:T(8,128)(2,1)S(1)} %collective-permute-done.9.refs_4_, ...), custom_call_target="tpu_custom_call" | custom-call | flops 939524096 | bytes 4000000 | tf_op jit(solution)/shard_map/weight_grads/pallas_call | solution.py:250
  (21 shorter events, 0.1 us)
Async XLA Ops:
  2.6 13.7 %collective-permute-start = (bf16[128,1792]{1,0:T(8,128)(2,1)}, bf16[128,1792]{1,0:T(8,128)(2,1)S(1)}, u32[]{:S(2)}, u32[]{:S(2)}) collective-permute-start(bf16[128,1792]{1,0:T(8,128)(2,1)} %share.1), channel_id=1, source_target_pairs={{0,16},{16,0},{1,17},{17,1},{2,18},{18,2},{3,19},{19,3},{4,20},{20... | collective-permute-start | bytes 1376264 | tf_op jit(solution)/shard_map/ppermute | solution.py:297
  16.4 2.0 %collective-permute-start.1 = (bf16[64,3584]{1,0:T(8,128)(2,1)}, bf16[64,3584]{1,0:T(8,128)(2,1)S(1)}, u32[]{:S(2)}, u32[]{:S(2)}) collective-permute-start(bf16[64,3584]{1,0:T(8,128)(2,1)} %get-tuple-element.22), channel_id=1, source_target_pairs={{0,1},{1,0},{2,3},{3,2},{4,5},{5,4},{6,7},{7,6},{8,9},{9,8},{10,11... | collective-permute-start | bytes 1376264 | tf_op jit(solution)/shard_map/ppermute | solution.py:294
  16.4 20.2 %collective-permute-start.7 = (bf16[3,256,512]{2,1,0:T(8,128)(2,1)}, bf16[3,256,512]{2,1,0:T(8,128)(2,1)S(1)}, u32[]{:S(2)}, u32[]{:S(2)}) collective-permute-start(bf16[3,256,512]{2,1,0:T(8,128)(2,1)} %get-tuple-element.26.refs_7_), channel_id=1, source_target_pairs={{0,16},{16,0},{1,17},{17,1},{2,18},{18,2},{3,19},{19,3},{4,20},{20... | collective-permute-start | bytes 2359304 | tf_op jit(solution)/shard_map/ppermute | solution.py:297
  18.1 3.3 %collective-permute-start.5 = (bf16[64,3584]{1,0:T(8,128)(2,1)}, bf16[64,3584]{1,0:T(8,128)(2,1)S(1)}, u32[]{:S(2)}, u32[]{:S(2)}) collective-permute-start(bf16[64,3584]{1,0:T(8,128)(2,1)} %get-tuple-element.25), channel_id=1, source_target_pairs={{0,1},{1,0},{2,3},{3,2},{4,5},{5,4},{6,7},{7,6},{8,9},{9,8},{10,11... | collective-permute-start | bytes 1376264 | tf_op jit(solution)/shard_map/ppermute | solution.py:294
  19.6 8.5 %collective-permute-start.2 = (bf16[32,3584]{1,0:T(8,128)(2,1)S(1)}, bf16[32,3584]{1,0:T(8,128)(2,1)S(1)}, u32[]{:S(2)}, u32[]{:S(2)}) collective-permute-start(bf16[32,3584]{1,0:T(8,128)(2,1)S(1)} %get-tuple-element.35), channel_id=1, source_target_pairs={{0,2},{1,3},{2,0},{3,1},{4,6},{5,7},{6,4},{7,5},{8,10},{9,11},{10,... | collective-permute-start | bytes 688136 | tf_op jit(solution)/shard_map/ppermute | solution.py:294
  21.4 24.2 %copy-start.1 = (bf16[1,1,64,4,3584]{4,3,2,1,0:T(4,128)(2,1)S(1)}, bf16[1,1,64,4,3584]{4,3,2,1,0:T(4,128)(2,1)}, u32[]{:S(2)}) copy-start(bf16[1,1,64,4,3584]{4,3,2,1,0:T(4,128)(2,1)} %param.7) | copy-start | bytes 5505028
  21.4 24.2 %copy-start.2 = (bf16[3,256,512]{2,1,0:T(8,128)(2,1)S(1)}, bf16[3,256,512]{2,1,0:T(8,128)(2,1)}, u32[]{:S(2)}) copy-start(bf16[3,256,512]{2,1,0:T(8,128)(2,1)} %get-tuple-element.26.refs_7_) | copy-start | bytes 2359300
  21.4 24.2 %copy-start.3 = (f32[1,1,64,4]{2,3,1,0:T(4,128)S(1)}, f32[1,1,64,4]{2,3,1,0:T(4,128)}, u32[]{:S(2)}) copy-start(f32[1,1,64,4]{2,3,1,0:T(4,128)} %param.9) | copy-start | bytes 3076
  21.4 24.2 %copy-start.4 = (s32[1,1,4]{2,1,0:T(1,128)S(1)}, s32[1,1,4]{2,1,0:T(1,128)}, u32[]{:S(2)}) copy-start(s32[1,1,4]{2,1,0:T(1,128)} %param.10) | copy-start | bytes 52
  22.8 11.4 %collective-permute-start.6 = (bf16[32,3584]{1,0:T(8,128)(2,1)S(1)}, bf16[32,3584]{1,0:T(8,128)(2,1)S(1)}, u32[]{:S(2)}, u32[]{:S(2)}) collective-permute-start(bf16[32,3584]{1,0:T(8,128)(2,1)S(1)} %get-tuple-element.33), channel_id=1, source_target_pairs={{0,2},{1,3},{2,0},{3,1},{4,6},{5,7},{6,4},{7,5},{8,10},{9,11},{10,... | collective-permute-start | bytes 688136 | tf_op jit(solution)/shard_map/ppermute | solution.py:294
  28.1 12.4 %collective-permute-start.3 = (bf16[16,3584]{1,0:T(8,128)(2,1)S(1)}, bf16[16,3584]{1,0:T(8,128)(2,1)S(1)}, u32[]{:S(2)}, u32[]{:S(2)}) collective-permute-start(bf16[16,3584]{1,0:T(8,128)(2,1)S(1)} %get-tuple-element.37), channel_id=1, source_target_pairs={{0,4},{4,8},{8,12},{12,0},{1,5},{5,9},{9,13},{13,1},{2,6},{6,10},{... | collective-permute-start | bytes 344072 | tf_op jit(solution)/shard_map/ppermute | solution.py:325
  30.0 10.5 %collective-permute-start.4 = (bf16[16,3584]{1,0:T(8,128)(2,1)S(1)}, bf16[16,3584]{1,0:T(8,128)(2,1)S(1)}, u32[]{:S(2)}, u32[]{:S(2)}) collective-permute-start(bf16[16,3584]{1,0:T(8,128)(2,1)S(1)} %get-tuple-element.36), channel_id=1, source_target_pairs={{0,8},{4,12},{8,0},{12,4},{1,9},{5,13},{9,1},{13,5},{2,10},{6,14},... | collective-permute-start | bytes 344072 | tf_op jit(solution)/shard_map/ppermute | solution.py:325
  32.6 11.2 %collective-permute-start.9 = (bf16[128,1792]{1,0:T(8,128)(2,1)S(1)}, bf16[128,1792]{1,0:T(8,128)(2,1)S(1)}, u32[]{:S(2)}, u32[]{:S(2)}) collective-permute-start(bf16[128,1792]{1,0:T(8,128)(2,1)S(1)} %collective-permute-done.refs_3_), channel_id=1, source_target_pairs={{0,2},{1,3},{2,0},{3,1},{4,6},{5,7},{6,4},{7,5},{8,10},{9,11},{10,... | collective-permute-start | bytes 1376264 | tf_op jit(solution)/shard_map/ppermute | solution.py:294
  36.5 6.2 %collective-permute-start.8 = (bf16[16,3584]{1,0:T(8,128)(2,1)S(1)}, bf16[16,3584]{1,0:T(8,128)(2,1)S(1)}, u32[]{:S(2)}, u32[]{:S(2)}) collective-permute-start(bf16[16,3584]{1,0:T(8,128)(2,1)S(1)} %add_convert_fusion.4), channel_id=1, source_target_pairs={{0,12},{4,0},{8,4},{12,8},{1,13},{5,1},{9,5},{13,9},{2,14},{6,2},{... | collective-permute-start | bytes 344072 | tf_op jit(solution)/shard_map/ppermute | solution.py:325
  40.4 3.4 %collective-permute-start.10 = (bf16[128,1792]{1,0:T(8,128)(2,1)S(1)}, bf16[128,1792]{1,0:T(8,128)(2,1)S(1)}, u32[]{:S(2)}, u32[]{:S(2)}) collective-permute-start(bf16[128,1792]{1,0:T(8,128)(2,1)S(1)} %collective-permute-done.refs_3_), channel_id=1, source_target_pairs={{0,1},{1,0},{2,3},{3,2},{4,5},{5,4},{6,7},{7,6},{8,9},{9,8},{10,11... | collective-permute-start | bytes 1376264 | tf_op jit(solution)/shard_map/ppermute | solution.py:294
  43.8 5.0 %copy-start = (bf16[1,1,64,4,3584]{4,3,2,1,0:T(4,128)(2,1)S(1)}, bf16[1,1,64,4,3584]{4,3,2,1,0:T(4,128)(2,1)}, u32[]{:S(2)}) copy-start(bf16[1,1,64,4,3584]{4,3,2,1,0:T(4,128)(2,1)} %param.8) | copy-start | bytes 5505028
  43.8 1.8 %collective-permute-start.11 = (bf16[128,1792]{1,0:T(8,128)(2,1)S(1)}, bf16[128,1792]{1,0:T(8,128)(2,1)S(1)}, u32[]{:S(2)}, u32[]{:S(2)}) collective-permute-start(bf16[128,1792]{1,0:T(8,128)(2,1)S(1)} %collective-permute-done.9.refs_4_), channel_id=1, source_target_pairs={{0,1},{1,0},{2,3},{3,2},{4,5},{5,4},{6,7},{7,6},{8,9},{9,8},{10,11... | collective-permute-start | bytes 1376264 | tf_op jit(solution)/shard_map/ppermute | solution.py:294

commit v5 on v4

--- a/solution.py
+++ b/solution.py
@@ -11,6 +11,7 @@
 MIB = 1024 * 1024
 VMEM_LIMIT = 24 * MIB
 VMEM = 58 * MIB
+FORWARD_LIMIT = 51 * MIB
 
 
 def dot(a, b, contract_a, contract_b):
@@ -188,7 +189,6 @@
     hid_local = gate_weight.shape[1]
     vmem, hbm = pl.BlockSpec(memory_space=pltpu.VMEM), pl.BlockSpec(memory_space=pltpu.HBM)
     chunk = 512
-    outside = 2 * (3 * rows * hid_local + rows * width + tokens.size // 2)
     return pl.pallas_call(
         functools.partial(forward_kernel, locals_, chunk),
         out_shape=[jax.ShapeDtypeStruct((3, rows, hid_local), BF16)] + [jax.ShapeDtypeStruct((rows // 4, width), BF16)] * 4,
@@ -199,65 +199,88 @@
             pltpu.VMEM(counts.shape, jnp.int32), pltpu.VMEM((width, 2 * hid_local), BF16), pltpu.VMEM((width, hid_local), BF16),
             pltpu.VMEM((rows, 2 * hid_local), F32), pltpu.VMEM((rows, hid_local), F32), pltpu.VMEM((rows, 2 * hid_local), BF16),
             pltpu.SemaphoreType.DMA((width // chunk + 1, 5))],
-        compiler_params=pltpu.CompilerParams(vmem_limit_bytes=VMEM - outside),
+        compiler_params=pltpu.CompilerParams(vmem_limit_bytes=FORWARD_LIMIT),
         cost_estimate=pl.CostEstimate(flops=10 * rows * width * hid_local, bytes_accessed=18_000_000, transcendentals=0),
         name="forward",
     )(tokens, grads, weights, counts, gate_weight, up_weight, down_weight)
 
 
-def weight_kernel(order, pieces, acts_at, scaled, *refs):
+def own_kernel(tok, grad, weights_ref, counts_ref, acts, gate_out, up_out, down_out):
+    slots, nodes, width = tok.shape
+    part = gate_out.shape[0]
+    replica = lax.axis_index("dp")
+    factor = column(weights_ref[...], counts_ref[...], 0, slots * nodes)
+    chunk = 896
+    for i in range(part // chunk):
+        cols = pl.ds(i * chunk, chunk)
+        mine = pl.ds(pl.multiple_of(replica * part + i * chunk, 128), chunk)
+        rows = flat_rows(tok[:, :, mine])
+        gate_out[cols] = dot(rows, acts[0], 0, 0).astype(BF16)
+        up_out[cols] = dot(rows, acts[1], 0, 0).astype(BF16)
+        scaled = (flat_rows(grad[:, :, mine].astype(F32)) * factor).astype(BF16)
+        down_out[cols] = dot(scaled, acts[2], 0, 0).astype(BF16)
+
+
+def own_grads(tokens, grads, weights, counts, acts):
+    slots, nodes, width = tokens.shape
+    rows, hid_local = acts.shape[1:]
+    part = width // 2
+    vmem = pl.BlockSpec(memory_space=pltpu.VMEM)
+    return pl.pallas_call(
+        own_kernel,
+        out_shape=[jax.ShapeDtypeStruct((part, hid_local), BF16)] * 3,
+        in_specs=[vmem] * 5,
+        out_specs=[vmem] * 3,
+        compiler_params=pltpu.CompilerParams(vmem_limit_bytes=VMEM_LIMIT),
+        cost_estimate=pl.CostEstimate(flops=6 * rows * part * hid_local, bytes_accessed=10_000_000, transcendentals=0),
+        name="own_grads",
+    )(tokens, grads, weights, counts, acts)
+
+
+def weight_kernel(order, first, acts_at, *refs):
     count = len(acts_at)
-    rows_ref, weights_ref, counts_ref = refs[:3]
-    shares = refs[3:3 + len(pieces)]
-    own_ref, there_ref = refs[3 + len(pieces):5 + len(pieces)]
-    outs = refs[5 + len(pieces):5 + len(pieces) + count]
-    left, right, bufs, sem = refs[5 + len(pieces) + count:]
-    slots, nodes, width = rows_ref.shape
-    rows = slots * nodes
-    part, hid_local = outs[0].shape
-    me, replica = lax.axis_index("local"), lax.axis_index("dp")
-    block = rows // len(order)
-    factor = column(weights_ref[...], counts_ref[...], 0, rows) if scaled else None
+    shares = refs[:len(order)]
+    there_ref = refs[len(order)]
+    parts = refs[len(order) + 1:len(order) + 1 + count]
+    outs = refs[len(order) + 1 + count:len(order) + 1 + 2 * count]
+    left, right, bufs, sem = refs[len(order) + 1 + 2 * count:]
+    part = outs[0].shape[0]
+    me = lax.axis_index("local")
+    block = shares[0].shape[0] // 2
     for n, a in enumerate(acts_at):
-        right[n, :rows] = own_ref[a]
         for b, d in enumerate(order):
-            right[n, rows + b * block:rows + (b + 1) * block] = there_ref[a, pl.ds(pl.multiple_of((me ^ d) * block, block), block)]
+            right[n, b * block:(b + 1) * block] = there_ref[a, pl.ds(pl.multiple_of((me ^ d) * block, block), block)]
     chunk = left.shape[1]
     copies = []
     for i in range(part // chunk):
         cols = pl.ds(i * chunk, chunk)
-        own = rows_ref[:, :, pl.ds(pl.multiple_of(replica * part + i * chunk, 128), chunk)]
-        left[:rows] = (flat_rows(own.astype(F32)) * factor).astype(BF16) if scaled else flat_rows(own)
-        at = rows
-        for ref, (first, size) in zip(shares, pieces):
-            left[at:at + size] = ref[first:first + size, cols]
-            at += size
+        for b, ref in enumerate(shares):
+            left[b * block:(b + 1) * block] = ref[first:first + block, cols]
         for n, out in enumerate(outs):
-            bufs[n, cols] = dot(left[...], right[n], 0, 0).astype(BF16)
+            bufs[n, cols] = (dot(left[...], right[n], 0, 0) + parts[n][cols].astype(F32)).astype(BF16)
             copies.append(pltpu.make_async_copy(bufs.at[n, cols], out.at[cols], sem.at[i, n]))
             copies[-1].start()
     for copy in copies:
         copy.wait()
 
 
-def weight_grads(order, rows3, weights, counts, shares, pieces, own_acts, there_acts, acts_at, scaled):
-    slots, nodes, width = rows3.shape
+def weight_grads(order, shares, first, there, parts, acts_at):
     part = shares[0].shape[-1]
-    rows, hid_local = own_acts.shape[1:]
+    rows, hid_local = there.shape[1:]
     count = len(acts_at)
     chunk = 896
     vmem = pl.BlockSpec(memory_space=pltpu.VMEM)
     return pl.pallas_call(
-        functools.partial(weight_kernel, order, pieces, acts_at, scaled),
+        functools.partial(weight_kernel, order, first, acts_at),
         out_shape=[jax.ShapeDtypeStruct((part, hid_local), BF16)] * count,
-        in_specs=[vmem] * (5 + len(shares)),
+        in_specs=[vmem] * (1 + len(shares) + count),
         out_specs=[pl.BlockSpec(memory_space=pltpu.HBM)] * count,
-        scratch_shapes=[pltpu.VMEM((2 * rows, chunk), BF16), pltpu.VMEM((count, 2 * rows, hid_local), BF16),
+        scratch_shapes=[pltpu.VMEM((rows, chunk), BF16), pltpu.VMEM((count, rows, hid_local), BF16),
                         pltpu.VMEM((count, part, hid_local), BF16), pltpu.SemaphoreType.DMA((part // chunk, count))],
         compiler_params=pltpu.CompilerParams(vmem_limit_bytes=VMEM_LIMIT),
-        cost_estimate=pl.CostEstimate(flops=4 * rows * part * hid_local * count, bytes_accessed=4_000_000, transcendentals=0),
+        cost_estimate=pl.CostEstimate(flops=2 * rows * part * hid_local * count, bytes_accessed=4_000_000, transcendentals=0),
         name="weight_grads",
-    )(rows3, weights, counts, *shares, own_acts, there_acts)
+    )(*shares, there, *parts)
 
 
 def collect_kernel(*refs):
@@ -312,19 +335,21 @@
         for g, (mine, other) in enumerate(held):
             half = mine.shape[0] // 2
             held[g] = (add(mine[:half], other[:half]), swap_local(add(mine[half:], other[half:]), bit))
-    first = after(first, held[0][1])
-    shares = [first]
+    shares = [after(first, held[0][1])]
     for bit in reversed(bits[1:]):
         shares = shares + [swap_local(v, bit) for v in shares]
+    parts = own_grads(tokens, grads, weights, counts, after(acts, held[1][0]))
+    held[0] = (after(held[0][0], parts[0]), held[0][1])
     for n, k in enumerate(hops):
         mine, other = (v[n % per * keep:(n % per + 1) * keep] for v in held[n // per])
         if k:
             total = add(mine, other)
-            if n == nodes - 2:
-                total = after(total, there)
             arrived[k] = lax.ppermute(total, "node", [(i, (i + k) % nodes) for i in range(nodes)])
         else:
             arrived[0] = (mine, other)
+    early = lax.optimization_barrier([arrived[k] for k in hops[:per]] + [there])
+    for k, value in zip(hops[:per], early):
+        arrived[k] = value
     d_tokens = pl.pallas_call(
         collect_kernel,
         out_shape=jax.ShapeDtypeStruct((keep, nodes, width), BF16),
@@ -333,11 +358,11 @@
         compiler_params=pltpu.CompilerParams(vmem_limit_bytes=VMEM_LIMIT),
         name="collect",
     )(*arrived[1:], *arrived[0])
+
     shares[-1] = after(shares[-1], d_tokens)
     shares = shares + [swap_local(v, bits[0]) for v in shares]
-
-    grad_gate, grad_up = weight_grads(order, tokens, weights, counts, shares, [(block, block)] * locals_, acts, there, (0, 1), False)
-    (grad_down,) = weight_grads(order, grads, weights, counts, shares, [(0, block)] * locals_, acts, there, (2,), True)
+    grad_gate, grad_up = weight_grads(order, shares, block, there, parts[:2], (0, 1))
+    (grad_down,) = weight_grads(order, shares, 0, there, parts[2:], (2,))
     return d_tokens[None, None], grad_gate[None], grad_up[None], grad_down[None]
 
 

time: 51.4 us -> 47.1 us (0.916)
  other arithmetic: 2.57 us -> 0.3 us
  Pallas kernels: 18.5 us -> 17.8 us
  waiting for transfers between devices: 12.2 us -> 11.5 us
    convert_element_type x4, other arithmetic: 2.57 us -> 0.3 us  [add(): return (a.astype(F32) + b.astype(F32)).astype(BF16)]
    ppermute x3, starting transfers between devices: 8.33 us -> 6.99 us  [on_device(): lax.ppermute(total, 'node', [(i, (i + k) % nodes) for i in range(nodes)])]
    pallas_call x1, Pallas kernels: 9.97 us -> 8.9 us  [forward(): pl.pallas_call(functools.partial(forward_kernel, locals_, chunk), out_sha...]
    ppermute x7, starting transfers between devices: 3.98 us -> 4.91 us  [swap_local(): return lax.ppermute(value, 'local', [(i, i ^ bit) for i in range(locals_)])]
    ppermute x7, waiting for transfers between devices: 6.85 us -> 5.96 us  [swap_local(): return lax.ppermute(value, 'local', [(i, i ^ bit) for i in range(locals_)])]
    ppermute x3, waiting for transfers between devices: 2.24 us -> 3.07 us  [on_device(): lax.ppermute(total, 'node', [(i, (i + k) % nodes) for i in range(nodes)])]
    ppermute x2, waiting for transfers between devices: 3.13 us -> 2.45 us  [swap_dp(): return lax.ppermute(value, 'dp', [(0, 1), (1, 0)])]
    pallas_call x2 -> x3, Pallas kernels: 5.51 us -> 5.77 us  [the longest x2 3.98 us: weight_grads(): pl.pallas_call(functools.partial(weight_kernel, order, first, acts_at), o...]
  transfers between devices with their start and end apart: 12 -> 12, of which waited for: 6 -> 7; matrix products, arithmetic and copies ran while one was open for 5% -> 1% of each run, Pallas kernels for 22% -> 25%
where the time goes in v5:
time: 47.1 us; the launch traced here: 46.9 us
  Pallas kernels  17.8 us (38%)
  starting transfers between devices  16.6 us (35%)
  waiting for transfers between devices  11.5 us (24%)
  between operations  0.73 us (2%)
    pallas_call x1, Pallas kernels, forward(): pl.pallas_call(functools.partial(forward_kernel, locals_, chunk), out_sha...  8.9 us
    ppermute x3, starting transfers between devices, on_device(): lax.ppermute(total, 'node', [(i, (i + k) % nodes) for i in range(nodes)])  6.99 us
    ppermute x7, waiting for transfers between devices, swap_local(): return lax.ppermute(value, 'local', [(i, i ^ bit) for i in range(locals_)])  5.96 us
    ppermute x7, starting transfers between devices, swap_local(): return lax.ppermute(value, 'local', [(i, i ^ bit) for i in range(locals_)])  4.91 us
    ppermute x2, starting transfers between devices, swap_dp(): return lax.ppermute(value, 'dp', [(0, 1), (1, 0)])  4.74 us
    pallas_call x2, Pallas kernels, weight_grads(): pl.pallas_call(functools.partial(weight_kernel, order, first, acts_at), o...  3.98 us
    ppermute x3, waiting for transfers between devices, on_device(): lax.ppermute(total, 'node', [(i, (i + k) % nodes) for i in range(nodes)])  3.07 us
    ppermute x2, waiting for transfers between devices, swap_dp(): return lax.ppermute(value, 'dp', [(0, 1), (1, 0)])  2.45 us
  transfers between devices with their start and end apart: 12, of which 7 were waited for; matrix products, arithmetic and copies ran while one was open for 1% of the time, Pallas kernels for 25%

profile of v5, /device:TPU:0, one launch (start us, length us, event | category | flops | bytes accessed | tf_op | source)
XLA Modules:
  0.0 46.9 jit_solution(15853842999240939995)
XLA Ops:
  0.7 2.1 %share.1 = bf16[128,1792]{1,0:T(8,128)(2,1)} custom-call(bf16[64,4,3584]{2,1,0:T(4,128)(2,1)} %bitcast.13, bf16[64,4,3584]{2,1,0:T(4,128)(2,1)} %bitcast.16, f32[4,64]{1,0:T(4,128)} %bitcast.19, s32[1,4]{1,0:T(1,128)} %bitcast.22), custom_call_target="tpu_custom_call" | custom-call | tf_op jit(solution)/shard_map/share/pallas_call | solution.py:93
  2.7 3.0 %collective-permute-start = (bf16[128,1792]{1,0:T(8,128)(2,1)}, bf16[128,1792]{1,0:T(8,128)(2,1)S(1)}, u32[]{:S(2)}, u32[]{:S(2)}) collective-permute-start(bf16[128,1792]{1,0:T(8,128)(2,1)} %share.1), channel_id=1, source_target_pairs={{0,16},{16,0},{1,17},{17,1},{2,18},{18,2},{3,19},{19,3},{4,20},{20... | collective-permute-start | bytes 1376264 | tf_op jit(solution)/shard_map/ppermute | solution.py:320
  5.7 8.9 %forward.1 = (bf16[3,256,512]{2,1,0:T(8,128)(2,1)S(1)}, bf16[64,3584]{1,0:T(8,128)(2,1)S(1)}, bf16[64,3584]{1,0:T(8,128)(2,1)S(1)}, bf16[64,3584]{1,0:T(8,128)(2,1)S(1)}, bf16[64,3584]{1,0:T(8,128)(2,1)S(1)}) custom-call(bf16[64,4,3584]{2,1,0:T(4,128)(2,1)} %bitcast.14, bf16[64,4,3584]{2,1,0:T(4,128)(2,1)} %bitcast.17, f32[4,64]{1,0:T(4,128)S(1)} %bitcast.20, ...), custom_call_target="tpu_custom_call" | custom-call | flops 4697620480 | bytes 18000000 | tf_op jit(solution)/shard_map/forward/pallas_call | solution.py:192
  14.6 1.8 %collective-permute-done.refs_0_ = bf16[128,1792]{1,0:T(8,128)(2,1)S(1)} collective-permute-done((bf16[128,1792]{1,0:T(8,128)(2,1)}, bf16[128,1792]{1,0:T(8,128)(2,1)S(1)}, u32[]{:S(2)}, u32[]{:S(2)}) %collective-permute-start) | collective-permute-done | bytes 458784 | tf_op jit(solution)/shard_map/ppermute | solution.py:320
  16.5 1.7 %collective-permute-start.6 = (bf16[3,256,512]{2,1,0:T(8,128)(2,1)S(1)}, bf16[3,256,512]{2,1,0:T(8,128)(2,1)S(1)}, u32[]{:S(2)}, u32[]{:S(2)}) collective-permute-start(bf16[3,256,512]{2,1,0:T(8,128)(2,1)S(1)} %get-tuple-element.33.acts), channel_id=1, source_target_pairs={{0,16},{16,0},{1,17},{17,1},{2,18},{18,2},{3,19},{19,3},{4,20},{20... | collective-permute-start | bytes 2359304 | tf_op jit(solution)/shard_map/ppermute | solution.py:320
  18.2 0.2 collective-permute-start.2
  18.4 0.1 add_convert_fusion.3
  18.5 1.7 %collective-permute-start.3 = (bf16[32,3584]{1,0:T(8,128)(2,1)S(1)}, bf16[32,3584]{1,0:T(8,128)(2,1)S(1)}, u32[]{:S(2)}, u32[]{:S(2)}) collective-permute-start(bf16[32,3584]{1,0:T(8,128)(2,1)S(1)} %get-tuple-element.47), channel_id=1, source_target_pairs={{0,2},{1,3},{2,0},{3,1},{4,6},{5,7},{6,4},{7,5},{8,10},{9,11},{10,... | collective-permute-start | bytes 688136 | tf_op jit(solution)/shard_map/ppermute | solution.py:317
  20.2 0.1 add_convert_fusion
  20.3 1.4 %collective-permute-start.7 = (bf16[32,3584]{1,0:T(8,128)(2,1)S(1)}, bf16[32,3584]{1,0:T(8,128)(2,1)S(1)}, u32[]{:S(2)}, u32[]{:S(2)}) collective-permute-start(bf16[32,3584]{1,0:T(8,128)(2,1)S(1)} %get-tuple-element.44), channel_id=1, source_target_pairs={{0,2},{1,3},{2,0},{3,1},{4,6},{5,7},{6,4},{7,5},{8,10},{9,11},{10,... | collective-permute-start | bytes 688136 | tf_op jit(solution)/shard_map/ppermute | solution.py:317
  21.7 1.8 %own_grads.1 = (bf16[1792,512]{1,0:T(8,128)(2,1)S(1)}, bf16[1792,512]{1,0:T(8,128)(2,1)S(1)}, bf16[1792,512]{1,0:T(8,128)(2,1)S(1)}) custom-call(bf16[64,4,3584]{2,1,0:T(4,128)(2,1)S(1)} %bitcast.15, bf16[64,4,3584]{2,1,0:T(4,128)(2,1)S(1)} %bitcast.18, f32[4,64]{1,0:T(4,128)S(1)} %bitcast.21, s32[1,4]{1,0:T(1,128)S(1)} %bitcast.24, ...), custom_call_target="tpu_custom_call" | custom-call | flops 1409286144 | bytes 10000000 | tf_op jit(solution)/shard_map/own_grads/pallas_call | solution.py:229
  23.5 3.5 %collective-permute-done.3 = bf16[32,3584]{1,0:T(8,128)(2,1)S(1)} collective-permute-done((bf16[32,3584]{1,0:T(8,128)(2,1)S(1)}, bf16[32,3584]{1,0:T(8,128)(2,1)S(1)}, u32[]{:S(2)}, u32[]{:S(2)}) %collective-permute-start.3) | collective-permute-done | bytes 229408 | tf_op jit(solution)/shard_map/ppermute | solution.py:317
  27.0 1.6 %collective-permute-start.9 = (bf16[128,1792]{1,0:T(8,128)(2,1)S(1)}, bf16[128,1792]{1,0:T(8,128)(2,1)S(1)}, u32[]{:S(2)}, u32[]{:S(2)}) collective-permute-start(bf16[128,1792]{1,0:T(8,128)(2,1)S(1)} %collective-permute-done.refs_0_), channel_id=1, source_target_pairs={{0,2},{1,3},{2,0},{3,1},{4,6},{5,7},{6,4},{7,5},{8,10},{9,11},{10,... | collective-permute-start | bytes 1376264 | tf_op jit(solution)/shard_map/ppermute | solution.py:317
  28.7 1.6 %collective-permute-start.5 = (bf16[16,3584]{1,0:T(8,128)(2,1)S(1)}, bf16[16,3584]{1,0:T(8,128)(2,1)S(1)}, u32[]{:S(2)}, u32[]{:S(2)}) collective-permute-start(bf16[16,3584]{1,0:T(8,128)(2,1)S(1)} %get-tuple-element.48), channel_id=1, source_target_pairs={{0,4},{4,8},{8,12},{12,0},{1,5},{5,9},{9,13},{13,1},{2,6},{6,10},{... | collective-permute-start | bytes 344072 | tf_op jit(solution)/shard_map/ppermute | solution.py:347
  30.3 2.6 %collective-permute-start.4 = (bf16[16,3584]{1,0:T(8,128)(2,1)S(1)}, bf16[16,3584]{1,0:T(8,128)(2,1)S(1)}, u32[]{:S(2)}, u32[]{:S(2)}) collective-permute-start(bf16[16,3584]{1,0:T(8,128)(2,1)S(1)} %get-tuple-element.49), channel_id=1, source_target_pairs={{0,8},{4,12},{8,0},{12,4},{1,9},{5,13},{9,1},{13,5},{2,10},{6,14},... | collective-permute-start | bytes 344072 | tf_op jit(solution)/shard_map/ppermute | solution.py:347
  33.0 2.8 %collective-permute-start.8 = (bf16[16,3584]{1,0:T(8,128)(2,1)S(1)}, bf16[16,3584]{1,0:T(8,128)(2,1)S(1)}, u32[]{:S(2)}, u32[]{:S(2)}) collective-permute-start(bf16[16,3584]{1,0:T(8,128)(2,1)S(1)} %add_convert_fusion.4), channel_id=1, source_target_pairs={{0,12},{4,0},{8,4},{12,8},{1,13},{5,1},{9,5},{13,9},{2,14},{6,2},{... | collective-permute-start | bytes 344072 | tf_op jit(solution)/shard_map/ppermute | solution.py:347
  35.8 0.6 %collective-permute-done.6.refs_4_ = bf16[3,256,512]{2,1,0:T(8,128)(2,1)S(1)} collective-permute-done((bf16[3,256,512]{2,1,0:T(8,128)(2,1)S(1)}, bf16[3,256,512]{2,1,0:T(8,128)(2,1)S(1)}, u32[]{:S(2)}, u32[]{:S(2)}) %collective-permute-start.6) | collective-permute-done | bytes 786464 | tf_op jit(solution)/shard_map/ppermute | solution.py:320
  36.4 2.7 %collective-permute-done.4.refs_1_ = bf16[16,3584]{1,0:T(8,128)(2,1)S(1)} collective-permute-done((bf16[16,3584]{1,0:T(8,128)(2,1)S(1)}, bf16[16,3584]{1,0:T(8,128)(2,1)S(1)}, u32[]{:S(2)}, u32[]{:S(2)}) %collective-permute-start.4) | collective-permute-done | bytes 114720 | tf_op jit(solution)/shard_map/ppermute | solution.py:347
  39.1 0.4 collective-permute-done.8.refs_2_
  39.5 1.0 %collect.1 = bf16[16,4,3584]{2,1,0:T(4,128)(2,1)} custom-call(bf16[16,3584]{1,0:T(8,128)(2,1)S(1)} %collective-permute-done.5.refs_0_, bf16[16,3584]{1,0:T(8,128)(2,1)S(1)} %collective-permute-done.4.refs_1_, bf16[16,3584]{1,0:T(8,128)(2,1)S(1)} %collective-permute-done.8.refs_2_, bf16[16,3584]{1,0:T(8,128)(2,1)S(1)} %slice.72.refs_3_, ...), custom_call_target="tpu_custom_call" | custom-call | tf_op jit(solution)/shard_map/collect/pallas_call | solution.py:353
  40.5 0.6 %collective-permute-done.9.refs_1_ = bf16[128,1792]{1,0:T(8,128)(2,1)S(1)} collective-permute-done((bf16[128,1792]{1,0:T(8,128)(2,1)S(1)}, bf16[128,1792]{1,0:T(8,128)(2,1)S(1)}, u32[]{:S(2)}, u32[]{:S(2)}) %collective-permute-start.9) | collective-permute-done | bytes 458784 | tf_op jit(solution)/shard_map/ppermute | solution.py:317
  41.1 1.8 %collective-permute-done.11.refs_3_ = bf16[128,1792]{1,0:T(8,128)(2,1)S(1)} collective-permute-done((bf16[128,1792]{1,0:T(8,128)(2,1)S(1)}, bf16[128,1792]{1,0:T(8,128)(2,1)S(1)}, u32[]{:S(2)}, u32[]{:S(2)}) %collective-permute-start.11) | collective-permute-done | bytes 458784 | tf_op jit(solution)/shard_map/ppermute | solution.py:317
  43.0 1.7 %weight_grads.3 = bf16[1792,512]{1,0:T(8,128)(2,1)} custom-call(bf16[128,1792]{1,0:T(8,128)(2,1)S(1)} %collective-permute-done.refs_0_, bf16[128,1792]{1,0:T(8,128)(2,1)S(1)} %collective-permute-done.9.refs_1_, bf16[128,1792]{1,0:T(8,128)(2,1)S(1)} %collective-permute-done.10.refs_2_, bf16[128,1792]{1,0:T(8,128)(2,1)S(1)} %collective-permute-done.11.refs_3_, ...), custom_call_target="tpu_custom_call" | custom-call | flops 469762048 | bytes 4000000 | tf_op jit(solution)/shard_map/weight_grads/pallas_call | solution.py:273
  44.6 2.3 %weight_grads.2 = (bf16[1792,512]{1,0:T(8,128)(2,1)}, bf16[1792,512]{1,0:T(8,128)(2,1)}) custom-call(bf16[128,1792]{1,0:T(8,128)(2,1)S(1)} %collective-permute-done.refs_0_, bf16[128,1792]{1,0:T(8,128)(2,1)S(1)} %collective-permute-done.9.refs_1_, bf16[128,1792]{1,0:T(8,128)(2,1)S(1)} %collective-permute-done.10.refs_2_, ...), custom_call_target="tpu_custom_call" | custom-call | flops 939524096 | bytes 4000000 | tf_op jit(solution)/shard_map/weight_grads/pallas_call | solution.py:273
  (20 shorter events, 0.1 us)
Async XLA Ops:
  0.6 5.1 %copy-start.2 = (f32[1,1,64,4]{2,3,1,0:T(4,128)S(1)}, f32[1,1,64,4]{2,3,1,0:T(4,128)}, u32[]{:S(2)}) copy-start(f32[1,1,64,4]{2,3,1,0:T(4,128)} %param.9) | copy-start | bytes 3076
  0.6 5.1 %copy-start.3 = (s32[1,1,4]{2,1,0:T(1,128)S(1)}, s32[1,1,4]{2,1,0:T(1,128)}, u32[]{:S(2)}) copy-start(s32[1,1,4]{2,1,0:T(1,128)} %param.10) | copy-start | bytes 52
  2.7 13.7 %collective-permute-start = (bf16[128,1792]{1,0:T(8,128)(2,1)}, bf16[128,1792]{1,0:T(8,128)(2,1)S(1)}, u32[]{:S(2)}, u32[]{:S(2)}) collective-permute-start(bf16[128,1792]{1,0:T(8,128)(2,1)} %share.1), channel_id=1, source_target_pairs={{0,16},{16,0},{1,17},{17,1},{2,18},{18,2},{3,19},{19,3},{4,20},{20... | collective-permute-start | bytes 1376264 | tf_op jit(solution)/shard_map/ppermute | solution.py:320
  5.7 16.0 %copy-start.1 = (bf16[1,1,64,4,3584]{4,3,2,1,0:T(4,128)(2,1)S(1)}, bf16[1,1,64,4,3584]{4,3,2,1,0:T(4,128)(2,1)}, u32[]{:S(2)}) copy-start(bf16[1,1,64,4,3584]{4,3,2,1,0:T(4,128)(2,1)} %param.8) | copy-start | bytes 5505028
  14.6 7.1 %copy-start = (bf16[1,1,64,4,3584]{4,3,2,1,0:T(4,128)(2,1)S(1)}, bf16[1,1,64,4,3584]{4,3,2,1,0:T(4,128)(2,1)}, u32[]{:S(2)}) copy-start(bf16[1,1,64,4,3584]{4,3,2,1,0:T(4,128)(2,1)} %param.7) | copy-start | bytes 5505028
  16.5 2.0 %collective-permute-start.1 = (bf16[64,3584]{1,0:T(8,128)(2,1)S(1)}, bf16[64,3584]{1,0:T(8,128)(2,1)S(1)}, u32[]{:S(2)}, u32[]{:S(2)}) collective-permute-start(bf16[64,3584]{1,0:T(8,128)(2,1)S(1)} %get-tuple-element.28), channel_id=1, source_target_pairs={{0,1},{1,0},{2,3},{3,2},{4,5},{5,4},{6,7},{7,6},{8,9},{9,8},{10,11... | collective-permute-start | bytes 1376264 | tf_op jit(solution)/shard_map/ppermute | solution.py:317
  16.5 20.0 %collective-permute-start.6 = (bf16[3,256,512]{2,1,0:T(8,128)(2,1)S(1)}, bf16[3,256,512]{2,1,0:T(8,128)(2,1)S(1)}, u32[]{:S(2)}, u32[]{:S(2)}) collective-permute-start(bf16[3,256,512]{2,1,0:T(8,128)(2,1)S(1)} %get-tuple-element.33.acts), channel_id=1, source_target_pairs={{0,16},{16,0},{1,17},{17,1},{2,18},{18,2},{3,19},{19,3},{4,20},{20... | collective-permute-start | bytes 2359304 | tf_op jit(solution)/shard_map/ppermute | solution.py:320
  18.2 2.0 %collective-permute-start.2 = (bf16[64,3584]{1,0:T(8,128)(2,1)S(1)}, bf16[64,3584]{1,0:T(8,128)(2,1)S(1)}, u32[]{:S(2)}, u32[]{:S(2)}) collective-permute-start(bf16[64,3584]{1,0:T(8,128)(2,1)S(1)} %get-tuple-element.32), channel_id=1, source_target_pairs={{0,1},{1,0},{2,3},{3,2},{4,5},{5,4},{6,7},{7,6},{8,9},{9,8},{10,11... | collective-permute-start | bytes 1376264 | tf_op jit(solution)/shard_map/ppermute | solution.py:317
  18.5 8.5 %collective-permute-start.3 = (bf16[32,3584]{1,0:T(8,128)(2,1)S(1)}, bf16[32,3584]{1,0:T(8,128)(2,1)S(1)}, u32[]{:S(2)}, u32[]{:S(2)}) collective-permute-start(bf16[32,3584]{1,0:T(8,128)(2,1)S(1)} %get-tuple-element.47), channel_id=1, source_target_pairs={{0,2},{1,3},{2,0},{3,1},{4,6},{5,7},{6,4},{7,5},{8,10},{9,11},{10,... | collective-permute-start | bytes 688136 | tf_op jit(solution)/shard_map/ppermute | solution.py:317
  20.3 12.6 %collective-permute-start.7 = (bf16[32,3584]{1,0:T(8,128)(2,1)S(1)}, bf16[32,3584]{1,0:T(8,128)(2,1)S(1)}, u32[]{:S(2)}, u32[]{:S(2)}) collective-permute-start(bf16[32,3584]{1,0:T(8,128)(2,1)S(1)} %get-tuple-element.44), channel_id=1, source_target_pairs={{0,2},{1,3},{2,0},{3,1},{4,6},{5,7},{6,4},{7,5},{8,10},{9,11},{10,... | collective-permute-start | bytes 688136 | tf_op jit(solution)/shard_map/ppermute | solution.py:317
  27.0 14.1 %collective-permute-start.9 = (bf16[128,1792]{1,0:T(8,128)(2,1)S(1)}, bf16[128,1792]{1,0:T(8,128)(2,1)S(1)}, u32[]{:S(2)}, u32[]{:S(2)}) collective-permute-start(bf16[128,1792]{1,0:T(8,128)(2,1)S(1)} %collective-permute-done.refs_0_), channel_id=1, source_target_pairs={{0,2},{1,3},{2,0},{3,1},{4,6},{5,7},{6,4},{7,5},{8,10},{9,11},{10,... | collective-permute-start | bytes 1376264 | tf_op jit(solution)/shard_map/ppermute | solution.py:317
  28.7 7.7 %collective-permute-start.5 = (bf16[16,3584]{1,0:T(8,128)(2,1)S(1)}, bf16[16,3584]{1,0:T(8,128)(2,1)S(1)}, u32[]{:S(2)}, u32[]{:S(2)}) collective-permute-start(bf16[16,3584]{1,0:T(8,128)(2,1)S(1)} %get-tuple-element.48), channel_id=1, source_target_pairs={{0,4},{4,8},{8,12},{12,0},{1,5},{5,9},{9,13},{13,1},{2,6},{6,10},{... | collective-permute-start | bytes 344072 | tf_op jit(solution)/shard_map/ppermute | solution.py:347
  30.3 8.8 %collective-permute-start.4 = (bf16[16,3584]{1,0:T(8,128)(2,1)S(1)}, bf16[16,3584]{1,0:T(8,128)(2,1)S(1)}, u32[]{:S(2)}, u32[]{:S(2)}) collective-permute-start(bf16[16,3584]{1,0:T(8,128)(2,1)S(1)} %get-tuple-element.49), channel_id=1, source_target_pairs={{0,8},{4,12},{8,0},{12,4},{1,9},{5,13},{9,1},{13,5},{2,10},{6,14},... | collective-permute-start | bytes 344072 | tf_op jit(solution)/shard_map/ppermute | solution.py:347
  33.0 6.5 %collective-permute-start.8 = (bf16[16,3584]{1,0:T(8,128)(2,1)S(1)}, bf16[16,3584]{1,0:T(8,128)(2,1)S(1)}, u32[]{:S(2)}, u32[]{:S(2)}) collective-permute-start(bf16[16,3584]{1,0:T(8,128)(2,1)S(1)} %add_convert_fusion.4), channel_id=1, source_target_pairs={{0,12},{4,0},{8,4},{12,8},{1,13},{5,1},{9,5},{13,9},{2,14},{6,2},{... | collective-permute-start | bytes 344072 | tf_op jit(solution)/shard_map/ppermute | solution.py:347
  36.4 4.7 %collective-permute-start.10 = (bf16[128,1792]{1,0:T(8,128)(2,1)S(1)}, bf16[128,1792]{1,0:T(8,128)(2,1)S(1)}, u32[]{:S(2)}, u32[]{:S(2)}) collective-permute-start(bf16[128,1792]{1,0:T(8,128)(2,1)S(1)} %collective-permute-done.refs_0_), channel_id=1, source_target_pairs={{0,1},{1,0},{2,3},{3,2},{4,5},{5,4},{6,7},{7,6},{8,9},{9,8},{10,11... | collective-permute-start | bytes 1376264 | tf_op jit(solution)/shard_map/ppermute | solution.py:317
  41.1 1.8 %collective-permute-start.11 = (bf16[128,1792]{1,0:T(8,128)(2,1)S(1)}, bf16[128,1792]{1,0:T(8,128)(2,1)S(1)}, u32[]{:S(2)}, u32[]{:S(2)}) collective-permute-start(bf16[128,1792]{1,0:T(8,128)(2,1)S(1)} %collective-permute-done.9.refs_1_), channel_id=1, source_target_pairs={{0,1},{1,0},{2,3},{3,2},{4,5},{5,4},{6,7},{7,6},{8,9},{9,8},{10,11... | collective-permute-start | bytes 1376264 | tf_op jit(solution)/shard_map/ppermute | solution.py:317

commit v6 on v5

--- a/solution.py
+++ b/solution.py
@@ -104,7 +104,7 @@
 
 
 def forward_kernel(locals_, chunk, tok_hbm, grad_hbm, weights_hbm, counts_hbm, wg_hbm, wu_hbm, wd_hbm,
-                   acts, own_a, own_b, send_a, send_b,
+                   acts, own_a, own_b, send_a_low, send_a_high, send_b_low, send_b_high,
                    tok, grad, weights, counts, wgu, wd, acc, acc_h, moved, sem):
     slots, nodes, width = tok.shape
     rows = slots * nodes
@@ -175,12 +175,13 @@
     one_hot = jnp.where(index == lax.broadcasted_iota(jnp.int32, (rows, rows), 1), 1.0, 0.0).astype(BF16)
     moved[:, :hid_local] = dot(one_hot, acts[0], 1, 0).astype(BF16)
     moved[:, hid_local:] = dot(one_hot, acts[1], 1, 0).astype(BF16)
-    quarter = rows // 4
     for i in range(steps):
         cols = pl.ds(i * chunk, chunk)
         total = dot(moved[...], wgu[cols], 1, 1).astype(BF16)
-        for n, out in enumerate((own_a, own_b, send_a, send_b)):
-            out[:, cols] = total[n * quarter:(n + 1) * quarter]
+        at = 0
+        for out in (own_a, own_b, send_a_low, send_a_high, send_b_low, send_b_high):
+            out[:, cols] = total[at:at + out.shape[0]]
+            at += out.shape[0]
 
 
 def forward(locals_, tokens, grads, weights, counts, gate_weight, up_weight, down_weight):
@@ -191,9 +192,10 @@
     chunk = 512
     return pl.pallas_call(
         functools.partial(forward_kernel, locals_, chunk),
-        out_shape=[jax.ShapeDtypeStruct((3, rows, hid_local), BF16)] + [jax.ShapeDtypeStruct((rows // 4, width), BF16)] * 4,
+        out_shape=[jax.ShapeDtypeStruct((3, rows, hid_local), BF16)] + [jax.ShapeDtypeStruct((rows // 4, width), BF16)] * 2
+        + [jax.ShapeDtypeStruct((rows // 8, width), BF16)] * 4,
         in_specs=[hbm] * 7,
-        out_specs=[vmem] * 5,
+        out_specs=[vmem] * 7,
         scratch_shapes=[
             pltpu.VMEM(tokens.shape, BF16), pltpu.VMEM(tokens.shape, BF16), pltpu.VMEM(weights.shape, F32),
             pltpu.VMEM(counts.shape, jnp.int32), pltpu.VMEM((width, 2 * hid_local), BF16), pltpu.VMEM((width, hid_local), BF16),
@@ -237,45 +239,42 @@
     )(tokens, grads, weights, counts, acts)
 
 
-def weight_kernel(order, first, acts_at, *refs):
-    count = len(acts_at)
+def weight_kernel(order, *refs):
     shares = refs[:len(order)]
-    there_ref = refs[len(order)]
-    parts = refs[len(order) + 1:len(order) + 1 + count]
-    outs = refs[len(order) + 1 + count:len(order) + 1 + 2 * count]
-    left, right, bufs, sem = refs[len(order) + 1 + 2 * count:]
+    there_ref, *parts = refs[len(order):len(order) + 4]
+    outs = refs[len(order) + 4:len(order) + 7]
+    left, right, bufs, sem = refs[len(order) + 7:]
     part = outs[0].shape[0]
     me = lax.axis_index("local")
     block = shares[0].shape[0] // 2
-    for n, a in enumerate(acts_at):
-        for b, d in enumerate(order):
-            right[n, b * block:(b + 1) * block] = there_ref[a, pl.ds(pl.multiple_of((me ^ d) * block, block), block)]
-    chunk = left.shape[1]
+    for b, d in enumerate(order):
+        right[:, b * block:(b + 1) * block] = there_ref[:, pl.ds(pl.multiple_of((me ^ d) * block, block), block)]
+    chunk = left.shape[2]
     copies = []
     for i in range(part // chunk):
         cols = pl.ds(i * chunk, chunk)
         for b, ref in enumerate(shares):
-            left[b * block:(b + 1) * block] = ref[first:first + block, cols]
+            left[0, b * block:(b + 1) * block] = ref[block:, cols]
+            left[1, b * block:(b + 1) * block] = ref[:block, cols]
         for n, out in enumerate(outs):
-            bufs[n, cols] = (dot(left[...], right[n], 0, 0) + parts[n][cols].astype(F32)).astype(BF16)
+            bufs[n, cols] = (dot(left[n // 2], right[n], 0, 0) + parts[n][cols].astype(F32)).astype(BF16)
             copies.append(pltpu.make_async_copy(bufs.at[n, cols], out.at[cols], sem.at[i, n]))
             copies[-1].start()
     for copy in copies:
         copy.wait()
 
 
-def weight_grads(order, shares, first, there, parts, acts_at):
+def weight_grads(order, shares, there, parts):
     part = shares[0].shape[-1]
-    rows, hid_local = there.shape[1:]
-    count = len(acts_at)
+    count, rows, hid_local = there.shape
     chunk = 896
     vmem = pl.BlockSpec(memory_space=pltpu.VMEM)
     return pl.pallas_call(
-        functools.partial(weight_kernel, order, first, acts_at),
+        functools.partial(weight_kernel, order),
         out_shape=[jax.ShapeDtypeStruct((part, hid_local), BF16)] * count,
         in_specs=[vmem] * (1 + len(shares) + count),
         out_specs=[pl.BlockSpec(memory_space=pltpu.HBM)] * count,
-        scratch_shapes=[pltpu.VMEM((rows, chunk), BF16), pltpu.VMEM((count, rows, hid_local), BF16),
+        scratch_shapes=[pltpu.VMEM((2, rows, chunk), BF16), pltpu.VMEM((count, rows, hid_local), BF16),
                         pltpu.VMEM((count, part, hid_local), BF16), pltpu.SemaphoreType.DMA((part // chunk, count))],
         compiler_params=pltpu.CompilerParams(vmem_limit_bytes=VMEM_LIMIT),
         cost_estimate=pl.CostEstimate(flops=2 * rows * part * hid_local * count, bytes_accessed=4_000_000, transcendentals=0),
@@ -323,22 +322,27 @@
     block = rows // locals_
     first, weights = lax.optimization_barrier((share(order, tokens, grads, weights, counts), weights))
     first = swap_dp(first)
-    acts, own_a, own_b, send_a, send_b = forward(locals_, tokens, grads, weights, counts, w_gate[0], w_up[0], w_down[0])
+    acts, own_a, own_b, *send = forward(locals_, tokens, grads, weights, counts, w_gate[0], w_up[0], w_down[0])
     there = swap_dp(acts)
 
     per = nodes // 2
     hops = shift_order(nodes)
     arrived = [None] * nodes
-    send_a, send_b = after(send_a, first), after(send_b, first)
-    held = [(own_a, swap_local(send_a, bits[0])), (own_b, swap_local(send_b, bits[0]))]
-    for bit in bits[1:]:
+    low_a, high_a, low_b, high_b = send
+    came = [swap_local(v, bits[0]) for v in (high_a, high_b, low_a, low_b)]
+    came[0] = after(came[0], first)
+    held = []
+    for own, high, low in ((own_a, came[0], came[2]), (own_b, came[1], came[3])):
+        half = own.shape[0] // 2
+        held.append((add(own[:half], low), swap_local(add(own[half:], high), bits[1])))
+    for bit in bits[2:]:
         for g, (mine, other) in enumerate(held):
             half = mine.shape[0] // 2
             held[g] = (add(mine[:half], other[:half]), swap_local(add(mine[half:], other[half:]), bit))
     shares = [after(first, held[0][1])]
     for bit in reversed(bits[1:]):
         shares = shares + [swap_local(v, bit) for v in shares]
-    parts = own_grads(tokens, grads, weights, counts, after(acts, held[1][0]))
+    parts = own_grads(tokens, grads, weights, counts, after(acts, held[0][0]))
     held[0] = (after(held[0][0], parts[0]), held[0][1])
     for n, k in enumerate(hops):
         mine, other = (v[n % per * keep:(n % per + 1) * keep] for v in held[n // per])
@@ -361,8 +365,7 @@
 
     shares[-1] = after(shares[-1], d_tokens)
     shares = shares + [swap_local(v, bits[0]) for v in shares]
-    grad_gate, grad_up = weight_grads(order, shares, block, there, parts[:2], (0, 1))
-    (grad_down,) = weight_grads(order, shares, 0, there, parts[2:], (2,))
+    grad_gate, grad_up, grad_down = weight_grads(order, shares, there, parts)
     return d_tokens[None, None], grad_gate[None], grad_up[None], grad_down[None]
 
 

time: 47.1 us -> 44.1 us (0.936)
  starting transfers between devices: 16.6 us -> 15 us
  Pallas kernels: 17.8 us -> 16.7 us
    ppermute x2, starting transfers between devices: 4.74 us -> 3.05 us  [swap_dp(): return lax.ppermute(value, 'dp', [(0, 1), (1, 0)])]
    ppermute x7 -> x9, waiting for transfers between devices: 5.96 us -> 7.38 us  [swap_local(): return lax.ppermute(value, 'local', [(i, i ^ bit) for i in range(locals_)])]
    ppermute x3, waiting for transfers between devices: 3.07 us -> 1.75 us  [on_device(): lax.ppermute(total, 'node', [(i, (i + k) % nodes) for i in range(nodes)])]
    pallas_call x2 -> x1, Pallas kernels: 3.98 us -> 2.94 us  [weight_grads(): pl.pallas_call(functools.partial(weight_kernel, order), out_shape=[jax.Sh...]
    ppermute x2, waiting for transfers between devices: 2.45 us -> 1.96 us  [swap_dp(): return lax.ppermute(value, 'dp', [(0, 1), (1, 0)])]
    ppermute x7 -> x9, starting transfers between devices: 4.91 us -> 5.01 us  [swap_local(): return lax.ppermute(value, 'local', [(i, i ^ bit) for i in range(locals_)])]
  transfers between devices with their start and end apart: 12 -> 14, of which waited for: 7 -> 8; matrix products, arithmetic and copies ran while one was open for 1% -> 1% of each run, Pallas kernels for 25% -> 27%
where the time goes in v6:
time: 44.1 us; the launch traced here: 43.9 us
  Pallas kernels  16.7 us (38%)
  starting transfers between devices  15 us (34%)
  waiting for transfers between devices  11.1 us (25%)
  between operations  0.73 us (2%)
    pallas_call x1, Pallas kernels, forward(): pl.pallas_call(functools.partial(forward_kernel, locals_, chunk), out_sha...  8.9 us
    ppermute x9, waiting for transfers between devices, swap_local(): return lax.ppermute(value, 'local', [(i, i ^ bit) for i in range(locals_)])  7.38 us
    ppermute x3, starting transfers between devices, on_device(): lax.ppermute(total, 'node', [(i, (i + k) % nodes) for i in range(nodes)])  6.97 us
    ppermute x9, starting transfers between devices, swap_local(): return lax.ppermute(value, 'local', [(i, i ^ bit) for i in range(locals_)])  5.01 us
    ppermute x2, starting transfers between devices, swap_dp(): return lax.ppermute(value, 'dp', [(0, 1), (1, 0)])  3.05 us
    pallas_call x1, Pallas kernels, weight_grads(): pl.pallas_call(functools.partial(weight_kernel, order), out_shape=[jax.Sh...  2.94 us
    pallas_call x1, Pallas kernels, share(): pl.pallas_call(functools.partial(share_kernel, blocks), out_shape=jax.Sha...  2.06 us
    ppermute x2, waiting for transfers between devices, swap_dp(): return lax.ppermute(value, 'dp', [(0, 1), (1, 0)])  1.96 us
  transfers between devices with their start and end apart: 14, of which 8 were waited for; matrix products, arithmetic and copies ran while one was open for 1% of the time, Pallas kernels for 27%

profile of v6, /device:TPU:0, one launch (start us, length us, event | category | flops | bytes accessed | tf_op | source)
XLA Modules:
  0.0 43.9 jit_solution(9053963903463599556)
XLA Ops:
  0.7 2.1 %share.1 = bf16[128,1792]{1,0:T(8,128)(2,1)} custom-call(bf16[64,4,3584]{2,1,0:T(4,128)(2,1)} %bitcast.13, bf16[64,4,3584]{2,1,0:T(4,128)(2,1)} %bitcast.16, f32[4,64]{1,0:T(4,128)} %bitcast.19, s32[1,4]{1,0:T(1,128)} %bitcast.22), custom_call_target="tpu_custom_call" | custom-call | tf_op jit(solution)/shard_map/share/pallas_call | solution.py:93
  2.7 3.0 %collective-permute-start.2 = (bf16[128,1792]{1,0:T(8,128)(2,1)}, bf16[128,1792]{1,0:T(8,128)(2,1)S(1)}, u32[]{:S(2)}, u32[]{:S(2)}) collective-permute-start(bf16[128,1792]{1,0:T(8,128)(2,1)} %share.1), channel_id=1, source_target_pairs={{0,16},{16,0},{1,17},{17,1},{2,18},{18,2},{3,19},{19,3},{4,20},{20... | collective-permute-start | bytes 1376264 | tf_op jit(solution)/shard_map/ppermute | solution.py:319
  5.7 8.9 %forward.1 = (bf16[3,256,512]{2,1,0:T(8,128)(2,1)S(1)}, bf16[64,3584]{1,0:T(8,128)(2,1)S(1)}, bf16[64,3584]{1,0:T(8,128)(2,1)S(1)}, bf16[32,3584]{1,0:T(8,128)(2...) custom-call(bf16[64,4,3584]{2,1,0:T(4,128)(2,1)} %bitcast.14, ...), custom_call_target="tpu_custom_call" | custom-call | flops 4697620480 | bytes 18000000 | tf_op jit(solution)/shard_map/forward/pallas_call | solution.py:193
  14.7 0.5 %collective-permute-start = (bf16[32,3584]{1,0:T(8,128)(2,1)S(1)}, bf16[32,3584]{1,0:T(8,128)(2,1)S(1)}, u32[]{:S(2)}, u32[]{:S(2)}) collective-permute-start(bf16[32,3584]{1,0:T(8,128)(2,1)S(1)} %get-tuple-element.28), channel_id=1, source_target_pairs={{0,1},{1,0},{2,3},{3,2},{4,5},{5,4},{6,7},{7,6},{8,9},{9,8},{10,11... | collective-permute-start | bytes 688136 | tf_op jit(solution)/shard_map/ppermute | solution.py:316
  15.2 0.1 collective-permute-start.7
  15.3 0.4 collective-permute-start.8
  15.7 0.5 %collective-permute-done.1 = bf16[32,3584]{1,0:T(8,128)(2,1)S(1)} collective-permute-done((bf16[32,3584]{1,0:T(8,128)(2,1)S(1)}, bf16[32,3584]{1,0:T(8,128)(2,1)S(1)}, u32[]{:S(2)}, u32[]{:S(2)}) %collective-permute-start.1) | collective-permute-done | bytes 229408 | tf_op jit(solution)/shard_map/ppermute | solution.py:316
  16.2 0.2 collective-permute-done.2.refs_0_
  16.5 0.1 add_convert_fusion.3
  16.6 1.8 %collective-permute-start.3 = (bf16[32,3584]{1,0:T(8,128)(2,1)S(1)}, bf16[32,3584]{1,0:T(8,128)(2,1)S(1)}, u32[]{:S(2)}, u32[]{:S(2)}) collective-permute-start(bf16[32,3584]{1,0:T(8,128)(2,1)S(1)} %get-tuple-element.53), channel_id=1, source_target_pairs={{0,2},{1,3},{2,0},{3,1},{4,6},{5,7},{6,4},{7,5},{8,10},{9,11},{10,... | collective-permute-start | bytes 688136 | tf_op jit(solution)/shard_map/ppermute | solution.py:316
  18.5 0.1 add_convert_fusion.1
  18.6 0.4 collective-permute-start.9
  18.9 1.8 %own_grads.1 = (bf16[1792,512]{1,0:T(8,128)(2,1)S(1)}, bf16[1792,512]{1,0:T(8,128)(2,1)S(1)}, bf16[1792,512]{1,0:T(8,128)(2,1)S(1)}) custom-call(bf16[64,4,3584]{2,1,0:T(4,128)(2,1)S(1)} %bitcast.15, bf16[64,4,3584]{2,1,0:T(4,128)(2,1)S(1)} %bitcast.18, f32[4,64]{1,0:T(4,128)S(1)} %bitcast.21, s32[1,4]{1,0:T(1,128)S(1)} %bitcast.24, ...), custom_call_target="tpu_custom_call" | custom-call | flops 1409286144 | bytes 10000000 | tf_op jit(solution)/shard_map/own_grads/pallas_call | solution.py:231
  20.7 4.4 %collective-permute-done.3 = bf16[32,3584]{1,0:T(8,128)(2,1)S(1)} collective-permute-done((bf16[32,3584]{1,0:T(8,128)(2,1)S(1)}, bf16[32,3584]{1,0:T(8,128)(2,1)S(1)}, u32[]{:S(2)}, u32[]{:S(2)}) %collective-permute-start.3) | collective-permute-done | bytes 229408 | tf_op jit(solution)/shard_map/ppermute | solution.py:316
  25.2 1.8 %collective-permute-start.11 = (bf16[128,1792]{1,0:T(8,128)(2,1)S(1)}, bf16[128,1792]{1,0:T(8,128)(2,1)S(1)}, u32[]{:S(2)}, u32[]{:S(2)}) collective-permute-start(bf16[128,1792]{1,0:T(8,128)(2,1)S(1)} %collective-permute-done.2.refs_0_), channel_id=1, source_target_pairs={{0,2},{1,3},{2,0},{3,1},{4,6},{5,7},{6,4},{7,5},{8,10},{9,11},{10,... | collective-permute-start | bytes 1376264 | tf_op jit(solution)/shard_map/ppermute | solution.py:316
  27.0 1.6 %collective-permute-start.5 = (bf16[16,3584]{1,0:T(8,128)(2,1)S(1)}, bf16[16,3584]{1,0:T(8,128)(2,1)S(1)}, u32[]{:S(2)}, u32[]{:S(2)}) collective-permute-start(bf16[16,3584]{1,0:T(8,128)(2,1)S(1)} %get-tuple-element.50), channel_id=1, source_target_pairs={{0,4},{4,8},{8,12},{12,0},{1,5},{5,9},{9,13},{13,1},{2,6},{6,10},{... | collective-permute-start | bytes 344072 | tf_op jit(solution)/shard_map/ppermute | solution.py:351
  28.6 2.6 %collective-permute-start.4 = (bf16[16,3584]{1,0:T(8,128)(2,1)S(1)}, bf16[16,3584]{1,0:T(8,128)(2,1)S(1)}, u32[]{:S(2)}, u32[]{:S(2)}) collective-permute-start(bf16[16,3584]{1,0:T(8,128)(2,1)S(1)} %get-tuple-element.51), channel_id=1, source_target_pairs={{0,8},{4,12},{8,0},{12,4},{1,9},{5,13},{9,1},{13,5},{2,10},{6,14},... | collective-permute-start | bytes 344072 | tf_op jit(solution)/shard_map/ppermute | solution.py:351
  31.3 2.8 %collective-permute-start.10 = (bf16[16,3584]{1,0:T(8,128)(2,1)S(1)}, bf16[16,3584]{1,0:T(8,128)(2,1)S(1)}, u32[]{:S(2)}, u32[]{:S(2)}) collective-permute-start(bf16[16,3584]{1,0:T(8,128)(2,1)S(1)} %add_convert_fusion.4), channel_id=1, source_target_pairs={{0,12},{4,0},{8,4},{12,8},{1,13},{5,1},{9,5},{13,9},{2,14},{6,2},{... | collective-permute-start | bytes 344072 | tf_op jit(solution)/shard_map/ppermute | solution.py:351
  34.0 1.7 %collective-permute-done.6.refs_4_ = bf16[3,256,512]{2,1,0:T(8,128)(2,1)S(1)} collective-permute-done((bf16[3,256,512]{2,1,0:T(8,128)(2,1)S(1)}, bf16[3,256,512]{2,1,0:T(8,128)(2,1)S(1)}, u32[]{:S(2)}, u32[]{:S(2)}) %collective-permute-start.6) | collective-permute-done | bytes 786464 | tf_op jit(solution)/shard_map/ppermute | solution.py:319
  35.8 1.7 %collective-permute-done.4.refs_1_ = bf16[16,3584]{1,0:T(8,128)(2,1)S(1)} collective-permute-done((bf16[16,3584]{1,0:T(8,128)(2,1)S(1)}, bf16[16,3584]{1,0:T(8,128)(2,1)S(1)}, u32[]{:S(2)}, u32[]{:S(2)}) %collective-permute-start.4) | collective-permute-done | bytes 114720 | tf_op jit(solution)/shard_map/ppermute | solution.py:351
  37.5 1.0 %collect.1 = bf16[16,4,3584]{2,1,0:T(4,128)(2,1)} custom-call(bf16[16,3584]{1,0:T(8,128)(2,1)S(1)} %collective-permute-done.5.refs_0_, bf16[16,3584]{1,0:T(8,128)(2,1)S(1)} %collective-permute-done.4.refs_1_, bf16[16,3584]{1,0:T(8,128)(2,1)S(1)} %collective-permute-done.10.refs_2_, bf16[16,3584]{1,0:T(8,128)(2,1)S(1)} %slice.52.refs_3_, ...), custom_call_target="tpu_custom_call" | custom-call | tf_op jit(solution)/shard_map/collect/pallas_call | solution.py:357
  38.6 0.6 %collective-permute-done.11.refs_1_ = bf16[128,1792]{1,0:T(8,128)(2,1)S(1)} collective-permute-done((bf16[128,1792]{1,0:T(8,128)(2,1)S(1)}, bf16[128,1792]{1,0:T(8,128)(2,1)S(1)}, u32[]{:S(2)}, u32[]{:S(2)}) %collective-permute-start.11) | collective-permute-done | bytes 458784 | tf_op jit(solution)/shard_map/ppermute | solution.py:316
  39.2 1.8 %collective-permute-done.13.refs_3_ = bf16[128,1792]{1,0:T(8,128)(2,1)S(1)} collective-permute-done((bf16[128,1792]{1,0:T(8,128)(2,1)S(1)}, bf16[128,1792]{1,0:T(8,128)(2,1)S(1)}, u32[]{:S(2)}, u32[]{:S(2)}) %collective-permute-start.13) | collective-permute-done | bytes 458784 | tf_op jit(solution)/shard_map/ppermute | solution.py:316
  41.0 2.9 %weight_grads.1 = (bf16[1792,512]{1,0:T(8,128)(2,1)}, bf16[1792,512]{1,0:T(8,128)(2,1)}, bf16[1792,512]{1,0:T(8,128)(2,1)}) custom-call(bf16[128,1792]{1,0:T(8,128)(2,1)S(1)} %collective-permute-done.2.refs_0_, bf16[128,1792]{1,0:T(8,128)(2,1)S(1)} %collective-permute-done.11.refs_1_, bf16[128,1792]{1,0:T(8,128)(2,1)S(1)} %collective-permute-done.12.refs_2_, ...), custom_call_target="tpu_custom_call" | custom-call | flops 1409286144 | bytes 4000000 | tf_op jit(solution)/shard_map/weight_grads/pallas_call | solution.py:272
  (23 shorter events, 0.3 us)
Async XLA Ops:
  0.6 5.1 %copy-start.2 = (f32[1,1,64,4]{2,3,1,0:T(4,128)S(1)}, f32[1,1,64,4]{2,3,1,0:T(4,128)}, u32[]{:S(2)}) copy-start(f32[1,1,64,4]{2,3,1,0:T(4,128)} %param.9) | copy-start | bytes 3076
  0.6 5.1 %copy-start.3 = (s32[1,1,4]{2,1,0:T(1,128)S(1)}, s32[1,1,4]{2,1,0:T(1,128)}, u32[]{:S(2)}) copy-start(s32[1,1,4]{2,1,0:T(1,128)} %param.10) | copy-start | bytes 52
  2.7 13.7 %collective-permute-start.2 = (bf16[128,1792]{1,0:T(8,128)(2,1)}, bf16[128,1792]{1,0:T(8,128)(2,1)S(1)}, u32[]{:S(2)}, u32[]{:S(2)}) collective-permute-start(bf16[128,1792]{1,0:T(8,128)(2,1)} %share.1), channel_id=1, source_target_pairs={{0,16},{16,0},{1,17},{17,1},{2,18},{18,2},{3,19},{19,3},{4,20},{20... | collective-permute-start | bytes 1376264 | tf_op jit(solution)/shard_map/ppermute | solution.py:319
  5.7 13.2 %copy-start.1 = (bf16[1,1,64,4,3584]{4,3,2,1,0:T(4,128)(2,1)S(1)}, bf16[1,1,64,4,3584]{4,3,2,1,0:T(4,128)(2,1)}, u32[]{:S(2)}) copy-start(bf16[1,1,64,4,3584]{4,3,2,1,0:T(4,128)(2,1)} %param.8) | copy-start | bytes 5505028
  14.6 4.3 %copy-start = (bf16[1,1,64,4,3584]{4,3,2,1,0:T(4,128)(2,1)S(1)}, bf16[1,1,64,4,3584]{4,3,2,1,0:T(4,128)(2,1)}, u32[]{:S(2)}) copy-start(bf16[1,1,64,4,3584]{4,3,2,1,0:T(4,128)(2,1)} %param.7) | copy-start | bytes 5505028
  14.6 1.6 %collective-permute-start.1 = (bf16[32,3584]{1,0:T(8,128)(2,1)S(1)}, bf16[32,3584]{1,0:T(8,128)(2,1)S(1)}, u32[]{:S(2)}, u32[]{:S(2)}) collective-permute-start(bf16[32,3584]{1,0:T(8,128)(2,1)S(1)} %get-tuple-element.33), channel_id=1, source_target_pairs={{0,1},{1,0},{2,3},{3,2},{4,5},{5,4},{6,7},{7,6},{8,9},{9,8},{10,11... | collective-permute-start | bytes 688136 | tf_op jit(solution)/shard_map/ppermute | solution.py:316
  14.7 1.8 %collective-permute-start = (bf16[32,3584]{1,0:T(8,128)(2,1)S(1)}, bf16[32,3584]{1,0:T(8,128)(2,1)S(1)}, u32[]{:S(2)}, u32[]{:S(2)}) collective-permute-start(bf16[32,3584]{1,0:T(8,128)(2,1)S(1)} %get-tuple-element.28), channel_id=1, source_target_pairs={{0,1},{1,0},{2,3},{3,2},{4,5},{5,4},{6,7},{7,6},{8,9},{9,8},{10,11... | collective-permute-start | bytes 688136 | tf_op jit(solution)/shard_map/ppermute | solution.py:316
  15.2 3.2 %collective-permute-start.7 = (bf16[32,3584]{1,0:T(8,128)(2,1)S(1)}, bf16[32,3584]{1,0:T(8,128)(2,1)S(1)}, u32[]{:S(2)}, u32[]{:S(2)}) collective-permute-start(bf16[32,3584]{1,0:T(8,128)(2,1)S(1)} %get-tuple-element.39), channel_id=1, source_target_pairs={{0,1},{1,0},{2,3},{3,2},{4,5},{5,4},{6,7},{7,6},{8,9},{9,8},{10,11... | collective-permute-start | bytes 688136 | tf_op jit(solution)/shard_map/ppermute | solution.py:316
  15.3 3.2 %collective-permute-start.8 = (bf16[32,3584]{1,0:T(8,128)(2,1)S(1)}, bf16[32,3584]{1,0:T(8,128)(2,1)S(1)}, u32[]{:S(2)}, u32[]{:S(2)}) collective-permute-start(bf16[32,3584]{1,0:T(8,128)(2,1)S(1)} %get-tuple-element.40), channel_id=1, source_target_pairs={{0,1},{1,0},{2,3},{3,2},{4,5},{5,4},{6,7},{7,6},{8,9},{9,8},{10,11... | collective-permute-start | bytes 688136 | tf_op jit(solution)/shard_map/ppermute | solution.py:316
  16.2 19.6 %collective-permute-start.6 = (bf16[3,256,512]{2,1,0:T(8,128)(2,1)S(1)}, bf16[3,256,512]{2,1,0:T(8,128)(2,1)S(1)}, u32[]{:S(2)}, u32[]{:S(2)}) collective-permute-start(bf16[3,256,512]{2,1,0:T(8,128)(2,1)S(1)} %get-tuple-element.30.acts), channel_id=1, source_target_pairs={{0,16},{16,0},{1,17},{17,1},{2,18},{18,2},{3,19},{19,3},{4,20},{20... | collective-permute-start | bytes 2359304 | tf_op jit(solution)/shard_map/ppermute | solution.py:319
  16.6 8.5 %collective-permute-start.3 = (bf16[32,3584]{1,0:T(8,128)(2,1)S(1)}, bf16[32,3584]{1,0:T(8,128)(2,1)S(1)}, u32[]{:S(2)}, u32[]{:S(2)}) collective-permute-start(bf16[32,3584]{1,0:T(8,128)(2,1)S(1)} %get-tuple-element.53), channel_id=1, source_target_pairs={{0,2},{1,3},{2,0},{3,1},{4,6},{5,7},{6,4},{7,5},{8,10},{9,11},{10,... | collective-permute-start | bytes 688136 | tf_op jit(solution)/shard_map/ppermute | solution.py:316
  18.6 12.6 %collective-permute-start.9 = (bf16[32,3584]{1,0:T(8,128)(2,1)S(1)}, bf16[32,3584]{1,0:T(8,128)(2,1)S(1)}, u32[]{:S(2)}, u32[]{:S(2)}) collective-permute-start(bf16[32,3584]{1,0:T(8,128)(2,1)S(1)} %get-tuple-element.49), channel_id=1, source_target_pairs={{0,2},{1,3},{2,0},{3,1},{4,6},{5,7},{6,4},{7,5},{8,10},{9,11},{10,... | collective-permute-start | bytes 688136 | tf_op jit(solution)/shard_map/ppermute | solution.py:316
  25.2 14.0 %collective-permute-start.11 = (bf16[128,1792]{1,0:T(8,128)(2,1)S(1)}, bf16[128,1792]{1,0:T(8,128)(2,1)S(1)}, u32[]{:S(2)}, u32[]{:S(2)}) collective-permute-start(bf16[128,1792]{1,0:T(8,128)(2,1)S(1)} %collective-permute-done.2.refs_0_), channel_id=1, source_target_pairs={{0,2},{1,3},{2,0},{3,1},{4,6},{5,7},{6,4},{7,5},{8,10},{9,11},{10,... | collective-permute-start | bytes 1376264 | tf_op jit(solution)/shard_map/ppermute | solution.py:316
  27.0 8.8 %collective-permute-start.5 = (bf16[16,3584]{1,0:T(8,128)(2,1)S(1)}, bf16[16,3584]{1,0:T(8,128)(2,1)S(1)}, u32[]{:S(2)}, u32[]{:S(2)}) collective-permute-start(bf16[16,3584]{1,0:T(8,128)(2,1)S(1)} %get-tuple-element.50), channel_id=1, source_target_pairs={{0,4},{4,8},{8,12},{12,0},{1,5},{5,9},{9,13},{13,1},{2,6},{6,10},{... | collective-permute-start | bytes 344072 | tf_op jit(solution)/shard_map/ppermute | solution.py:351
  28.6 8.9 %collective-permute-start.4 = (bf16[16,3584]{1,0:T(8,128)(2,1)S(1)}, bf16[16,3584]{1,0:T(8,128)(2,1)S(1)}, u32[]{:S(2)}, u32[]{:S(2)}) collective-permute-start(bf16[16,3584]{1,0:T(8,128)(2,1)S(1)} %get-tuple-element.51), channel_id=1, source_target_pairs={{0,8},{4,12},{8,0},{12,4},{1,9},{5,13},{9,1},{13,5},{2,10},{6,14},... | collective-permute-start | bytes 344072 | tf_op jit(solution)/shard_map/ppermute | solution.py:351
  31.3 6.3 %collective-permute-start.10 = (bf16[16,3584]{1,0:T(8,128)(2,1)S(1)}, bf16[16,3584]{1,0:T(8,128)(2,1)S(1)}, u32[]{:S(2)}, u32[]{:S(2)}) collective-permute-start(bf16[16,3584]{1,0:T(8,128)(2,1)S(1)} %add_convert_fusion.4), channel_id=1, source_target_pairs={{0,12},{4,0},{8,4},{12,8},{1,13},{5,1},{9,5},{13,9},{2,14},{6,2},{... | collective-permute-start | bytes 344072 | tf_op jit(solution)/shard_map/ppermute | solution.py:351
  35.8 3.4 %collective-permute-start.12 = (bf16[128,1792]{1,0:T(8,128)(2,1)S(1)}, bf16[128,1792]{1,0:T(8,128)(2,1)S(1)}, u32[]{:S(2)}, u32[]{:S(2)}) collective-permute-start(bf16[128,1792]{1,0:T(8,128)(2,1)S(1)} %collective-permute-done.2.refs_0_), channel_id=1, source_target_pairs={{0,1},{1,0},{2,3},{3,2},{4,5},{5,4},{6,7},{7,6},{8,9},{9,8},{10,11... | collective-permute-start | bytes 1376264 | tf_op jit(solution)/shard_map/ppermute | solution.py:316
  39.2 1.8 %collective-permute-start.13 = (bf16[128,1792]{1,0:T(8,128)(2,1)S(1)}, bf16[128,1792]{1,0:T(8,128)(2,1)S(1)}, u32[]{:S(2)}, u32[]{:S(2)}) collective-permute-start(bf16[128,1792]{1,0:T(8,128)(2,1)S(1)} %collective-permute-done.11.refs_1_), channel_id=1, source_target_pairs={{0,1},{1,0},{2,3},{3,2},{4,5},{5,4},{6,7},{7,6},{8,9},{9,8},{10,11... | collective-permute-start | bytes 1376264 | tf_op jit(solution)/shard_map/ppermute | solution.py:316

commit v7 on v6

v7 whole, which is shorter than its diff:
```python
import functools

import jax
import jax.numpy as jnp
from jax import lax
from jax.experimental import pallas as pl
from jax.experimental.pallas import tpu as pltpu
from jax.sharding import PartitionSpec as P

F32, BF16 = jnp.float32, jnp.bfloat16
MIB = 1024 * 1024
VMEM_LIMIT = 32 * MIB
TAIL, PIECE = 16, 256


def dot(a, b, contract_a, contract_b):
    return lax.dot_general(a, b, (((contract_a,), (contract_b,)), ((), ())), preferred_element_type=F32)


def flat_rows(block):
    return block.reshape(block.shape[0] * block.shape[1], block.shape[2])


def in_hbm(*arrays):
    return [pltpu.with_memory_space_constraint(a, pltpu.HBM) for a in arrays]


def log2(n):
    assert n & (n - 1) == 0
    return n.bit_length() - 1


def halving_order(size):
    order = [0]
    for i in reversed(range(log2(size))):
        order = order + [d ^ (1 << i) for d in order]
    return order


def bit_reverse(value, bits):
    out = jnp.zeros_like(value)
    for i in range(bits):
        out = out | (((value >> i) & 1) << (bits - 1 - i))
    return out


def shift_order(nodes):
    return sorted(range(1, nodes), key=lambda k: (-min(k, nodes - k), k)) + [0]


def column(weights, counts, first, out_rows):
    weights = weights.T
    slots, nodes = weights.shape
    slot = first + lax.broadcasted_iota(jnp.int32, (slots, nodes), 0)
    factor = weights * jnp.where(slot < counts, 1.0, 0.0)
    spread = jnp.broadcast_to(factor[:, None, :], (slots, nodes, nodes)).reshape(out_rows, nodes)
    row = lax.broadcasted_iota(jnp.int32, (out_rows, nodes), 0)
    lane = lax.broadcasted_iota(jnp.int32, (out_rows, nodes), 1)
    return jnp.sum(jnp.where((row & (nodes - 1)) == lane, spread, 0.0), axis=1, keepdims=True)


def pick_slots(weights, first, keep):
    out = weights[:, :keep]
    for at in range(keep, weights.shape[1], keep):
        out = jnp.where(first == at, weights[:, at:at + keep], out)
    return out


def share_kernel(tok_hbm, grad_hbm, weights_hbm, counts_hbm, out, tok, grad, weights, counts, sem):
    keep, nodes, part = tok.shape
    head = grad.shape[0]
    me, other = lax.axis_index("local"), 1 - lax.axis_index("dp")
    cols = pl.ds(pl.multiple_of(other * part, 128), part)
    first = me * keep
    copies = [pltpu.make_async_copy(weights_hbm, weights, sem.at[0]), pltpu.make_async_copy(counts_hbm, counts, sem.at[1]),
              pltpu.make_async_copy(grad_hbm.at[pl.ds(first, head), :, cols], grad, sem.at[2]),
              pltpu.make_async_copy(tok_hbm.at[pl.ds(first, keep), :, cols], tok, sem.at[3])]
    for copy in copies:
        copy.start()
    for copy in copies[:2]:
        copy.wait()
    factor = column(pick_slots(weights[...], first, keep), counts[...], first, keep * nodes)
    copies[2].wait()
    out[keep * nodes:] = (flat_rows(grad[...].astype(F32)) * factor[:head * nodes]).astype(BF16)
    copies[3].wait()
    out[:keep * nodes] = flat_rows(tok[...])


def share(locals_, tokens, grads, weights, counts):
    slots, nodes, width = tokens.shape
    keep, part = slots // locals_, width // 2
    head = keep - TAIL // nodes
    vmem, hbm = pl.BlockSpec(memory_space=pltpu.VMEM), pl.BlockSpec(memory_space=pltpu.HBM)
    return pl.pallas_call(
        share_kernel,
        out_shape=jax.ShapeDtypeStruct(((keep + head) * nodes, part), BF16),
        in_specs=[hbm] * 4,
        out_specs=vmem,
        scratch_shapes=[pltpu.VMEM((keep, nodes, part), BF16), pltpu.VMEM((head, nodes, part), BF16),
                        pltpu.VMEM(weights.shape, F32), pltpu.VMEM(counts.shape, jnp.int32), pltpu.SemaphoreType.DMA((4,))],
        compiler_params=pltpu.CompilerParams(vmem_limit_bytes=VMEM_LIMIT),
        name="share",
    )(*in_hbm(tokens, grads, weights, counts))


def tail_rows(part, hid_local, blocks):
    return -(-blocks * (part // PIECE) // (hid_local // PIECE)) * TAIL


def tail_spot(i, hid_local):
    across = hid_local // PIECE
    return slice(i // across * TAIL, (i // across + 1) * TAIL), slice(i % across * PIECE, (i % across + 1) * PIECE)


def forward_kernel(locals_, chunk, tok_hbm, grad_hbm, weights_hbm, counts_hbm, wg, wu_hbm, wd_hbm,
                   acts, own_a, own_b, send_a_low, send_a_high, send_b_low, send_b_high,
                   tok, grad, weights, counts, wu, wd, acc, acc_h, moved, sem):
    slots, nodes, width = tok.shape
    rows = slots * nodes
    keep = slots // locals_
    steps = width // chunk
    hid_local = wd.shape[1]
    me, node = lax.axis_index("local"), lax.axis_index("node")

    def fetch(i):
        cols = pl.ds(i * chunk, chunk)
        ends = [(tok_hbm.at[:, :, cols], tok.at[:, :, cols]), (wu_hbm.at[cols], wu.at[cols]), (grad_hbm.at[:, :, cols], grad.at[:, :, cols]), (wd_hbm.at[cols], wd.at[cols])]
        return [pltpu.make_async_copy(src, dst, sem.at[i, n]) for n, (src, dst) in enumerate(ends)]

    small = [pltpu.make_async_copy(weights_hbm, weights, sem.at[steps, 0]), pltpu.make_async_copy(counts_hbm, counts, sem.at[steps, 1])]
    copies = [fetch(i) for i in range(steps)]
    for group in [small] + copies:
        for copy in group:
            copy.start()
    for copy in small:
        copy.wait()
    factor = column(weights[...], counts[...], 0, rows)
    for i in range(steps):
        cols = pl.ds(i * chunk, chunk)
        copies[i][0].wait()
        t = flat_rows(tok[:, :, cols])
        gate = dot(t, wg[cols], 1, 0)
        copies[i][1].wait()
        up = dot(t, wu[cols], 1, 0)
        for copy in copies[i][2:]:
            copy.wait()
        scaled = (flat_rows(grad[:, :, cols].astype(F32)) * factor).astype(BF16)
        back = dot(scaled, wd[cols], 1, 0)
        if i:
            acc[:, :hid_local] += gate
            acc[:, hid_local:] += up
            acc_h[...] += back
        else:
            acc[:, :hid_local] = gate
            acc[:, hid_local:] = up
            acc_h[...] = back

    part, block = width // 2, keep * nodes
    cols = pl.ds(pl.multiple_of((1 - lax.axis_index("dp")) * part, 128), part)
    pieces = part // PIECE
    for b, d in enumerate(halving_order(locals_)[:locals_ // 2]):
        place = me ^ d
        picked = jnp.zeros((TAIL, 1), F32)
        for n in range(locals_):
            picked = jnp.where(place == n, factor[(n + 1) * block - TAIL:(n + 1) * block], picked)
        slot = pl.ds((place + 1) * keep - TAIL // nodes, TAIL // nodes)
        tail = (flat_rows(grad[slot, :, cols].astype(F32)) * picked).astype(BF16)
        for i in range(pieces):
            down, across = tail_spot(b * pieces + i, hid_local)
            acts[3 * rows + down.start:3 * rows + down.stop, across] = tail[:, i * PIECE:(i + 1) * PIECE]

    band = 64

    def activate(i, carry):
        at = pl.ds(pl.multiple_of(i * band, band), band)
        gate, up, back = acc[at, :hid_local], acc[at, hid_local:], acc_h[at]
        sig = jax.nn.sigmoid(gate)
        act = gate * sig
        acts[pl.ds(pl.multiple_of(2 * rows + i * band, band), band)] = (act * up).astype(BF16)
        acts[at] = (back * up * sig * (1.0 + gate * (1.0 - sig))).astype(BF16)
        acts[pl.ds(pl.multiple_of(rows + i * band, band), band)] = (back * act).astype(BF16)
        return carry

    lax.fori_loop(0, rows // band, activate, 0)

    per = nodes // 2
    p = lax.broadcasted_iota(jnp.int32, (rows, 1), 0)
    j = p & (keep - 1)
    at = log2(keep)
    quick = (p >> at) & (per - 1)
    at += log2(per)
    low = (p >> at) & (locals_ // 2 - 1)
    at += log2(locals_ // 2)
    group = (p >> at) & 1
    high = p >> (at + 1)
    place = bit_reverse(high * (locals_ // 2) + low, log2(locals_)) ^ me
    hop = jnp.zeros_like(p)
    for n, k in enumerate(shift_order(nodes)):
        hop = jnp.where(group * per + quick == n, k, hop)
    index = (place * keep + j) * nodes + ((node + hop) & (nodes - 1))
    one_hot = jnp.where(index == lax.broadcasted_iota(jnp.int32, (rows, rows), 1), 1.0, 0.0).astype(BF16)
    moved[:, :hid_local] = dot(one_hot, acts[:rows], 1, 0).astype(BF16)
    moved[:, hid_local:] = dot(one_hot, acts[rows:2 * rows], 1, 0).astype(BF16)
    for i in range(steps):
        cols = pl.ds(i * chunk, chunk)
        total = (dot(moved[:, :hid_local], wg[cols], 1, 1) + dot(moved[:, hid_local:], wu[cols], 1, 1)).astype(BF16)
        at = 0
        for out in (own_a, own_b, send_a_low, send_a_high, send_b_low, send_b_high):
            out[:, cols] = total[at:at + out.shape[0]]
            at += out.shape[0]


def forward(locals_, tokens, grads, weights, counts, gate_weight, up_weight, down_weight):
    slots, nodes, width = tokens.shape
    rows = slots * nodes
    hid_local = gate_weight.shape[1]
    vmem, hbm = pl.BlockSpec(memory_space=pltpu.VMEM), pl.BlockSpec(memory_space=pltpu.HBM)
    chunk = 512
    return pl.pallas_call(
        functools.partial(forward_kernel, locals_, chunk),
        out_shape=[jax.ShapeDtypeStruct((3 * rows + tail_rows(width // 2, hid_local, locals_ // 2), hid_local), BF16)] + [jax.ShapeDtypeStruct((rows // 4, width), BF16)] * 2
        + [jax.ShapeDtypeStruct((rows // 8, width), BF16)] * 4,
        in_specs=[hbm] * 4 + [vmem] + [hbm] * 2,
        out_specs=[vmem] * 7,
        scratch_shapes=[
            pltpu.VMEM(tokens.shape, BF16), pltpu.VMEM(tokens.shape, BF16), pltpu.VMEM(weights.shape, F32),
            pltpu.VMEM(counts.shape, jnp.int32), pltpu.VMEM((width, hid_local), BF16), pltpu.VMEM((width, hid_local), BF16),
            pltpu.VMEM((rows, 2 * hid_local), F32), pltpu.VMEM((rows, hid_local), F32), pltpu.VMEM((rows, 2 * hid_local), BF16),
            pltpu.SemaphoreType.DMA((width // chunk + 1, 4))],
        compiler_params=pltpu.CompilerParams(vmem_limit_bytes=VMEM_LIMIT),
        cost_estimate=pl.CostEstimate(flops=10 * rows * width * hid_local, bytes_accessed=18_000_000, transcendentals=0),
        name="forward",
    )(*in_hbm(tokens, grads, weights, counts), gate_weight, *in_hbm(up_weight, down_weight))


def own_kernel(tok, grad, weights_ref, counts_ref, acts, gate_out, up_out, down_out):
    slots, nodes, width = tok.shape
    part = gate_out.shape[0]
    replica = lax.axis_index("dp")
    count = slots * nodes
    factor = column(weights_ref[...], counts_ref[...], 0, count)
    chunk = 896
    for i in range(part // chunk):
        cols = pl.ds(i * chunk, chunk)
        mine = pl.ds(pl.multiple_of(replica * part + i * chunk, 128), chunk)
        rows = flat_rows(tok[:, :, mine])
        gate_out[cols] = dot(rows, acts[:count], 0, 0).astype(BF16)
        up_out[cols] = dot(rows, acts[count:2 * count], 0, 0).astype(BF16)
        scaled = (flat_rows(grad[:, :, mine].astype(F32)) * factor).astype(BF16)
        down_out[cols] = dot(scaled, acts[2 * count:3 * count], 0, 0).astype(BF16)


def own_grads(tokens, grads, weights, counts, acts):
    slots, nodes, width = tokens.shape
    rows, hid_local = slots * nodes, acts.shape[1]
    part = width // 2
    vmem = pl.BlockSpec(memory_space=pltpu.VMEM)
    return pl.pallas_call(
        own_kernel,
        out_shape=[jax.ShapeDtypeStruct((part, hid_local), BF16)] * 3,
        in_specs=[vmem] * 5,
        out_specs=[vmem] * 3,
        compiler_params=pltpu.CompilerParams(vmem_limit_bytes=VMEM_LIMIT),
        cost_estimate=pl.CostEstimate(flops=6 * rows * part * hid_local, bytes_accessed=10_000_000, transcendentals=0),
        name="own_grads",
    )(tokens, grads, weights, counts, acts)


def weight_kernel(order, block, *refs):
    shares = refs[:len(order)]
    there_ref, tails_ref, *parts = refs[len(order):len(order) + 5]
    outs = refs[len(order) + 5:len(order) + 8]
    left, right, bufs, sem = refs[len(order) + 8:]
    part, hid_local = outs[0].shape
    me = lax.axis_index("local")
    rows = len(order) * block
    for b, d in enumerate(order):
        for n in range(3):
            right[n, b * block:(b + 1) * block] = there_ref[pl.ds(pl.multiple_of(n * rows + (me ^ d) * block, block), block)]
    pieces = part // PIECE
    half = len(order) // 2
    for b, ref in enumerate(shares):
        left[0, b * block:(b + 1) * block] = ref[:block]
        left[1, b * block:(b + 1) * block - TAIL] = ref[block:]
        source, first = (there_ref, 3 * rows) if b < half else (tails_ref, 0)
        for i in range(pieces):
            down, across = tail_spot(b % half * pieces + i, hid_local)
            left[1, (b + 1) * block - TAIL:(b + 1) * block, i * PIECE:(i + 1) * PIECE] = (
                source[first + down.start:first + down.stop, across])
    chunk = 896
    copies = []
    for i in range(part // chunk):
        cols = pl.ds(i * chunk, chunk)
        for n, out in enumerate(outs):
            bufs[n, cols] = (dot(left[n // 2, :, cols], right[n], 0, 0) + parts[n][cols].astype(F32)).astype(BF16)
            copies.append(pltpu.make_async_copy(bufs.at[n, cols], out.at[cols], sem.at[i, n]))
            copies[-1].start()
    for copy in copies:
        copy.wait()


def weight_grads(order, block, shares, there, tails, parts):
    part = shares[0].shape[-1]
    hid_local = there.shape[1]
    rows = len(order) * block
    vmem = pl.BlockSpec(memory_space=pltpu.VMEM)
    return pl.pallas_call(
        functools.partial(weight_kernel, order, block),
        out_shape=[jax.ShapeDtypeStruct((part, hid_local), BF16)] * 3,
        in_specs=[vmem] * (5 + len(shares)),
        out_specs=[pl.BlockSpec(memory_space=pltpu.HBM)] * 3,
        scratch_shapes=[pltpu.VMEM((2, rows, part), BF16), pltpu.VMEM((3, rows, hid_local), BF16),
                        pltpu.VMEM((3, part, hid_local), BF16), pltpu.SemaphoreType.DMA((part // 896, 3))],
        compiler_params=pltpu.CompilerParams(vmem_limit_bytes=VMEM_LIMIT),
        cost_estimate=pl.CostEstimate(flops=6 * rows * part * hid_local, bytes_accessed=4_000_000, transcendentals=0),
        name="weight_grads",
    )(*shares, there, tails, *parts)


def collect_kernel(*refs):
    *arrived, kept, came, out = refs
    keep, nodes, width = out.shape
    node = lax.axis_index("node")
    last = (kept[...].astype(F32) + came[...].astype(F32)).astype(BF16)
    stacked = jnp.concatenate([last] + [a[...] for a in arrived], axis=0)
    rows = keep * nodes
    p = lax.broadcasted_iota(jnp.int32, (rows, rows), 0)
    source = ((node - (p & (nodes - 1))) & (nodes - 1)) * keep + (p >> log2(nodes))
    one_hot = jnp.where(source == lax.broadcasted_iota(jnp.int32, (rows, rows), 1), 1.0, 0.0).astype(BF16)
    out[...] = dot(one_hot, stacked, 1, 0).astype(BF16).reshape(out.shape)


def after(value, other):
    return lax.optimization_barrier((value, other))[0]


def add(a, b):
    return (a.astype(F32) + b.astype(F32)).astype(BF16)


def on_device(tokens_in, grad_rows, combine_weights, live_counts, w_gate, w_up, w_down):
    slots, nodes, width = tokens_in.shape[2:]
    replicas, locals_ = lax.axis_size("dp"), lax.axis_size("local")
    assert replicas == 2
    keep = slots // locals_
    tokens, grads, weights, counts = tokens_in[0, 0], grad_rows[0, 0], combine_weights[0, 0].T, live_counts[0]
    order = halving_order(locals_)
    bits = [1 << i for i in range(log2(locals_))]

    def swap_local(value, bit):
        return lax.ppermute(value, "local", [(i, i ^ bit) for i in range(locals_)])

    def swap_dp(value):
        return lax.ppermute(value, "dp", [(0, 1), (1, 0)])

    rows = slots * nodes
    block = rows // locals_
    first, weights = lax.optimization_barrier((share(locals_, tokens, grads, weights, counts), weights))
    first = swap_dp(first)
    acts, own_a, own_b, *send = forward(locals_, tokens, grads, weights, counts, w_gate[0], w_up[0], w_down[0])
    there = swap_dp(acts)

    per = nodes // 2
    hops = shift_order(nodes)
    arrived = [None] * nodes
    low_a, high_a, low_b, high_b = send
    came = [swap_local(v, bits[0]) for v in (high_a, high_b, low_a, low_b)]
    came[0] = after(came[0], first)
    half = own_a.shape[0] // 2
    held = [(add(own_a[:half], came[2]), swap_local(add(own_a[half:], came[0]), bits[1]))]
    parts = own_grads(tokens, grads, weights, counts, after(acts, held[0][0]))
    held.append((add(own_b[:half], came[3]), swap_local(after(add(own_b[half:], came[1]), parts[0]), bits[1])))
    for bit in bits[2:]:
        for g, (mine, other) in enumerate(held):
            half = mine.shape[0] // 2
            held[g] = (add(mine[:half], other[:half]), swap_local(add(mine[half:], other[half:]), bit))
    shares = [after(first, held[0][1])]
    for bit in reversed(bits[1:]):
        shares = shares + [swap_local(v, bit) for v in shares]
    for n, k in enumerate(hops):
        mine, other = (v[n % per * keep:(n % per + 1) * keep] for v in held[n // per])
        if k:
            total = add(mine, other)
            arrived[k] = lax.ppermute(total, "node", [(i, (i + k) % nodes) for i in range(nodes)])
        else:
            arrived[0] = (mine, other)
    early = lax.optimization_barrier([arrived[k] for k in hops[:per]])
    for k, value in zip(hops[:per], early):
        arrived[k] = value
    d_tokens = pl.pallas_call(
        collect_kernel,
        out_shape=jax.ShapeDtypeStruct((keep, nodes, width), BF16),
        in_specs=[pl.BlockSpec(memory_space=pltpu.VMEM)] * (nodes + 1),
        out_specs=pl.BlockSpec(memory_space=pltpu.VMEM),
        compiler_params=pltpu.CompilerParams(vmem_limit_bytes=VMEM_LIMIT),
        name="collect",
    )(*arrived[1:], *arrived[0])

    shares[-1] = after(shares[-1], d_tokens)
    shares = shares + [swap_local(v, bits[0]) for v in shares]
    tails = swap_local(there[3 * rows:], bits[0])
    grad_gate, grad_up, grad_down = weight_grads(order, block, shares, there, tails, parts)
    return d_tokens[None, None], grad_gate[None], grad_up[None], grad_down[None]


def solution(mesh):
    return jax.shard_map(
        on_device,
        mesh=mesh,
        in_specs=(
            P("dp", "node", None, None, None),
            P("dp", "node", None, None, None),
            P("dp", "node", None, None),
            P("dp", "node", None),
            P("node", None, "local"),
            P("node", None, "local"),
            P("node", None, "local"),
        ),
        out_specs=(
            P("dp", "node", "local", None, None),
            P("node", "dp", "local"),
            P("node", "dp", "local"),
            P("node", "dp", "local"),
        ),
        check_vma=False,
    )
```

time: 44.1 us -> 42.3 us (0.959)
  waiting for transfers between devices: 11.1 us -> 9.27 us
  starting transfers between devices: 15 us -> 16.2 us
  Pallas kernels: 16.7 us -> 15.6 us
    ppermute x2, waiting for transfers between devices: 1.96 us -> 0.01 us  [swap_dp(): return lax.ppermute(value, 'dp', [(0, 1), (1, 0)])]
    ppermute x3, waiting for transfers between devices: 1.75 us -> 2.54 us  [on_device(): lax.ppermute(total, 'node', [(i, (i + k) % nodes) for i in range(nodes)])]
    ppermute x2, starting transfers between devices: 3.05 us -> 3.81 us  [swap_dp(): return lax.ppermute(value, 'dp', [(0, 1), (1, 0)])]
    pallas_call x2, Pallas kernels: 5 us -> 4.3 us  [the longest x1 2.93 us: weight_grads(): pl.pallas_call(functools.partial(weight_kernel, order, block), out_shape=...]
    ppermute x9 -> x10, waiting for transfers between devices: 7.38 us -> 6.72 us  [swap_local(): return lax.ppermute(value, 'local', [(i, i ^ bit) for i in range(locals_)])]
    pallas_call x1, Pallas kernels: 8.9 us -> 8.44 us  [forward(): pl.pallas_call(functools.partial(forward_kernel, locals_, chunk), out_sha...]
    ppermute x9 -> x10, starting transfers between devices: 5.01 us -> 5.41 us  [swap_local(): return lax.ppermute(value, 'local', [(i, i ^ bit) for i in range(locals_)])]
  transfers between devices with their start and end apart: 14 -> 15, of which waited for: 8 -> 6; matrix products, arithmetic and copies ran while one was open for 1% -> 1% of each run, Pallas kernels for 27% -> 27%
where the time goes in v7:
time: 42.3 us; the launch traced here: 42.2 us
  starting transfers between devices  16.2 us (38%)
  Pallas kernels  15.6 us (37%)
  waiting for transfers between devices  9.27 us (22%)
  between operations  0.79 us (2%)
    pallas_call x1, Pallas kernels, forward(): pl.pallas_call(functools.partial(forward_kernel, locals_, chunk), out_sha...  8.44 us
    ppermute x3, starting transfers between devices, on_device(): lax.ppermute(total, 'node', [(i, (i + k) % nodes) for i in range(nodes)])  6.96 us
    ppermute x10, waiting for transfers between devices, swap_local(): return lax.ppermute(value, 'local', [(i, i ^ bit) for i in range(locals_)])  6.72 us
    ppermute x10, starting transfers between devices, swap_local(): return lax.ppermute(value, 'local', [(i, i ^ bit) for i in range(locals_)])  5.41 us
    ppermute x2, starting transfers between devices, swap_dp(): return lax.ppermute(value, 'dp', [(0, 1), (1, 0)])  3.81 us
    pallas_call x1, Pallas kernels, weight_grads(): pl.pallas_call(functools.partial(weight_kernel, order, block), out_shape=...  2.93 us
    ppermute x3, waiting for transfers between devices, on_device(): lax.ppermute(total, 'node', [(i, (i + k) % nodes) for i in range(nodes)])  2.54 us
    pallas_call x1, Pallas kernels, own_grads(): pl.pallas_call(own_kernel, out_shape=[jax.ShapeDtypeStruct((part, hid_loc...  1.79 us
  transfers between devices with their start and end apart: 15, of which 6 were waited for; matrix products, arithmetic and copies ran while one was open for 1% of the time, Pallas kernels for 27%

profile of v7, /device:TPU:0, one launch (start us, length us, event | category | flops | bytes accessed | tf_op | source)
XLA Modules:
  0.0 42.2 jit_solution(4923717391146872302)
XLA Ops:
  0.6 1.4 %share.1 = bf16[112,1792]{1,0:T(8,128)(2,1)S(1)} custom-call(bf16[64,4,3584]{2,1,0:T(4,128)(2,1)} %bitcast.13, bf16[64,4,3584]{2,1,0:T(4,128)(2,1)} %bitcast.16, f32[4,64]{1,0:T(4,128)} %bitcast.19, s32[1,4]{1,0:T(1,128)} %bitcast.22), custom_call_target="tpu_custom_call" | custom-call | tf_op jit(solution)/shard_map/share/pallas_call | solution.py:94
  2.0 3.0 %collective-permute-start.2 = (bf16[112,1792]{1,0:T(8,128)(2,1)S(1)}, bf16[112,1792]{1,0:T(8,128)(2,1)S(1)}, u32[]{:S(2)}, u32[]{:S(2)}) collective-permute-start(bf16[112,1792]{1,0:T(8,128)(2,1)S(1)} %share.1), channel_id=1, source_target_pairs={{0,16},{16,0},{1,17},{17,1},{2,18},{18,2},{3,19},{19,3},{4,20},{20... | collective-permute-start | bytes 1204232 | tf_op jit(solution)/shard_map/ppermute | solution.py:354
  5.0 8.4 %forward.1 = (bf16[880,512]{1,0:T(8,128)(2,1)S(1)}, bf16[64,3584]{1,0:T(8,128)(2,1)S(1)}, bf16[64,3584]{1,0:T(8,128)(2,1)S(1)}, bf16[32,3584]{1,0:T(8,128)(2,1)S...) custom-call(bf16[64,4,3584]{2,1,0:T(4,128)(2,1)} %bitcast.14, ...), custom_call_target="tpu_custom_call" | custom-call | flops 4697620480 | bytes 18000000 | tf_op jit(solution)/shard_map/forward/pallas_call | solution.py:219
  13.6 0.5 %collective-permute-start = (bf16[32,3584]{1,0:T(8,128)(2,1)S(1)}, bf16[32,3584]{1,0:T(8,128)(2,1)S(1)}, u32[]{:S(2)}, u32[]{:S(2)}) collective-permute-start(bf16[32,3584]{1,0:T(8,128)(2,1)S(1)} %get-tuple-element.28), channel_id=1, source_target_pairs={{0,1},{1,0},{2,3},{3,2},{4,5},{5,4},{6,7},{7,6},{8,9},{9,8},{10,11... | collective-permute-start | bytes 688136 | tf_op jit(solution)/shard_map/ppermute | solution.py:351
  14.2 0.4 %collective-permute-start.7 = (bf16[32,3584]{1,0:T(8,128)(2,1)S(1)}, bf16[32,3584]{1,0:T(8,128)(2,1)S(1)}, u32[]{:S(2)}, u32[]{:S(2)}) collective-permute-start(bf16[32,3584]{1,0:T(8,128)(2,1)S(1)} %get-tuple-element.36), channel_id=1, source_target_pairs={{0,1},{1,0},{2,3},{3,2},{4,5},{5,4},{6,7},{7,6},{8,9},{9,8},{10,11... | collective-permute-start | bytes 688136 | tf_op jit(solution)/shard_map/ppermute | solution.py:351
  14.6 0.5 %collective-permute-done.1 = bf16[32,3584]{1,0:T(8,128)(2,1)S(1)} collective-permute-done((bf16[32,3584]{1,0:T(8,128)(2,1)S(1)}, bf16[32,3584]{1,0:T(8,128)(2,1)S(1)}, u32[]{:S(2)}, u32[]{:S(2)}) %collective-permute-start.1) | collective-permute-done | bytes 229408 | tf_op jit(solution)/shard_map/ppermute | solution.py:351
  15.1 0.8 %collective-permute-start.13 = (bf16[880,512]{1,0:T(8,128)(2,1)S(1)}, bf16[880,512]{1,0:T(8,128)(2,1)S(1)}, u32[]{:S(2)}, u32[]{:S(2)}) collective-permute-start(bf16[880,512]{1,0:T(8,128)(2,1)S(1)} %get-tuple-element.38.acts), channel_id=1, source_target_pairs={{0,16},{16,0},{1,17},{17,1},{2,18},{18,2},{3,19},{19,3},{4,20},{20... | collective-permute-start | bytes 2703368 | tf_op jit(solution)/shard_map/ppermute | solution.py:354
  15.9 0.1 add_convert_fusion.3
  16.0 1.6 %collective-permute-start.3 = (bf16[32,3584]{1,0:T(8,128)(2,1)S(1)}, bf16[32,3584]{1,0:T(8,128)(2,1)S(1)}, u32[]{:S(2)}, u32[]{:S(2)}) collective-permute-start(bf16[32,3584]{1,0:T(8,128)(2,1)S(1)} %get-tuple-element.53), channel_id=1, source_target_pairs={{0,2},{1,3},{2,0},{3,1},{4,6},{5,7},{6,4},{7,5},{8,10},{9,11},{10,... | collective-permute-start | bytes 688136 | tf_op jit(solution)/shard_map/ppermute | solution.py:351
  17.6 0.1 add_convert_fusion.1
  17.8 1.8 %own_grads.1 = (bf16[1792,512]{1,0:T(8,128)(2,1)S(1)}, bf16[1792,512]{1,0:T(8,128)(2,1)S(1)}, bf16[1792,512]{1,0:T(8,128)(2,1)S(1)}) custom-call(bf16[64,4,3584]{2,1,0:T(4,128)(2,1)S(1)} %bitcast.15, bf16[64,4,3584]{2,1,0:T(4,128)(2,1)S(1)} %bitcast.18, f32[4,64]{1,0:T(4,128)S(1)} %bitcast.21, s32[1,4]{1,0:T(1,128)S(1)} %bitcast.24, ...), custom_call_target="tpu_custom_call" | custom-call | flops 1409286144 | bytes 10000000 | tf_op jit(solution)/shard_map/own_grads/pallas_call | solution.py:258
  19.5 0.6 %collective-permute-start.8 = (bf16[32,3584]{1,0:T(8,128)(2,1)S(1)}, bf16[32,3584]{1,0:T(8,128)(2,1)S(1)}, u32[]{:S(2)}, u32[]{:S(2)}) collective-permute-start(bf16[32,3584]{1,0:T(8,128)(2,1)S(1)} %get-tuple-element.40), channel_id=1, source_target_pairs={{0,2},{1,3},{2,0},{3,1},{4,6},{5,7},{6,4},{7,5},{8,10},{9,11},{10,... | collective-permute-start | bytes 688136 | tf_op jit(solution)/shard_map/ppermute | solution.py:351
  20.1 4.4 %collective-permute-done.3 = bf16[32,3584]{1,0:T(8,128)(2,1)S(1)} collective-permute-done((bf16[32,3584]{1,0:T(8,128)(2,1)S(1)}, bf16[32,3584]{1,0:T(8,128)(2,1)S(1)}, u32[]{:S(2)}, u32[]{:S(2)}) %collective-permute-start.3) | collective-permute-done | bytes 229408 | tf_op jit(solution)/shard_map/ppermute | solution.py:351
  24.6 1.6 %collective-permute-start.5 = (bf16[16,3584]{1,0:T(8,128)(2,1)S(1)}, bf16[16,3584]{1,0:T(8,128)(2,1)S(1)}, u32[]{:S(2)}, u32[]{:S(2)}) collective-permute-start(bf16[16,3584]{1,0:T(8,128)(2,1)S(1)} %get-tuple-element.50), channel_id=1, source_target_pairs={{0,4},{4,8},{8,12},{12,0},{1,5},{5,9},{9,13},{13,1},{2,6},{6,10},{... | collective-permute-start | bytes 344072 | tf_op jit(solution)/shard_map/ppermute | solution.py:384
  26.2 2.6 %collective-permute-start.4 = (bf16[16,3584]{1,0:T(8,128)(2,1)S(1)}, bf16[16,3584]{1,0:T(8,128)(2,1)S(1)}, u32[]{:S(2)}, u32[]{:S(2)}) collective-permute-start(bf16[16,3584]{1,0:T(8,128)(2,1)S(1)} %get-tuple-element.51), channel_id=1, source_target_pairs={{0,8},{4,12},{8,0},{12,4},{1,9},{5,13},{9,1},{13,5},{2,10},{6,14},... | collective-permute-start | bytes 344072 | tf_op jit(solution)/shard_map/ppermute | solution.py:384
  28.8 1.5 %collective-permute-start.10 = (bf16[112,1792]{1,0:T(8,128)(2,1)S(1)}, bf16[112,1792]{1,0:T(8,128)(2,1)S(1)}, u32[]{:S(2)}, u32[]{:S(2)}) collective-permute-start(bf16[112,1792]{1,0:T(8,128)(2,1)S(1)} %collective-permute-done.2.refs_0_), channel_id=1, source_target_pairs={{0,2},{1,3},{2,0},{3,1},{4,6},{5,7},{6,4},{7,5},{8,10},{9,11},{10,... | collective-permute-start | bytes 1204232 | tf_op jit(solution)/shard_map/ppermute | solution.py:351
  30.4 2.7 %collective-permute-start.9 = (bf16[16,3584]{1,0:T(8,128)(2,1)S(1)}, bf16[16,3584]{1,0:T(8,128)(2,1)S(1)}, u32[]{:S(2)}, u32[]{:S(2)}) collective-permute-start(bf16[16,3584]{1,0:T(8,128)(2,1)S(1)} %add_convert_fusion.4), channel_id=1, source_target_pairs={{0,12},{4,0},{8,4},{12,8},{1,13},{5,1},{9,5},{13,9},{2,14},{6,2},{... | collective-permute-start | bytes 344072 | tf_op jit(solution)/shard_map/ppermute | solution.py:384
  33.3 1.9 %collective-permute-done.4.refs_1_ = bf16[16,3584]{1,0:T(8,128)(2,1)S(1)} collective-permute-done((bf16[16,3584]{1,0:T(8,128)(2,1)S(1)}, bf16[16,3584]{1,0:T(8,128)(2,1)S(1)}, u32[]{:S(2)}, u32[]{:S(2)}) %collective-permute-start.4) | collective-permute-done | bytes 114720 | tf_op jit(solution)/shard_map/ppermute | solution.py:384
  35.1 0.7 %collective-permute-done.9.refs_2_ = bf16[16,3584]{1,0:T(8,128)(2,1)S(1)} collective-permute-done((bf16[16,3584]{1,0:T(8,128)(2,1)S(1)}, bf16[16,3584]{1,0:T(8,128)(2,1)S(1)}, u32[]{:S(2)}, u32[]{:S(2)}) %collective-permute-start.9) | collective-permute-done | bytes 114720 | tf_op jit(solution)/shard_map/ppermute | solution.py:384
  35.8 1.0 %collect.1 = bf16[16,4,3584]{2,1,0:T(4,128)(2,1)} custom-call(bf16[16,3584]{1,0:T(8,128)(2,1)S(1)} %collective-permute-done.5.refs_0_, bf16[16,3584]{1,0:T(8,128)(2,1)S(1)} %collective-permute-done.4.refs_1_, bf16[16,3584]{1,0:T(8,128)(2,1)S(1)} %collective-permute-done.9.refs_2_, bf16[16,3584]{1,0:T(8,128)(2,1)S(1)} %slice.58.refs_3_, ...), custom_call_target="tpu_custom_call" | custom-call | tf_op jit(solution)/shard_map/collect/pallas_call | solution.py:390
  36.8 0.5 %collective-permute-done.10.refs_1_ = bf16[112,1792]{1,0:T(8,128)(2,1)S(1)} collective-permute-done((bf16[112,1792]{1,0:T(8,128)(2,1)S(1)}, bf16[112,1792]{1,0:T(8,128)(2,1)S(1)}, u32[]{:S(2)}, u32[]{:S(2)}) %collective-permute-start.10) | collective-permute-done | bytes 401440 | tf_op jit(solution)/shard_map/ppermute | solution.py:351
  37.4 0.6 %collective-permute-start.14 = (bf16[112,512]{1,0:T(8,128)(2,1)S(1)}, bf16[112,512]{1,0:T(8,128)(2,1)S(1)}, u32[]{:S(2)}, u32[]{:S(2)}) collective-permute-start(bf16[112,512]{1,0:T(8,128)(2,1)S(1)} %slice.60), channel_id=1, source_target_pairs={{0,1},{1,0},{2,3},{3,2},{4,5},{5,4},{6,7},{7,6},{8,9},{9,8},{10,11... | collective-permute-start | bytes 344072 | tf_op jit(solution)/shard_map/ppermute | solution.py:351
  37.9 1.3 %collective-permute-done.14.refs_5_ = bf16[112,512]{1,0:T(8,128)(2,1)S(1)} collective-permute-done((bf16[112,512]{1,0:T(8,128)(2,1)S(1)}, bf16[112,512]{1,0:T(8,128)(2,1)S(1)}, u32[]{:S(2)}, u32[]{:S(2)}) %collective-permute-start.14) | collective-permute-done | bytes 114720 | tf_op jit(solution)/shard_map/ppermute | solution.py:351
  39.2 2.9 %weight_grads.1 = (bf16[1792,512]{1,0:T(8,128)(2,1)}, bf16[1792,512]{1,0:T(8,128)(2,1)}, bf16[1792,512]{1,0:T(8,128)(2,1)}) custom-call(bf16[112,1792]{1,0:T(8,128)(2,1)S(1)} %collective-permute-done.2.refs_0_, bf16[112,1792]{1,0:T(8,128)(2,1)S(1)} %collective-permute-done.10.refs_1_, bf16[112,1792]{1,0:T(8,128)(2,1)S(1)} %collective-permute-done.11.refs_2_, ...), custom_call_target="tpu_custom_call" | custom-call | flops 1409286144 | bytes 4000000 | tf_op jit(solution)/shard_map/weight_grads/pallas_call | solution.py:307
  (28 shorter events, 0.4 us)
Async XLA Ops:
  0.6 4.4 %copy-start.4 = (bf16[1,3584,512]{2,1,0:T(8,128)(2,1)S(1)}, bf16[1,3584,512]{2,1,0:T(8,128)(2,1)}, u32[]{:S(2)}) copy-start(bf16[1,3584,512]{2,1,0:T(8,128)(2,1)} %param.11) | copy-start | bytes 11010052
  2.0 13.9 %collective-permute-start.2 = (bf16[112,1792]{1,0:T(8,128)(2,1)S(1)}, bf16[112,1792]{1,0:T(8,128)(2,1)S(1)}, u32[]{:S(2)}, u32[]{:S(2)}) collective-permute-start(bf16[112,1792]{1,0:T(8,128)(2,1)S(1)} %share.1), channel_id=1, source_target_pairs={{0,16},{16,0},{1,17},{17,1},{2,18},{18,2},{3,19},{19,3},{4,20},{20... | collective-permute-start | bytes 1204232 | tf_op jit(solution)/shard_map/ppermute | solution.py:354
  5.0 12.7 %copy-start.1 = (bf16[1,1,64,4,3584]{4,3,2,1,0:T(4,128)(2,1)S(1)}, bf16[1,1,64,4,3584]{4,3,2,1,0:T(4,128)(2,1)}, u32[]{:S(2)}) copy-start(bf16[1,1,64,4,3584]{4,3,2,1,0:T(4,128)(2,1)} %param.8) | copy-start | bytes 5505028
  13.5 4.2 %copy-start = (bf16[1,1,64,4,3584]{4,3,2,1,0:T(4,128)(2,1)S(1)}, bf16[1,1,64,4,3584]{4,3,2,1,0:T(4,128)(2,1)}, u32[]{:S(2)}) copy-start(bf16[1,1,64,4,3584]{4,3,2,1,0:T(4,128)(2,1)} %param.7) | copy-start | bytes 5505028
  13.5 4.2 %copy-start.2 = (f32[1,1,64,4]{2,3,1,0:T(4,128)S(1)}, f32[1,1,64,4]{2,3,1,0:T(4,128)}, u32[]{:S(2)}) copy-start(f32[1,1,64,4]{2,3,1,0:T(4,128)} %param.9) | copy-start | bytes 3076
  13.5 4.2 %copy-start.3 = (s32[1,1,4]{2,1,0:T(1,128)S(1)}, s32[1,1,4]{2,1,0:T(1,128)}, u32[]{:S(2)}) copy-start(s32[1,1,4]{2,1,0:T(1,128)} %param.10) | copy-start | bytes 52
  13.5 1.6 %collective-permute-start.1 = (bf16[32,3584]{1,0:T(8,128)(2,1)S(1)}, bf16[32,3584]{1,0:T(8,128)(2,1)S(1)}, u32[]{:S(2)}, u32[]{:S(2)}) collective-permute-start(bf16[32,3584]{1,0:T(8,128)(2,1)S(1)} %get-tuple-element.29), channel_id=1, source_target_pairs={{0,1},{1,0},{2,3},{3,2},{4,5},{5,4},{6,7},{7,6},{8,9},{9,8},{10,11... | collective-permute-start | bytes 688136 | tf_op jit(solution)/shard_map/ppermute | solution.py:351
  13.6 2.3 %collective-permute-start = (bf16[32,3584]{1,0:T(8,128)(2,1)S(1)}, bf16[32,3584]{1,0:T(8,128)(2,1)S(1)}, u32[]{:S(2)}, u32[]{:S(2)}) collective-permute-start(bf16[32,3584]{1,0:T(8,128)(2,1)S(1)} %get-tuple-element.28), channel_id=1, source_target_pairs={{0,1},{1,0},{2,3},{3,2},{4,5},{5,4},{6,7},{7,6},{8,9},{9,8},{10,11... | collective-permute-start | bytes 688136 | tf_op jit(solution)/shard_map/ppermute | solution.py:351
  14.1 3.5 %collective-permute-start.6 = (bf16[32,3584]{1,0:T(8,128)(2,1)S(1)}, bf16[32,3584]{1,0:T(8,128)(2,1)S(1)}, u32[]{:S(2)}, u32[]{:S(2)}) collective-permute-start(bf16[32,3584]{1,0:T(8,128)(2,1)S(1)} %get-tuple-element.35), channel_id=1, source_target_pairs={{0,1},{1,0},{2,3},{3,2},{4,5},{5,4},{6,7},{7,6},{8,9},{9,8},{10,11... | collective-permute-start | bytes 688136 | tf_op jit(solution)/shard_map/ppermute | solution.py:351
  14.2 3.4 %collective-permute-start.7 = (bf16[32,3584]{1,0:T(8,128)(2,1)S(1)}, bf16[32,3584]{1,0:T(8,128)(2,1)S(1)}, u32[]{:S(2)}, u32[]{:S(2)}) collective-permute-start(bf16[32,3584]{1,0:T(8,128)(2,1)S(1)} %get-tuple-element.36), channel_id=1, source_target_pairs={{0,1},{1,0},{2,3},{3,2},{4,5},{5,4},{6,7},{7,6},{8,9},{9,8},{10,11... | collective-permute-start | bytes 688136 | tf_op jit(solution)/shard_map/ppermute | solution.py:351
  15.1 22.3 %collective-permute-start.13 = (bf16[880,512]{1,0:T(8,128)(2,1)S(1)}, bf16[880,512]{1,0:T(8,128)(2,1)S(1)}, u32[]{:S(2)}, u32[]{:S(2)}) collective-permute-start(bf16[880,512]{1,0:T(8,128)(2,1)S(1)} %get-tuple-element.38.acts), channel_id=1, source_target_pairs={{0,16},{16,0},{1,17},{17,1},{2,18},{18,2},{3,19},{19,3},{4,20},{20... | collective-permute-start | bytes 2703368 | tf_op jit(solution)/shard_map/ppermute | solution.py:354
  16.0 8.6 %collective-permute-start.3 = (bf16[32,3584]{1,0:T(8,128)(2,1)S(1)}, bf16[32,3584]{1,0:T(8,128)(2,1)S(1)}, u32[]{:S(2)}, u32[]{:S(2)}) collective-permute-start(bf16[32,3584]{1,0:T(8,128)(2,1)S(1)} %get-tuple-element.53), channel_id=1, source_target_pairs={{0,2},{1,3},{2,0},{3,1},{4,6},{5,7},{6,4},{7,5},{8,10},{9,11},{10,... | collective-permute-start | bytes 688136 | tf_op jit(solution)/shard_map/ppermute | solution.py:351
  19.5 10.8 %collective-permute-start.8 = (bf16[32,3584]{1,0:T(8,128)(2,1)S(1)}, bf16[32,3584]{1,0:T(8,128)(2,1)S(1)}, u32[]{:S(2)}, u32[]{:S(2)}) collective-permute-start(bf16[32,3584]{1,0:T(8,128)(2,1)S(1)} %get-tuple-element.40), channel_id=1, source_target_pairs={{0,2},{1,3},{2,0},{3,1},{4,6},{5,7},{6,4},{7,5},{8,10},{9,11},{10,... | collective-permute-start | bytes 688136 | tf_op jit(solution)/shard_map/ppermute | solution.py:351
  24.6 8.6 %collective-permute-start.5 = (bf16[16,3584]{1,0:T(8,128)(2,1)S(1)}, bf16[16,3584]{1,0:T(8,128)(2,1)S(1)}, u32[]{:S(2)}, u32[]{:S(2)}) collective-permute-start(bf16[16,3584]{1,0:T(8,128)(2,1)S(1)} %get-tuple-element.50), channel_id=1, source_target_pairs={{0,4},{4,8},{8,12},{12,0},{1,5},{5,9},{9,13},{13,1},{2,6},{6,10},{... | collective-permute-start | bytes 344072 | tf_op jit(solution)/shard_map/ppermute | solution.py:384
  26.2 8.9 %collective-permute-start.4 = (bf16[16,3584]{1,0:T(8,128)(2,1)S(1)}, bf16[16,3584]{1,0:T(8,128)(2,1)S(1)}, u32[]{:S(2)}, u32[]{:S(2)}) collective-permute-start(bf16[16,3584]{1,0:T(8,128)(2,1)S(1)} %get-tuple-element.51), channel_id=1, source_target_pairs={{0,8},{4,12},{8,0},{12,4},{1,9},{5,13},{9,1},{13,5},{2,10},{6,14},... | collective-permute-start | bytes 344072 | tf_op jit(solution)/shard_map/ppermute | solution.py:384
  28.8 8.5 %collective-permute-start.10 = (bf16[112,1792]{1,0:T(8,128)(2,1)S(1)}, bf16[112,1792]{1,0:T(8,128)(2,1)S(1)}, u32[]{:S(2)}, u32[]{:S(2)}) collective-permute-start(bf16[112,1792]{1,0:T(8,128)(2,1)S(1)} %collective-permute-done.2.refs_0_), channel_id=1, source_target_pairs={{0,2},{1,3},{2,0},{3,1},{4,6},{5,7},{6,4},{7,5},{8,10},{9,11},{10,... | collective-permute-start | bytes 1204232 | tf_op jit(solution)/shard_map/ppermute | solution.py:351
  30.4 5.4 %collective-permute-start.9 = (bf16[16,3584]{1,0:T(8,128)(2,1)S(1)}, bf16[16,3584]{1,0:T(8,128)(2,1)S(1)}, u32[]{:S(2)}, u32[]{:S(2)}) collective-permute-start(bf16[16,3584]{1,0:T(8,128)(2,1)S(1)} %add_convert_fusion.4), channel_id=1, source_target_pairs={{0,12},{4,0},{8,4},{12,8},{1,13},{5,1},{9,5},{13,9},{2,14},{6,2},{... | collective-permute-start | bytes 344072 | tf_op jit(solution)/shard_map/ppermute | solution.py:384
  33.2 6.1 %collective-permute-start.11 = (bf16[112,1792]{1,0:T(8,128)(2,1)S(1)}, bf16[112,1792]{1,0:T(8,128)(2,1)S(1)}, u32[]{:S(2)}, u32[]{:S(2)}) collective-permute-start(bf16[112,1792]{1,0:T(8,128)(2,1)S(1)} %collective-permute-done.2.refs_0_), channel_id=1, source_target_pairs={{0,1},{1,0},{2,3},{3,2},{4,5},{5,4},{6,7},{7,6},{8,9},{9,8},{10,11... | collective-permute-start | bytes 1204232 | tf_op jit(solution)/shard_map/ppermute | solution.py:351
  37.3 1.9 %collective-permute-start.12 = (bf16[112,1792]{1,0:T(8,128)(2,1)S(1)}, bf16[112,1792]{1,0:T(8,128)(2,1)S(1)}, u32[]{:S(2)}, u32[]{:S(2)}) collective-permute-start(bf16[112,1792]{1,0:T(8,128)(2,1)S(1)} %collective-permute-done.10.refs_1_), channel_id=1, source_target_pairs={{0,1},{1,0},{2,3},{3,2},{4,5},{5,4},{6,7},{7,6},{8,9},{9,8},{10,11... | collective-permute-start | bytes 1204232 | tf_op jit(solution)/shard_map/ppermute | solution.py:351
  37.4 1.9 %collective-permute-start.14 = (bf16[112,512]{1,0:T(8,128)(2,1)S(1)}, bf16[112,512]{1,0:T(8,128)(2,1)S(1)}, u32[]{:S(2)}, u32[]{:S(2)}) collective-permute-start(bf16[112,512]{1,0:T(8,128)(2,1)S(1)} %slice.60), channel_id=1, source_target_pairs={{0,1},{1,0},{2,3},{3,2},{4,5},{5,4},{6,7},{7,6},{8,9},{9,8},{10,11... | collective-permute-start | bytes 344072 | tf_op jit(solution)/shard_map/ppermute | solution.py:351

commit v8 on v7

--- a/solution.py
+++ b/solution.py
@@ -44,8 +44,8 @@
     return out
 
 
-def shift_order(nodes):
-    return sorted(range(1, nodes), key=lambda k: (-min(k, nodes - k), k)) + [0]
+def hop_order(nodes):
+    return sorted(range(1, nodes), key=lambda k: (-k.bit_length(), k)) + [0]
 
 
 def column(weights, counts, first, out_rows):
@@ -195,9 +195,9 @@
     high = p >> (at + 1)
     place = bit_reverse(high * (locals_ // 2) + low, log2(locals_)) ^ me
     hop = jnp.zeros_like(p)
-    for n, k in enumerate(shift_order(nodes)):
+    for n, k in enumerate(hop_order(nodes)):
         hop = jnp.where(group * per + quick == n, k, hop)
-    index = (place * keep + j) * nodes + ((node + hop) & (nodes - 1))
+    index = (place * keep + j) * nodes + (node ^ hop)
     one_hot = jnp.where(index == lax.broadcasted_iota(jnp.int32, (rows, rows), 1), 1.0, 0.0).astype(BF16)
     moved[:, :hid_local] = dot(one_hot, acts[:rows], 1, 0).astype(BF16)
     moved[:, hid_local:] = dot(one_hot, acts[rows:2 * rows], 1, 0).astype(BF16)
@@ -325,7 +325,7 @@
     stacked = jnp.concatenate([last] + [a[...] for a in arrived], axis=0)
     rows = keep * nodes
     p = lax.broadcasted_iota(jnp.int32, (rows, rows), 0)
-    source = ((node - (p & (nodes - 1))) & (nodes - 1)) * keep + (p >> log2(nodes))
+    source = (node ^ (p & (nodes - 1))) * keep + (p >> log2(nodes))
     one_hot = jnp.where(source == lax.broadcasted_iota(jnp.int32, (rows, rows), 1), 1.0, 0.0).astype(BF16)
     out[...] = dot(one_hot, stacked, 1, 0).astype(BF16).reshape(out.shape)
 
@@ -361,7 +361,7 @@
     there = swap_dp(acts)
 
     per = nodes // 2
-    hops = shift_order(nodes)
+    hops = hop_order(nodes)
     arrived = [None] * nodes
     low_a, high_a, low_b, high_b = send
     came = [swap_local(v, bits[0]) for v in (high_a, high_b, low_a, low_b)]
@@ -381,7 +381,7 @@
         mine, other = (v[n % per * keep:(n % per + 1) * keep] for v in held[n // per])
         if k:
             total = add(mine, other)
-            arrived[k] = lax.ppermute(total, "node", [(i, (i + k) % nodes) for i in range(nodes)])
+            arrived[k] = lax.ppermute(total, "node", [(i, i ^ k) for i in range(nodes)])
         else:
             arrived[0] = (mine, other)
     early = lax.optimization_barrier([arrived[k] for k in hops[:per]])
@@ -396,7 +396,8 @@
         name="collect",
     )(*arrived[1:], *arrived[0])
 
-    shares[-1] = after(shares[-1], d_tokens)
+    for value in arrived[1:]:
+        shares[-1] = after(shares[-1], value)
     shares = shares + [swap_local(v, bits[0]) for v in shares]
     tails = swap_local(there[3 * rows:], bits[0])
     grad_gate, grad_up, grad_down = weight_grads(order, block, shares, there, tails, parts)

time: 42.3 us -> 42 us (level)
  starting transfers between devices: 16.2 us -> 13.7 us
  waiting for transfers between devices: 9.27 us -> 11.5 us
    ppermute x3, waiting for transfers between devices: 2.54 us -> 5.78 us  [on_device(): arrived[k] = lax.ppermute(total, 'node', [(i, i ^ k) for i in range(nodes)])]
    ppermute x3, starting transfers between devices: 6.96 us -> 4.6 us  [on_device(): arrived[k] = lax.ppermute(total, 'node', [(i, i ^ k) for i in range(nodes)])]
    ppermute x10, waiting for transfers between devices: 6.72 us -> 5.64 us  [swap_local(): return lax.ppermute(value, 'local', [(i, i ^ bit) for i in range(locals_)])]
  transfers between devices with their start and end apart: 15 -> 15, of which waited for: 6 -> 7; matrix products, arithmetic and copies ran while one was open for 1% -> 1% of each run, Pallas kernels for 27% -> 27%
where the time goes in v8:
time: 42 us; the launch traced here: 41.9 us
  Pallas kernels  15.6 us (37%)
  starting transfers between devices  13.7 us (33%)
  waiting for transfers between devices  11.5 us (27%)
  between operations  0.78 us (2%)
    pallas_call x1, Pallas kernels, forward(): pl.pallas_call(functools.partial(forward_kernel, locals_, chunk), out_sha...  8.44 us
    ppermute x3, waiting for transfers between devices, on_device(): arrived[k] = lax.ppermute(total, 'node', [(i, i ^ k) for i in range(nodes)])  5.78 us
    ppermute x10, waiting for transfers between devices, swap_local(): return lax.ppermute(value, 'local', [(i, i ^ bit) for i in range(locals_)])  5.64 us
    ppermute x10, starting transfers between devices, swap_local(): return lax.ppermute(value, 'local', [(i, i ^ bit) for i in range(locals_)])  5.3 us
    ppermute x3, starting transfers between devices, on_device(): arrived[k] = lax.ppermute(total, 'node', [(i, i ^ k) for i in range(nodes)])  4.6 us
    ppermute x2, starting transfers between devices, swap_dp(): return lax.ppermute(value, 'dp', [(0, 1), (1, 0)])  3.81 us
    pallas_call x1, Pallas kernels, weight_grads(): pl.pallas_call(functools.partial(weight_kernel, order, block), out_shape=...  2.93 us
    pallas_call x1, Pallas kernels, own_grads(): pl.pallas_call(own_kernel, out_shape=[jax.ShapeDtypeStruct((part, hid_loc...  1.79 us
  transfers between devices with their start and end apart: 15, of which 7 were waited for; matrix products, arithmetic and copies ran while one was open for 1% of the time, Pallas kernels for 27%

profile of v8, /device:TPU:0, one launch (start us, length us, event | category | flops | bytes accessed | tf_op | source)
XLA Modules:
  0.0 41.9 jit_solution(788627325491980399)
XLA Ops:
  0.6 1.4 %share.1 = bf16[112,1792]{1,0:T(8,128)(2,1)S(1)} custom-call(bf16[64,4,3584]{2,1,0:T(4,128)(2,1)} %bitcast.13, bf16[64,4,3584]{2,1,0:T(4,128)(2,1)} %bitcast.16, f32[4,64]{1,0:T(4,128)} %bitcast.19, s32[1,4]{1,0:T(1,128)} %bitcast.22), custom_call_target="tpu_custom_call" | custom-call | tf_op jit(solution)/shard_map/share/pallas_call | solution.py:94
  2.0 3.0 %collective-permute-start.6 = (bf16[112,1792]{1,0:T(8,128)(2,1)S(1)}, bf16[112,1792]{1,0:T(8,128)(2,1)S(1)}, u32[]{:S(2)}, u32[]{:S(2)}) collective-permute-start(bf16[112,1792]{1,0:T(8,128)(2,1)S(1)} %share.1), channel_id=1, source_target_pairs={{0,16},{16,0},{1,17},{17,1},{2,18},{18,2},{3,19},{19,3},{4,20},{20... | collective-permute-start | bytes 1204232 | tf_op jit(solution)/shard_map/ppermute | solution.py:354
  5.0 8.4 %forward.1 = (bf16[880,512]{1,0:T(8,128)(2,1)S(1)}, bf16[64,3584]{1,0:T(8,128)(2,1)S(1)}, bf16[64,3584]{1,0:T(8,128)(2,1)S(1)}, bf16[32,3584]{1,0:T(8,128)(2,1)S...) custom-call(bf16[64,4,3584]{2,1,0:T(4,128)(2,1)} %bitcast.14, ...), custom_call_target="tpu_custom_call" | custom-call | flops 4697620480 | bytes 18000000 | tf_op jit(solution)/shard_map/forward/pallas_call | solution.py:219
  13.6 0.5 %collective-permute-start.2 = (bf16[32,3584]{1,0:T(8,128)(2,1)S(1)}, bf16[32,3584]{1,0:T(8,128)(2,1)S(1)}, u32[]{:S(2)}, u32[]{:S(2)}) collective-permute-start(bf16[32,3584]{1,0:T(8,128)(2,1)S(1)} %get-tuple-element.34), channel_id=1, source_target_pairs={{0,1},{1,0},{2,3},{3,2},{4,5},{5,4},{6,7},{7,6},{8,9},{9,8},{10,11... | collective-permute-start | bytes 688136 | tf_op jit(solution)/shard_map/ppermute | solution.py:351
  14.2 0.4 %collective-permute-start.1 = (bf16[32,3584]{1,0:T(8,128)(2,1)S(1)}, bf16[32,3584]{1,0:T(8,128)(2,1)S(1)}, u32[]{:S(2)}, u32[]{:S(2)}) collective-permute-start(bf16[32,3584]{1,0:T(8,128)(2,1)S(1)} %get-tuple-element.31), channel_id=1, source_target_pairs={{0,1},{1,0},{2,3},{3,2},{4,5},{5,4},{6,7},{7,6},{8,9},{9,8},{10,11... | collective-permute-start | bytes 688136 | tf_op jit(solution)/shard_map/ppermute | solution.py:351
  14.6 0.5 %collective-permute-done.5 = bf16[32,3584]{1,0:T(8,128)(2,1)S(1)} collective-permute-done((bf16[32,3584]{1,0:T(8,128)(2,1)S(1)}, bf16[32,3584]{1,0:T(8,128)(2,1)S(1)}, u32[]{:S(2)}, u32[]{:S(2)}) %collective-permute-start.5) | collective-permute-done | bytes 229408 | tf_op jit(solution)/shard_map/ppermute | solution.py:351
  15.1 0.8 %collective-permute-start.13 = (bf16[880,512]{1,0:T(8,128)(2,1)S(1)}, bf16[880,512]{1,0:T(8,128)(2,1)S(1)}, u32[]{:S(2)}, u32[]{:S(2)}) collective-permute-start(bf16[880,512]{1,0:T(8,128)(2,1)S(1)} %get-tuple-element.35.acts), channel_id=1, source_target_pairs={{0,16},{16,0},{1,17},{17,1},{2,18},{18,2},{3,19},{19,3},{4,20},{20... | collective-permute-start | bytes 2703368 | tf_op jit(solution)/shard_map/ppermute | solution.py:354
  15.9 0.1 add_convert_fusion
  16.0 1.6 %collective-permute-start.7 = (bf16[32,3584]{1,0:T(8,128)(2,1)S(1)}, bf16[32,3584]{1,0:T(8,128)(2,1)S(1)}, u32[]{:S(2)}, u32[]{:S(2)}) collective-permute-start(bf16[32,3584]{1,0:T(8,128)(2,1)S(1)} %get-tuple-element.54), channel_id=1, source_target_pairs={{0,2},{1,3},{2,0},{3,1},{4,6},{5,7},{6,4},{7,5},{8,10},{9,11},{10,... | collective-permute-start | bytes 688136 | tf_op jit(solution)/shard_map/ppermute | solution.py:351
  17.6 0.1 add_convert_fusion.3
  17.8 1.8 %own_grads.1 = (bf16[1792,512]{1,0:T(8,128)(2,1)S(1)}, bf16[1792,512]{1,0:T(8,128)(2,1)S(1)}, bf16[1792,512]{1,0:T(8,128)(2,1)S(1)}) custom-call(bf16[64,4,3584]{2,1,0:T(4,128)(2,1)S(1)} %bitcast.15, bf16[64,4,3584]{2,1,0:T(4,128)(2,1)S(1)} %bitcast.18, f32[4,64]{1,0:T(4,128)S(1)} %bitcast.21, s32[1,4]{1,0:T(1,128)S(1)} %bitcast.24, ...), custom_call_target="tpu_custom_call" | custom-call | flops 1409286144 | bytes 10000000 | tf_op jit(solution)/shard_map/own_grads/pallas_call | solution.py:258
  19.6 0.6 %collective-permute-start.3 = (bf16[32,3584]{1,0:T(8,128)(2,1)S(1)}, bf16[32,3584]{1,0:T(8,128)(2,1)S(1)}, u32[]{:S(2)}, u32[]{:S(2)}) collective-permute-start(bf16[32,3584]{1,0:T(8,128)(2,1)S(1)} %get-tuple-element.37), channel_id=1, source_target_pairs={{0,2},{1,3},{2,0},{3,1},{4,6},{5,7},{6,4},{7,5},{8,10},{9,11},{10,... | collective-permute-start | bytes 688136 | tf_op jit(solution)/shard_map/ppermute | solution.py:351
  20.1 4.4 %collective-permute-done.7 = bf16[32,3584]{1,0:T(8,128)(2,1)S(1)} collective-permute-done((bf16[32,3584]{1,0:T(8,128)(2,1)S(1)}, bf16[32,3584]{1,0:T(8,128)(2,1)S(1)}, u32[]{:S(2)}, u32[]{:S(2)}) %collective-permute-start.7) | collective-permute-done | bytes 229408 | tf_op jit(solution)/shard_map/ppermute | solution.py:351
  24.6 3.7 %collective-permute-start.9 = (bf16[16,3584]{1,0:T(8,128)(2,1)S(1)}, bf16[16,3584]{1,0:T(8,128)(2,1)S(1)}, u32[]{:S(2)}, u32[]{:S(2)}) collective-permute-start(bf16[16,3584]{1,0:T(8,128)(2,1)S(1)} %get-tuple-element.52), channel_id=1, source_target_pairs={{0,12},{4,8},{8,4},{12,0},{1,13},{5,9},{9,5},{13,1},{2,14},{6,10},... | collective-permute-start | bytes 344072 | tf_op jit(solution)/shard_map/ppermute | solution.py:384
  28.3 1.5 %collective-permute-start.10 = (bf16[112,1792]{1,0:T(8,128)(2,1)S(1)}, bf16[112,1792]{1,0:T(8,128)(2,1)S(1)}, u32[]{:S(2)}, u32[]{:S(2)}) collective-permute-start(bf16[112,1792]{1,0:T(8,128)(2,1)S(1)} %collective-permute-done.6.refs_0_), channel_id=1, source_target_pairs={{0,2},{1,3},{2,0},{3,1},{4,6},{5,7},{6,4},{7,5},{8,10},{9,11},{10,... | collective-permute-start | bytes 1204232 | tf_op jit(solution)/shard_map/ppermute | solution.py:351
  29.8 0.9 %collective-permute-start.4 = (bf16[16,3584]{1,0:T(8,128)(2,1)S(1)}, bf16[16,3584]{1,0:T(8,128)(2,1)S(1)}, u32[]{:S(2)}, u32[]{:S(2)}) collective-permute-start(bf16[16,3584]{1,0:T(8,128)(2,1)S(1)} %add_convert_fusion.6), channel_id=1, source_target_pairs={{0,4},{4,0},{8,12},{12,8},{1,5},{5,1},{9,13},{13,9},{2,6},{6,2},{1... | collective-permute-start | bytes 344072 | tf_op jit(solution)/shard_map/ppermute | solution.py:384
  30.8 0.8 %collective-permute-done.9.refs_2_ = bf16[16,3584]{1,0:T(8,128)(2,1)S(1)} collective-permute-done((bf16[16,3584]{1,0:T(8,128)(2,1)S(1)}, bf16[16,3584]{1,0:T(8,128)(2,1)S(1)}, u32[]{:S(2)}, u32[]{:S(2)}) %collective-permute-start.9) | collective-permute-done | bytes 114720 | tf_op jit(solution)/shard_map/ppermute | solution.py:384
  31.6 4.5 %collective-permute-done.8.refs_1_ = bf16[16,3584]{1,0:T(8,128)(2,1)S(1)} collective-permute-done((bf16[16,3584]{1,0:T(8,128)(2,1)S(1)}, bf16[16,3584]{1,0:T(8,128)(2,1)S(1)}, u32[]{:S(2)}, u32[]{:S(2)}) %collective-permute-start.8) | collective-permute-done | bytes 114720 | tf_op jit(solution)/shard_map/ppermute | solution.py:384
  36.1 0.5 %collective-permute-done.4.refs_0_ = bf16[16,3584]{1,0:T(8,128)(2,1)S(1)} collective-permute-done((bf16[16,3584]{1,0:T(8,128)(2,1)S(1)}, bf16[16,3584]{1,0:T(8,128)(2,1)S(1)}, u32[]{:S(2)}, u32[]{:S(2)}) %collective-permute-start.4) | collective-permute-done | bytes 114720 | tf_op jit(solution)/shard_map/ppermute | solution.py:384
  36.6 0.5 %collective-permute-done.10.refs_1_ = bf16[112,1792]{1,0:T(8,128)(2,1)S(1)} collective-permute-done((bf16[112,1792]{1,0:T(8,128)(2,1)S(1)}, bf16[112,1792]{1,0:T(8,128)(2,1)S(1)}, u32[]{:S(2)}, u32[]{:S(2)}) %collective-permute-start.10) | collective-permute-done | bytes 401440 | tf_op jit(solution)/shard_map/ppermute | solution.py:351
  37.1 0.5 %collective-permute-start.14 = (bf16[112,512]{1,0:T(8,128)(2,1)S(1)}, bf16[112,512]{1,0:T(8,128)(2,1)S(1)}, u32[]{:S(2)}, u32[]{:S(2)}) collective-permute-start(bf16[112,512]{1,0:T(8,128)(2,1)S(1)} %slice.60), channel_id=1, source_target_pairs={{0,1},{1,0},{2,3},{3,2},{4,5},{5,4},{6,7},{7,6},{8,9},{9,8},{10,11... | collective-permute-start | bytes 344072 | tf_op jit(solution)/shard_map/ppermute | solution.py:351
  37.7 1.0 %collect.1 = bf16[16,4,3584]{2,1,0:T(4,128)(2,1)} custom-call(bf16[16,3584]{1,0:T(8,128)(2,1)S(1)} %collective-permute-done.4.refs_0_, bf16[16,3584]{1,0:T(8,128)(2,1)S(1)} %collective-permute-done.8.refs_1_, bf16[16,3584]{1,0:T(8,128)(2,1)S(1)} %collective-permute-done.9.refs_2_, bf16[16,3584]{1,0:T(8,128)(2,1)S(1)} %slice.58.refs_3_, ...), custom_call_target="tpu_custom_call" | custom-call | tf_op jit(solution)/shard_map/collect/pallas_call | solution.py:390
  38.7 0.2 collective-permute-done.14.refs_5_
  39.0 2.9 %weight_grads.1 = (bf16[1792,512]{1,0:T(8,128)(2,1)}, bf16[1792,512]{1,0:T(8,128)(2,1)}, bf16[1792,512]{1,0:T(8,128)(2,1)}) custom-call(bf16[112,1792]{1,0:T(8,128)(2,1)S(1)} %collective-permute-done.6.refs_0_, bf16[112,1792]{1,0:T(8,128)(2,1)S(1)} %collective-permute-done.10.refs_1_, bf16[112,1792]{1,0:T(8,128)(2,1)S(1)} %collective-permute-done.11.refs_2_, ...), custom_call_target="tpu_custom_call" | custom-call | flops 1409286144 | bytes 4000000 | tf_op jit(solution)/shard_map/weight_grads/pallas_call | solution.py:307
  (28 shorter events, 0.4 us)
Async XLA Ops:
  0.6 4.4 %copy-start.4 = (bf16[1,3584,512]{2,1,0:T(8,128)(2,1)S(1)}, bf16[1,3584,512]{2,1,0:T(8,128)(2,1)}, u32[]{:S(2)}) copy-start(bf16[1,3584,512]{2,1,0:T(8,128)(2,1)} %param.11) | copy-start | bytes 11010052
  2.0 13.9 %collective-permute-start.6 = (bf16[112,1792]{1,0:T(8,128)(2,1)S(1)}, bf16[112,1792]{1,0:T(8,128)(2,1)S(1)}, u32[]{:S(2)}, u32[]{:S(2)}) collective-permute-start(bf16[112,1792]{1,0:T(8,128)(2,1)S(1)} %share.1), channel_id=1, source_target_pairs={{0,16},{16,0},{1,17},{17,1},{2,18},{18,2},{3,19},{19,3},{4,20},{20... | collective-permute-start | bytes 1204232 | tf_op jit(solution)/shard_map/ppermute | solution.py:354
  5.0 12.7 %copy-start.1 = (bf16[1,1,64,4,3584]{4,3,2,1,0:T(4,128)(2,1)S(1)}, bf16[1,1,64,4,3584]{4,3,2,1,0:T(4,128)(2,1)}, u32[]{:S(2)}) copy-start(bf16[1,1,64,4,3584]{4,3,2,1,0:T(4,128)(2,1)} %param.8) | copy-start | bytes 5505028
  13.5 4.3 %copy-start = (bf16[1,1,64,4,3584]{4,3,2,1,0:T(4,128)(2,1)S(1)}, bf16[1,1,64,4,3584]{4,3,2,1,0:T(4,128)(2,1)}, u32[]{:S(2)}) copy-start(bf16[1,1,64,4,3584]{4,3,2,1,0:T(4,128)(2,1)} %param.7) | copy-start | bytes 5505028
  13.5 4.3 %copy-start.2 = (f32[1,1,64,4]{2,3,1,0:T(4,128)S(1)}, f32[1,1,64,4]{2,3,1,0:T(4,128)}, u32[]{:S(2)}) copy-start(f32[1,1,64,4]{2,3,1,0:T(4,128)} %param.9) | copy-start | bytes 3076
  13.5 4.3 %copy-start.3 = (s32[1,1,4]{2,1,0:T(1,128)S(1)}, s32[1,1,4]{2,1,0:T(1,128)}, u32[]{:S(2)}) copy-start(s32[1,1,4]{2,1,0:T(1,128)} %param.10) | copy-start | bytes 52
  13.5 1.6 %collective-permute-start.5 = (bf16[32,3584]{1,0:T(8,128)(2,1)S(1)}, bf16[32,3584]{1,0:T(8,128)(2,1)S(1)}, u32[]{:S(2)}, u32[]{:S(2)}) collective-permute-start(bf16[32,3584]{1,0:T(8,128)(2,1)S(1)} %get-tuple-element.38), channel_id=1, source_target_pairs={{0,1},{1,0},{2,3},{3,2},{4,5},{5,4},{6,7},{7,6},{8,9},{9,8},{10,11... | collective-permute-start | bytes 688136 | tf_op jit(solution)/shard_map/ppermute | solution.py:351
  13.6 2.3 %collective-permute-start.2 = (bf16[32,3584]{1,0:T(8,128)(2,1)S(1)}, bf16[32,3584]{1,0:T(8,128)(2,1)S(1)}, u32[]{:S(2)}, u32[]{:S(2)}) collective-permute-start(bf16[32,3584]{1,0:T(8,128)(2,1)S(1)} %get-tuple-element.34), channel_id=1, source_target_pairs={{0,1},{1,0},{2,3},{3,2},{4,5},{5,4},{6,7},{7,6},{8,9},{9,8},{10,11... | collective-permute-start | bytes 688136 | tf_op jit(solution)/shard_map/ppermute | solution.py:351
  14.1 3.5 %collective-permute-start = (bf16[32,3584]{1,0:T(8,128)(2,1)S(1)}, bf16[32,3584]{1,0:T(8,128)(2,1)S(1)}, u32[]{:S(2)}, u32[]{:S(2)}) collective-permute-start(bf16[32,3584]{1,0:T(8,128)(2,1)S(1)} %get-tuple-element.30), channel_id=1, source_target_pairs={{0,1},{1,0},{2,3},{3,2},{4,5},{5,4},{6,7},{7,6},{8,9},{9,8},{10,11... | collective-permute-start | bytes 688136 | tf_op jit(solution)/shard_map/ppermute | solution.py:351
  14.2 3.4 %collective-permute-start.1 = (bf16[32,3584]{1,0:T(8,128)(2,1)S(1)}, bf16[32,3584]{1,0:T(8,128)(2,1)S(1)}, u32[]{:S(2)}, u32[]{:S(2)}) collective-permute-start(bf16[32,3584]{1,0:T(8,128)(2,1)S(1)} %get-tuple-element.31), channel_id=1, source_target_pairs={{0,1},{1,0},{2,3},{3,2},{4,5},{5,4},{6,7},{7,6},{8,9},{9,8},{10,11... | collective-permute-start | bytes 688136 | tf_op jit(solution)/shard_map/ppermute | solution.py:351
  15.1 22.0 %collective-permute-start.13 = (bf16[880,512]{1,0:T(8,128)(2,1)S(1)}, bf16[880,512]{1,0:T(8,128)(2,1)S(1)}, u32[]{:S(2)}, u32[]{:S(2)}) collective-permute-start(bf16[880,512]{1,0:T(8,128)(2,1)S(1)} %get-tuple-element.35.acts), channel_id=1, source_target_pairs={{0,16},{16,0},{1,17},{17,1},{2,18},{18,2},{3,19},{19,3},{4,20},{20... | collective-permute-start | bytes 2703368 | tf_op jit(solution)/shard_map/ppermute | solution.py:354
  16.0 8.6 %collective-permute-start.7 = (bf16[32,3584]{1,0:T(8,128)(2,1)S(1)}, bf16[32,3584]{1,0:T(8,128)(2,1)S(1)}, u32[]{:S(2)}, u32[]{:S(2)}) collective-permute-start(bf16[32,3584]{1,0:T(8,128)(2,1)S(1)} %get-tuple-element.54), channel_id=1, source_target_pairs={{0,2},{1,3},{2,0},{3,1},{4,6},{5,7},{6,4},{7,5},{8,10},{9,11},{10,... | collective-permute-start | bytes 688136 | tf_op jit(solution)/shard_map/ppermute | solution.py:351
  19.6 10.3 %collective-permute-start.3 = (bf16[32,3584]{1,0:T(8,128)(2,1)S(1)}, bf16[32,3584]{1,0:T(8,128)(2,1)S(1)}, u32[]{:S(2)}, u32[]{:S(2)}) collective-permute-start(bf16[32,3584]{1,0:T(8,128)(2,1)S(1)} %get-tuple-element.37), channel_id=1, source_target_pairs={{0,2},{1,3},{2,0},{3,1},{4,6},{5,7},{6,4},{7,5},{8,10},{9,11},{10,... | collective-permute-start | bytes 688136 | tf_op jit(solution)/shard_map/ppermute | solution.py:351
  24.6 7.0 %collective-permute-start.9 = (bf16[16,3584]{1,0:T(8,128)(2,1)S(1)}, bf16[16,3584]{1,0:T(8,128)(2,1)S(1)}, u32[]{:S(2)}, u32[]{:S(2)}) collective-permute-start(bf16[16,3584]{1,0:T(8,128)(2,1)S(1)} %get-tuple-element.52), channel_id=1, source_target_pairs={{0,12},{4,8},{8,4},{12,0},{1,13},{5,9},{9,5},{13,1},{2,14},{6,10},... | collective-permute-start | bytes 344072 | tf_op jit(solution)/shard_map/ppermute | solution.py:384
  28.3 7.8 %collective-permute-start.8 = (bf16[16,3584]{1,0:T(8,128)(2,1)S(1)}, bf16[16,3584]{1,0:T(8,128)(2,1)S(1)}, u32[]{:S(2)}, u32[]{:S(2)}) collective-permute-start(bf16[16,3584]{1,0:T(8,128)(2,1)S(1)} %get-tuple-element.53), channel_id=1, source_target_pairs={{0,8},{4,12},{8,0},{12,4},{1,9},{5,13},{9,1},{13,5},{2,10},{6,14},... | collective-permute-start | bytes 344072 | tf_op jit(solution)/shard_map/ppermute | solution.py:384
  28.3 8.8 %collective-permute-start.10 = (bf16[112,1792]{1,0:T(8,128)(2,1)S(1)}, bf16[112,1792]{1,0:T(8,128)(2,1)S(1)}, u32[]{:S(2)}, u32[]{:S(2)}) collective-permute-start(bf16[112,1792]{1,0:T(8,128)(2,1)S(1)} %collective-permute-done.6.refs_0_), channel_id=1, source_target_pairs={{0,2},{1,3},{2,0},{3,1},{4,6},{5,7},{6,4},{7,5},{8,10},{9,11},{10,... | collective-permute-start | bytes 1204232 | tf_op jit(solution)/shard_map/ppermute | solution.py:351
  29.8 6.7 %collective-permute-start.4 = (bf16[16,3584]{1,0:T(8,128)(2,1)S(1)}, bf16[16,3584]{1,0:T(8,128)(2,1)S(1)}, u32[]{:S(2)}, u32[]{:S(2)}) collective-permute-start(bf16[16,3584]{1,0:T(8,128)(2,1)S(1)} %add_convert_fusion.6), channel_id=1, source_target_pairs={{0,4},{4,0},{8,12},{12,8},{1,5},{5,1},{9,13},{13,9},{2,6},{6,2},{1... | collective-permute-start | bytes 344072 | tf_op jit(solution)/shard_map/ppermute | solution.py:384
  31.6 7.4 %collective-permute-start.11 = (bf16[112,1792]{1,0:T(8,128)(2,1)S(1)}, bf16[112,1792]{1,0:T(8,128)(2,1)S(1)}, u32[]{:S(2)}, u32[]{:S(2)}) collective-permute-start(bf16[112,1792]{1,0:T(8,128)(2,1)S(1)} %collective-permute-done.6.refs_0_), channel_id=1, source_target_pairs={{0,1},{1,0},{2,3},{3,2},{4,5},{5,4},{6,7},{7,6},{8,9},{9,8},{10,11... | collective-permute-start | bytes 1204232 | tf_op jit(solution)/shard_map/ppermute | solution.py:351
  37.1 1.9 %collective-permute-start.12 = (bf16[112,1792]{1,0:T(8,128)(2,1)S(1)}, bf16[112,1792]{1,0:T(8,128)(2,1)S(1)}, u32[]{:S(2)}, u32[]{:S(2)}) collective-permute-start(bf16[112,1792]{1,0:T(8,128)(2,1)S(1)} %collective-permute-done.10.refs_1_), channel_id=1, source_target_pairs={{0,1},{1,0},{2,3},{3,2},{4,5},{5,4},{6,7},{7,6},{8,9},{9,8},{10,11... | collective-permute-start | bytes 1204232 | tf_op jit(solution)/shard_map/ppermute | solution.py:351
  37.1 1.8 %collective-permute-start.14 = (bf16[112,512]{1,0:T(8,128)(2,1)S(1)}, bf16[112,512]{1,0:T(8,128)(2,1)S(1)}, u32[]{:S(2)}, u32[]{:S(2)}) collective-permute-start(bf16[112,512]{1,0:T(8,128)(2,1)S(1)} %slice.60), channel_id=1, source_target_pairs={{0,1},{1,0},{2,3},{3,2},{4,5},{5,4},{6,7},{7,6},{8,9},{9,8},{10,11... | collective-permute-start | bytes 344072 | tf_op jit(solution)/shard_map/ppermute | solution.py:351
